TPU v7x, 32 devices: a whole 2x2x4 slice. The times are simulated.
32 devices in a mesh: grp: 4 (over z), bis: 8 (over y, x, core).
Axes of the slice: x: 2, y: 2, z: 4, core: 2. Of those that a mesh axis runs over, the one named last changes fastest.
Arguments:
- state: float32 [5, 1024, 512], P(None, ('grp', 'bis')), may hold values from -0.75 to 2, as said below
- order: int32 [32, 8], P(('grp', 'bis')), may hold values from 0 to 7, each once within a row
- sweep: float32 [1024, 512], P(('grp', 'bis')), may hold values from 0.1 to 0.45
- owner: int32 [256, 1], P(('grp', 'bis')), may hold values from 0 to 7; in each aligned block of 8 rows (0 to 7, 8 to 15, ...) at most 2 rows name the same one
- slot_target: int32 [256], P(('grp', 'bis')), may hold values from 0 to 7
Outputs:
- mass_out: float32 [1024, 512], P(('grp', 'bis'))
- energy_out: float32 [1024, 512], P(('grp', 'bis'))
- velocity: float32 [2, 1024, 512], P(None, ('grp', 'bis'))
Inputs may be any that keep to these rules, and one draw needn't show every extreme that they name: `state`: velocities up to 0.75 in size, densities and energies from 1 to 2, adiabatic indices from 1.3 to 1.7. `order`: each row of a device is a permutation. Among the row blocks of one device no owner is named more than 2 times, a bound that some block reaches.
All inputs are finite; a program needn't handle non-finite values.
Results may differ from a plain program's by a relative error of at most 0.00016.
Values sent between devices are 32-bit elements; how exact they have to be, the bound alone decides.
No kernel may reach another device: no remote copies, remote signals or barrier semaphores. Data moves between devices by JAX's collectives and lax.ppermute only.
A program may use at most 64 MiB of HBM per device.

v0:
```python
import jax
import jax.numpy as jnp
from jax import lax
from jax.sharding import PartitionSpec as P

STEPS = 2
CAP = 2


STEP_DT = 0.15


def from_partner(block, axis, bit):
    count = lax.axis_size(axis)
    route = []
    for low in range(count):
        high = low | 1 << bit
        if high != low and high < count:
            route += [(low, high), (high, low)]
    return lax.ppermute(block, axis, route)


def with_halo(block, sides, width):
    for axis, dim in sides:
        count = lax.axis_size(axis)
        forward = [(i, i + 1) for i in range(count - 1)]
        backward = [(target, source) for source, target in forward]
        low = lax.ppermute(
            lax.slice_in_dim(block, block.shape[dim] - width, None, axis=dim), axis, forward
        )
        high = lax.ppermute(lax.slice_in_dim(block, 0, width, axis=dim), axis, backward)
        block = jnp.concatenate([low, block, high], axis=dim)
    return block


def advance(fields, volume, valid):
    rho = fields[0]
    ene = fields[1]
    velu = fields[2]
    velv = fields[3]
    gam = fields[4]
    press = (gam - 1.0) * rho * ene
    wide_p = jnp.pad(press[1:-1], ((0, 0), (1, 1)))
    wide_v = jnp.pad(velv[1:-1], ((0, 0), (1, 1)))
    grad_x = 0.5 * (press[2:] - press[:-2])
    grad_y = 0.5 * (wide_p[:, 2:] - wide_p[:, :-2])
    spread = 0.5 * (velu[2:] - velu[:-2] + wide_v[:, 2:] - wide_v[:, :-2])
    dens = jnp.where(valid, rho[1:-1], 1.0)
    growth = 1.0 + STEP_DT * spread
    center_g = gam[1:-1]
    updated = jnp.stack(
        [
            dens / growth,
            ene[1:-1] * (1.0 - STEP_DT * (center_g - 1.0) * spread),
            velu[1:-1] - STEP_DT * grad_x / dens,
            velv[1:-1] - STEP_DT * grad_y / dens,
            center_g,
        ]
    )
    updated = jnp.where(valid[None], updated, 0.0)
    return (updated, volume * growth)


def shards(state, order, sweep, owner, slot_target):
    rows = state.shape[1]
    width = state.shape[2]
    nbis = lax.axis_size("bis")
    block_rows = rows // nbis
    flat = block_rows * width
    picked = jnp.take(state.reshape(5, nbis, flat), order[0], axis=1)
    levels = nbis.bit_length() - 1
    bis_index = lax.axis_index("bis")
    moved = picked
    for level in range(levels):
        halves = moved.reshape(5, nbis >> level + 1, 2, 1 << level, flat)
        lower = halves[:, :, 0]
        upper = halves[:, :, 1]
        keep_low = bis_index >> level & 1 == 0
        outgoing = jnp.where(keep_low, upper, lower)
        incoming = from_partner(outgoing, "bis", level)
        lower = jnp.where(keep_low, lower, incoming)
        upper = jnp.where(keep_low, incoming, upper)
        moved = jnp.stack([lower, upper], axis=2).reshape(5, nbis, flat)
    fields = moved.reshape(5, rows, width)
    fields = with_halo(fields, ((("grp", "bis"), 1),), STEPS)
    device = lax.axis_index("grp") * nbis + lax.axis_index("bis")
    total = lax.axis_size("grp") * nbis * rows
    volume = jnp.ones((rows + 2 * STEPS, width), jnp.float32)
    for step in range(STEPS):
        extra = STEPS - 1 - step
        volume = volume[1:-1]
        row_ids = device * rows - extra + jnp.arange(rows + 2 * extra, dtype=jnp.int32)
        valid = ((row_ids >= 0) & (row_ids < total))[:, None]
        fields, volume = advance(fields, volume, valid)
    mass = fields[0] * volume
    heat = mass * fields[1]
    frac = sweep * volume / (1.0 + volume)
    amounts = jnp.stack([mass, heat])
    stay = ((1.0 - frac) * amounts).reshape(2, nbis, block_rows, width)
    leave = jnp.roll((frac * amounts).reshape(2, nbis, block_rows, width), 1, axis=2)
    partial_value = (stay + leave).reshape(2, nbis, flat)
    target = owner[:, 0]
    hits = (target[:, None] == jnp.arange(nbis, dtype=jnp.int32)[None, :]).astype(jnp.int32)
    rank = jnp.sum(jnp.cumsum(hits, axis=0) * hits, axis=1) - 1
    position = target * CAP + rank
    select = (position[None, :] == jnp.arange(nbis * CAP, dtype=jnp.int32)[:, None]).astype(
        jnp.float32
    )
    outgoing = jnp.einsum("pb,qbf->qpf", select, partial_value, precision=lax.Precision.HIGHEST)
    filled = jnp.sum(select, axis=1) > 0.0
    labels = jnp.where(
        filled,
        jnp.dot(select, slot_target.astype(jnp.float32), precision=lax.Precision.HIGHEST),
        -1.0,
    )
    arrived, arrived_labels = (
        lax.all_to_all(
            outgoing.reshape(2, nbis, CAP * flat), "bis", split_axis=1, concat_axis=1, tiled=True
        ),
        lax.all_to_all(
            labels.reshape(1, nbis, CAP), "bis", split_axis=1, concat_axis=1, tiled=True
        ),
    )
    arrived = arrived.reshape(2, nbis * CAP, flat)
    landing = (
        arrived_labels.reshape(nbis * CAP)[None, :] == jnp.arange(nbis, dtype=jnp.float32)[:, None]
    ).astype(jnp.float32)
    owned = jnp.einsum("bp,qpf->qbf", landing, arrived, precision=lax.Precision.HIGHEST).reshape(
        2, rows, width
    )
    return (owned[0], owned[1], fields[2:4])


def solution(mesh):
    placed = (
        P(None, ("grp", "bis"), None),
        P(("grp", "bis"), None),
        P(("grp", "bis"), None),
        P(("grp", "bis"), None),
        P(("grp", "bis")),
    )
    return jax.shard_map(
        shards,
        mesh=mesh,
        in_specs=placed,
        out_specs=(P(("grp", "bis"), None), P(("grp", "bis"), None), P(None, ("grp", "bis"), None)),
        check_vma=False,
    )
```

profile of v0, /device:TPU:8, one launch (start us, length us, event | category | flops | bytes accessed | tf_op | source)
XLA Modules:
  0.0 48.7 jit_solution(6637078511483607642)
XLA Ops:
  0.6 1.1 %reshape.218 = f32[5,8,2048]{2,1,0:T(8,128)S(1)} reshape(f32[5,32,512]{2,1,0:T(8,128)} %param.5) | data formatting | bytes 655360 | tf_op jit(solution)/shard_map/reshape | solution.py:70
  2.0 0.4 copy-done.2
  2.4 0.5 %broadcast.251 = s32[]{:T(128)} broadcast(s32[]{:T(128)} %constant.29.clone.1), dimensions={} | broadcast | bytes 8 | tf_op args[1]
  2.9 0.7 %reduce.8 = s32[8]{0:T(128)S(1)} reduce(s32[1,8]{1,0:T(1,128)S(1)} %copy-done.2, s32[]{:T(128)} %broadcast.251), dimensions={0}, to_apply=%param.6.reduce_sub_computation.3 | reduce | bytes 68 | tf_op args[1]
  3.7 0.6 %gather_fusion = f32[8,5,2048]{2,1,0:T(8,128)S(1)} fusion(f32[5,8,2048]{2,0,1:T(8,128)S(1)} %copy.27, s32[1024]{0:T(1024)S(1)} %pad_clamp_fusion), kind=kCustom, calls=%fused_computation | custom fusion | bytes 655392 | tf_op jit(solution)/shard_map/jit(_take)/gather | solution.py:70
  4.3 0.4 copy_select_fusion
  4.9 0.6 %copy-done.1 = s32[8,1]{0,1:T(1,128)S(1)} copy-done((s32[8,1]{0,1:T(1,128)S(1)}, s32[8,1]{0,1:T(1,128)}, u32[]{:S(2)}) %copy-start.1) | copy-done | bytes 56
  5.8 0.5 %collective-permute-done = f32[5,4,1,2048]{3,2,1,0:T(1,128)S(1)} collective-permute-done((f32[5,4,1,2048]{3,2,1,0:T(1,128)S(1)}, f32[5,4,1,2048]{3,2,1,0:T(1,128)S(1)}, u32[]{:S(2)}, u32[]{:S(2)}) %collective-permute-start) | collective-permute-done | bytes 163872 | tf_op jit(solution)/shard_map/ppermute | solution.py:20
  6.3 0.3 broadcast_select_fusion.1
  6.6 0.3 broadcast_select_fusion.8
  6.9 1.6 %collective-permute-start.1 = (f32[5,2,2,2048]{3,2,1,0:T(2,128)S(1)}, f32[5,2,2,2048]{3,2,1,0:T(2,128)S(1)}, u32[]{:S(2)}, u32[]{:S(2)}) collective-permute-start(f32[5,2,2,2048]{3,2,1,0:T(2,128)S(1)} %broadcast_select_fusion.8), channel_id=1, source_target_pairs={{0,2},{2,0},{1,3},{3,1},{4,6},{6,4},{5,7},{7,5},{8,10},{10,8},{9,1... | collective-permute-start | bytes 491528 | tf_op jit(solution)/shard_map/ppermute | solution.py:20
  8.6 4.7 %collective-permute-done.1 = f32[5,2,2,2048]{3,2,1,0:T(2,128)S(1)} collective-permute-done((f32[5,2,2,2048]{3,2,1,0:T(2,128)S(1)}, f32[5,2,2,2048]{3,2,1,0:T(2,128)S(1)}, u32[]{:S(2)}, u32[]{:S(2)}) %collective-permute-start.1) | collective-permute-done | bytes 163872 | tf_op jit(solution)/shard_map/ppermute | solution.py:20
  13.2 0.3 select_bitcast_fusion.1
  13.7 0.3 copy.30
  14.2 1.6 %collective-permute-start.2 = (f32[5,1,4,2048]{3,1,2,0:T(1,128)S(1)}, f32[5,1,4,2048]{3,1,2,0:T(1,128)S(1)}, u32[]{:S(2)}, u32[]{:S(2)}) collective-permute-start(f32[5,1,4,2048]{3,1,2,0:T(1,128)S(1)} %broadcast_select_fusion.5), channel_id=1, source_target_pairs={{0,4},{4,0},{1,5},{5,1},{2,6},{6,2},{3,7},{7,3},{8,12},{12,8},{9,1... | collective-permute-start | bytes 491528 | tf_op jit(solution)/shard_map/ppermute | solution.py:20
  15.9 0.7 %reshape.221 = f32[1,8,2]{2,1,0:T(8,128)} reshape(f32[16]{0:T(128)S(1)} %fusion) | data formatting | bytes 128 | tf_op jit(solution)/shard_map/reshape | solution.py:121
  16.6 3.3 %all-to-all-start.1 = ((f32[1,8,2]{2,0,1:T(1,128)}), f32[1,8,2]{2,0,1:T(1,128)S(1)}, u32[]{:S(2)}, u32[]{:S(2)}) async-start(f32[1,8,2]{2,0,1:T(1,128)} %bitcast.48), calls=%async_computation.1 | async-start | bytes 8192 | tf_op jit(solution)/shard_map/all_to_all | solution.py:120
  20.0 0.3 fusion.1
  20.3 1.0 %maximum_reduce_fusion = f32[5,2,4,2048]{3,2,1,0:T(4,128)S(1)} fusion(f32[5,1,1,4,2048]{4,1,3,2,0:T(1,128)S(1)} %get-tuple-element.11, f32[5,1,1,4,2048]{4,1,3,2,0:T(1,128)S(1)} %get-tuple-element.10), kind=kLoop, calls=%fused_computation.9 | loop fusion | flops 81920 | bytes 655360 | tf_op jit(solution)/shard_map/stack | solution.py:83
  21.4 4.4 %collective-permute-start.3 = (f32[5,2,512]{2,1,0:T(2,128)S(1)}, f32[5,2,512]{2,1,0:T(2,128)S(1)}, u32[]{:S(2)}, u32[]{:S(2)}) collective-permute-start(f32[5,2,512]{2,1,0:T(2,128)S(1)} %get-tuple-element.17), channel_id=1, source_target_pairs={{1,0},{2,1},{3,2},{4,3},{5,4},{6,5},{7,6},{8,7},{9,8},{10,9},{11,1... | collective-permute-start | bytes 61448 | tf_op jit(solution)/shard_map/ppermute | solution.py:31
  25.8 1.9 %collective-permute-start.4 = (f32[5,2,512]{2,1,0:T(2,128)S(1)}, f32[5,2,512]{2,1,0:T(2,128)S(1)}, u32[]{:S(2)}, u32[]{:S(2)}) collective-permute-start(f32[5,2,512]{2,1,0:T(2,128)S(1)} %get-tuple-element.16), channel_id=1, source_target_pairs={{0,1},{1,2},{2,3},{3,4},{4,5},{5,6},{6,7},{7,8},{8,9},{9,10},{10,1... | collective-permute-start | bytes 61448 | tf_op jit(solution)/shard_map/ppermute | solution.py:28
  27.8 4.9 %collective-permute-done.4 = f32[5,2,512]{2,1,0:T(2,128)S(1)} collective-permute-done((f32[5,2,512]{2,1,0:T(2,128)S(1)}, f32[5,2,512]{2,1,0:T(2,128)S(1)}, u32[]{:S(2)}, u32[]{:S(2)}) %collective-permute-start.4) | collective-permute-done | bytes 20512 | tf_op jit(solution)/shard_map/ppermute | solution.py:28
  33.5 0.8 %copy-done = f32[32,512]{1,0:T(8,128)S(1)} copy-done((f32[32,512]{1,0:T(8,128)S(1)}, f32[32,512]{1,0:T(8,128)}, u32[]{:S(2)}) %copy-start) | copy-done | bytes 65560
  35.3 0.4 convolution_bitcast_fusion
  35.8 0.9 %copy.32 = f32[2,8,4096]{2,0,1:T(2,128)} copy(f32[2,8,4096]{2,1,0:T(8,128)S(1)} %reshape.219) | data formatting | bytes 524288 | tf_op jit(solution)/shard_map/reshape | solution.py:118
  36.7 3.4 %all-to-all-start = ((f32[2,8,4096]{2,0,1:T(2,128)}), f32[2,8,4096]{2,0,1:T(2,128)S(1)}, u32[]{:S(2)}, u32[]{:S(2)}) async-start(f32[2,8,4096]{2,0,1:T(2,128)} %copy.32), calls=%async_computation | async-start | bytes 524288 | tf_op jit(solution)/shard_map/all_to_all | solution.py:117
  40.1 0.5 %broadcast.252 = f32[]{:T(128)} broadcast(f32[]{:T(128)} %constant.256), dimensions={} | broadcast | bytes 8 | tf_op jit(solution)/shard_map/all_to_all | solution.py:120
  40.6 0.7 %reduce.9 = f32[8,2]{1,0:T(8,128)S(1)} reduce(f32[1,8,2]{2,0,1:T(1,128)S(1)} %all-to-all-done.1, f32[]{:T(128)} %broadcast.252), dimensions={0}, to_apply=%all_to_all.7.reduce_sub_computation.3 | reduce | bytes 132 | tf_op jit(solution)/shard_map/all_to_all | solution.py:120
  41.4 0.7 %slice.317 = f32[2,32,512]{2,1,0:T(8,128)} slice(f32[5,32,512]{2,1,0:T(8,128)S(1)} %broadcast_select_fusion.7), slice={[2:4], [0:32], [0:512]} | slice | bytes 262144 | tf_op jit(solution)/shard_map/slice | solution.py:131
  42.1 4.9 %all-to-all-done = f32[2,8,4096]{2,0,1:T(2,128)S(1)} async-done(((f32[2,8,4096]{2,0,1:T(2,128)}), f32[2,8,4096]{2,0,1:T(2,128)S(1)}, u32[]{:S(2)}, u32[]{:S(2)}) %all-to-all-start) | async-done | bytes 262176 | tf_op jit(solution)/shard_map/all_to_all | solution.py:117
  47.4 0.6 %squeeze.59 = f32[32,512]{1,0:T(8,128)} reshape(f32[1,8,2048]{2,1,0:T(8,128)S(1)} %get-tuple-element.19) | data formatting | bytes 131072 | tf_op jit(solution)/shard_map/squeeze | solution.py:131
  48.1 0.6 %squeeze.60 = f32[32,512]{1,0:T(8,128)} reshape(f32[1,8,2048]{2,1,0:T(8,128)S(1)} %get-tuple-element.18) | data formatting | bytes 131072 | tf_op jit(solution)/shard_map/squeeze | solution.py:131
  (63 shorter events, 3.9 us)
Async XLA Ops:
  1.8 0.7 %copy-start.2 = (s32[1,8]{1,0:T(1,128)S(1)}, s32[1,8]{1,0:T(1,128)}, u32[]{:S(2)}) copy-start(s32[1,8]{1,0:T(1,128)} %param.6) | copy-start | bytes 100
  4.9 0.7 %copy-start.1 = (s32[8,1]{0,1:T(1,128)S(1)}, s32[8,1]{0,1:T(1,128)}, u32[]{:S(2)}) copy-start(s32[8,1]{0,1:T(1,128)} %param.8) | copy-start | bytes 100
  4.9 1.5 %collective-permute-start = (f32[5,4,1,2048]{3,2,1,0:T(1,128)S(1)}, f32[5,4,1,2048]{3,2,1,0:T(1,128)S(1)}, u32[]{:S(2)}, u32[]{:S(2)}) collective-permute-start(f32[5,4,1,2048]{3,2,1,0:T(1,128)S(1)} %broadcast_select_fusion.2), channel_id=1, source_target_pairs={{0,1},{1,0},{2,3},{3,2},{4,5},{5,4},{6,7},{7,6},{8,9},{9,8},{10,11... | collective-permute-start | bytes 491528 | tf_op jit(solution)/shard_map/ppermute | solution.py:20
  6.9 6.3 %collective-permute-start.1 = (f32[5,2,2,2048]{3,2,1,0:T(2,128)S(1)}, f32[5,2,2,2048]{3,2,1,0:T(2,128)S(1)}, u32[]{:S(2)}, u32[]{:S(2)}) collective-permute-start(f32[5,2,2,2048]{3,2,1,0:T(2,128)S(1)} %broadcast_select_fusion.8), channel_id=1, source_target_pairs={{0,2},{2,0},{1,3},{3,1},{4,6},{6,4},{5,7},{7,5},{8,10},{10,8},{9,1... | collective-permute-start | bytes 491528 | tf_op jit(solution)/shard_map/ppermute | solution.py:20
  14.0 1.8 %copy-start.3 = (s32[8]{0:T(128)S(1)}, s32[8]{0:T(128)}, u32[]{:S(2)}) copy-start(s32[8]{0:T(128)} %param.9) | copy-start | bytes 100
  14.2 5.8 %collective-permute-start.2 = (f32[5,1,4,2048]{3,1,2,0:T(1,128)S(1)}, f32[5,1,4,2048]{3,1,2,0:T(1,128)S(1)}, u32[]{:S(2)}, u32[]{:S(2)}) collective-permute-start(f32[5,1,4,2048]{3,1,2,0:T(1,128)S(1)} %broadcast_select_fusion.5), channel_id=1, source_target_pairs={{0,4},{4,0},{1,5},{5,1},{2,6},{6,2},{3,7},{7,3},{8,12},{12,8},{9,1... | collective-permute-start | bytes 491528 | tf_op jit(solution)/shard_map/ppermute | solution.py:20
  16.6 20.1 %all-to-all-start.1 = ((f32[1,8,2]{2,0,1:T(1,128)}), f32[1,8,2]{2,0,1:T(1,128)S(1)}, u32[]{:S(2)}, u32[]{:S(2)}) async-start(f32[1,8,2]{2,0,1:T(1,128)} %bitcast.48), calls=%async_computation.1 | async-start | bytes 8192 | tf_op jit(solution)/shard_map/all_to_all | solution.py:120
  21.4 6.3 %collective-permute-start.3 = (f32[5,2,512]{2,1,0:T(2,128)S(1)}, f32[5,2,512]{2,1,0:T(2,128)S(1)}, u32[]{:S(2)}, u32[]{:S(2)}) collective-permute-start(f32[5,2,512]{2,1,0:T(2,128)S(1)} %get-tuple-element.17), channel_id=1, source_target_pairs={{1,0},{2,1},{3,2},{4,3},{5,4},{6,5},{7,6},{8,7},{9,8},{10,9},{11,1... | collective-permute-start | bytes 61448 | tf_op jit(solution)/shard_map/ppermute | solution.py:31
  25.8 6.9 %collective-permute-start.4 = (f32[5,2,512]{2,1,0:T(2,128)S(1)}, f32[5,2,512]{2,1,0:T(2,128)S(1)}, u32[]{:S(2)}, u32[]{:S(2)}) collective-permute-start(f32[5,2,512]{2,1,0:T(2,128)S(1)} %get-tuple-element.16), channel_id=1, source_target_pairs={{0,1},{1,2},{2,3},{3,4},{4,5},{5,6},{6,7},{7,8},{8,9},{9,10},{10,1... | collective-permute-start | bytes 61448 | tf_op jit(solution)/shard_map/ppermute | solution.py:28
  33.4 0.8 %copy-start = (f32[32,512]{1,0:T(8,128)S(1)}, f32[32,512]{1,0:T(8,128)}, u32[]{:S(2)}) copy-start(f32[32,512]{1,0:T(8,128)} %param.7) | copy-start | bytes 196612
  36.7 10.3 %all-to-all-start = ((f32[2,8,4096]{2,0,1:T(2,128)}), f32[2,8,4096]{2,0,1:T(2,128)S(1)}, u32[]{:S(2)}, u32[]{:S(2)}) async-start(f32[2,8,4096]{2,0,1:T(2,128)} %copy.32), calls=%async_computation | async-start | bytes 524288 | tf_op jit(solution)/shard_map/all_to_all | solution.py:117
where the time goes:
time: 49.2 us; the launch traced here: 48.7 us
  starting transfers between devices  16.2 us (33%)
  waiting for transfers between devices  15.1 us (31%)
  local copies, waits for them, and re-layouts  9.54 us (19%)
  other arithmetic  6.01 us (12%)
  between operations  1.09 us (2%)
  matrix products  0.78 us (2%)
    ppermute x3, waiting for transfers between devices, from_partner(): return lax.ppermute(block, axis, route)  5.2 us
    ppermute x1, waiting for transfers between devices, with_halo(): lax.ppermute(lax.slice_in_dim(block, block.shape[dim] - width, None, axis...  4.95 us
    all_to_all x1, waiting for transfers between devices, shards(): lax.all_to_all(outgoing.reshape(2, nbis, CAP * flat), 'bis', split_axis=1...  4.94 us
    ppermute x1, starting transfers between devices, with_halo(): lax.ppermute(lax.slice_in_dim(block, 0, width, axis=dim), axis, backward)  4.39 us
    all_to_all x1, starting transfers between devices, shards(): lax.all_to_all(outgoing.reshape(2, nbis, CAP * flat), 'bis', split_axis=1...  3.41 us
    all_to_all x1, starting transfers between devices, shards(): lax.all_to_all(labels.reshape(1, nbis, CAP), 'bis', split_axis=1, concat_...  3.31 us
    ppermute x3, starting transfers between devices, from_partner(): return lax.ppermute(block, axis, route)  3.21 us
    unnamed x9, local copies, waits for them, and re-layouts  2.34 us
  transfers between devices with their start and end apart: 7, of which 4 were waited for; matrix products, arithmetic and copies ran while one was open for 16% of the time, Pallas kernels for 0%

commit v1 on v0

v1 whole, which is shorter than its diff:
```python
import functools

import jax
import jax.numpy as jnp
from jax import lax
from jax.experimental import pallas as pl
from jax.experimental.pallas import tpu as pltpu
from jax.sharding import PartitionSpec as P

BR = 4
CAP = 2
HALF_DT = 0.075
NF = 5
RHO, ENE, VELU, VELV, GAM = range(NF)
FAR_P, FAR_U = 5, 6
SMEM = pl.BlockSpec(memory_space=pltpu.SMEM)
VMEM = pl.BlockSpec(memory_space=pltpu.VMEM)


def sublane(width):
    return lax.broadcasted_iota(jnp.int32, (8, width), 0)


def turn(tile, shift):
    return pltpu.roll(tile, shift, 0)


def where_am_i():
    return lax.axis_index("grp"), lax.axis_index("bis")


def pack_kernel(n, order, state, *outs):
    chips = n // 2
    width = state.shape[2]
    _, me = where_am_i()
    chip = me // 2
    sub = sublane(width)
    first = me == 0
    chip_bufs, across = outs[:chips], outs[chips]

    def tile_of(field, block):
        return state[field, pl.ds(pl.multiple_of(block // 2 * 8, 8), 8), :]

    def halo(index):
        block = order[0, index]
        odd = block % 2 * 4
        near = odd + jnp.where(first, 0, BR - 1)
        far = odd + jnp.where(first, 1, BR - 2)
        tiles = [tile_of(field, block) for field in range(NF)]
        press = (tiles[GAM] - 1.0) * tiles[RHO] * tiles[ENE]
        out = turn(tiles[0], (8 - near) % 8)
        for field in range(1, NF):
            out = jnp.where(sub == field, turn(tiles[field], (field + 8 - near) % 8), out)
        out = jnp.where(sub == FAR_P, turn(press, (FAR_P + 8 - far) % 8), out)
        return jnp.where(sub == FAR_U, turn(tiles[VELU], (FAR_U + 8 - far) % 8), out)

    for mask in range(chips):
        goal = chip ^ mask
        low = order[0, 2 * goal]
        high = order[0, 2 * goal + 1]
        for field in range(NF):
            even = turn(tile_of(field, low), low % 2 * 4)
            odd = turn(tile_of(field, high), 4 - high % 2 * 4)
            chip_bufs[mask][8 * field : 8 * field + 8, :] = jnp.where(sub < 4, even, odd)
        beyond = jnp.where(first, jnp.minimum(2 * goal + 2, n - 1), jnp.maximum(2 * goal - 1, 0))
        chip_bufs[mask][8 * NF :, :] = halo(beyond)
    across[...] = halo(jnp.where(first, 0, n - 1))


def step_kernel(n, *refs):
    chips = n // 2
    refs = list(refs)
    take = lambda count: [refs.pop(0) for _ in range(count)]
    owner, slot, owner_sib, slot_sib = take(4)
    mine, theirs = take(chips), take(chips)
    across, across_sib, sweep, sweep_sib = take(4)
    (vel,) = take(1)
    sends = take(chips)
    fld, prs, vols, coef, halo, bins, tags, count = take(8)
    grp, me = where_am_i()
    chip, core = me // 2, me % 2
    width = sweep.shape[1]
    rows = sweep.shape[0]
    tiles = 2 * chips
    sub = sublane(width)
    lane = lax.broadcasted_iota(jnp.int32, (8, width), 1)
    is_low = core == 0

    def pair(own, sib):
        return jnp.where(is_low, own, sib), jnp.where(is_low, sib, own)

    def at(tile):
        return pl.ds(pl.multiple_of(tile * 8, 8), 8)

    for mask in range(chips):
        source = chip ^ mask
        for field in range(NF):
            span = pl.ds(8 * field, 8)
            even, odd = pair(mine[mask][span, :], theirs[mask][span, :])
            fld[field, at(1 + source), :] = jnp.where(sub < 4, even, turn(odd, 4))
            fld[field, at(1 + chips + source), :] = jnp.where(sub < 4, turn(even, 4), odd)
        even, odd = pair(mine[mask][8 * NF :, :], theirs[mask][8 * NF :, :])
        halo[0, source] = even
        halo[1, source] = odd
    even, odd = pair(across[...], across_sib[...])
    top = jnp.where(chip == 0, even, halo[1, chips - 1])
    bottom = jnp.where(chip == chips - 1, odd, halo[0, 0])

    def line(tile, index):
        return jnp.broadcast_to(tile[index : index + 1, :], (8, width))

    for tile, place, near in ((top, 0, 7), (bottom, tiles + 1, 0)):
        span = at(place)
        for field in (RHO, ENE, VELV, GAM):
            fld[field, span, :] = line(tile, field)
        fld[VELU, span, :] = jnp.where(sub == near, line(tile, VELU), line(tile, FAR_U))
        press = (line(tile, GAM) - 1.0) * line(tile, RHO) * line(tile, ENE)
        prs[0, span, :] = jnp.where(sub == near, press, line(tile, FAR_P))

    def left_right(x):
        left = jnp.where(lane == 0, 0.0, pltpu.roll(x, 1, 1))
        right = jnp.where(lane == width - 1, 0.0, pltpu.roll(x, width - 1, 1))
        return right - left

    def down_up(ref, index, tile, x, clip=False):
        before = ref[index, at(jnp.maximum(tile - 1, 0) if clip else tile - 1), :]
        after = ref[index, at(jnp.minimum(tile + 1, tiles + 1) if clip else tile + 1), :]
        return turn(jnp.where(sub == 0, after, x), 7) - turn(jnp.where(sub == 7, before, x), 1)

    def pressure(tile, _):
        span = at(tile)
        prs[0, span, :] = (fld[GAM, span, :] - 1.0) * fld[RHO, span, :] * fld[ENE, span, :]
        return 0

    lax.fori_loop(1, tiles + 1, pressure, 0, unroll=n <= 8)

    def first(tile, _):
        span = at(tile)
        velu, velv, press = fld[VELU, span, :], fld[VELV, span, :], prs[0, span, :]
        push = HALF_DT * (down_up(fld, VELU, tile, velu, True) + left_right(velv))
        grow = 1.0 + push
        scale = HALF_DT / fld[RHO, span, :]
        keep = 1.0 - (fld[GAM, span, :] - 1.0) * push
        nxt_p = press * keep / grow
        nxt_u = velu - down_up(prs, 0, tile, press, True) * scale
        nxt_v = velv - left_right(press) * scale
        prs[1, span, :] = nxt_p
        vols[0, span, :] = nxt_u
        vols[1, span, :] = nxt_v
        vols[2, span, :] = grow
        vols[3, span, :] = fld[ENE, span, :] * keep
        coef[span, :] = scale * grow
        return 0

    lax.fori_loop(0, tiles + 2, first, 0, unroll=n <= 8)
    inside_top = jnp.logical_or(grp > 0, chip > 0)
    inside_bottom = jnp.logical_or(grp < lax.axis_size("grp") - 1, chip < chips - 1)
    for place, inside in ((0, inside_top), (tiles + 1, inside_bottom)):
        span = at(place)
        prs[1, span, :] = jnp.where(inside, prs[1, span, :], 0.0)
        vols[0, span, :] = jnp.where(inside, vols[0, span, :], 0.0)

    def velocity(index, _):
        tile = 1 + core * chips + index
        span, dest = at(tile), at(index)
        press, scale = prs[1, span, :], coef[span, :]
        vel[0, dest, :] = vols[0, span, :] - down_up(prs, 1, tile, press) * scale
        vel[1, dest, :] = vols[1, span, :] - left_right(press) * scale
        return 0

    lax.fori_loop(0, chips, velocity, 0, unroll=n <= 8)

    for mask in range(chips + 1):
        count[mask] = 0
        tags[mask] = jnp.full((8, 128), -1.0, jnp.float32)
    sub128 = sublane(128)

    def cyclic(x):
        return jnp.where(sub % BR == 0, turn(x, 8 - (BR - 1)), turn(x, 1))

    def place(tile_out, who, where_to):
        fits = who % 2 == core
        mask = jnp.where(fits, (who // 2) ^ chip, chips)
        rank = count[mask]
        count[mask] = jnp.where(fits, rank + 1, 0)
        bins[mask, rank] = tile_out
        tags[mask] = jnp.where(sub128 == rank, where_to.astype(jnp.float32), tags[mask])

    def second(device, index):
        tile = 1 + device * chips + index
        span = at(tile)
        push = HALF_DT * (down_up(vols, 0, tile, vols[0, span, :]) + left_right(vols[1, span, :]))
        volume = vols[2, span, :] * (1.0 + push)
        heat_e = vols[3, span, :] * (1.0 - (fld[GAM, span, :] - 1.0) * push)
        mass = fld[RHO, span, :]
        heat = mass * heat_e
        from_own = (core == 0) if device == 0 else (core == 1)
        swept = jnp.where(from_own, sweep[at(index), :], sweep_sib[at(index), :])
        frac = swept * volume / (1.0 + volume)
        mass_go, heat_go = frac * mass, frac * heat
        mass_part = mass - mass_go + cyclic(mass_go)
        heat_part = heat - heat_go + cyclic(heat_go)
        for bit, tile_out in (
            (0, jnp.where(sub < 4, mass_part, turn(heat_part, 4))),
            (1, jnp.where(sub < 4, turn(mass_part, 4), heat_part)),
        ):
            block = 2 * index + bit
            who = jnp.where(from_own, owner[block, 0], owner_sib[block, 0])
            where_to = jnp.where(from_own, slot[block], slot_sib[block])
            place(tile_out, who, where_to)

    for device in range(2):
        lax.fori_loop(0, chips, lambda index, _, device=device: (second(device, index), 0)[1], 0, unroll=n <= 8)

    for mask in range(chips):
        for rank in range(2 * CAP):
            for part in range(width // 128):
                sends[mask][rank * (width // 128) + part] = bins[mask, rank, :, part * 128 : part * 128 + 128]
        sends[mask][2 * CAP * (width // 128)] = tags[mask]


def land_kernel(n, *refs):
    chips = n // 2
    arrived = refs[:chips]
    mass, energy = refs[chips:]
    parts = mass.shape[1] // 128
    sub = sublane(128)

    def tile_pair(index, _):
        span = pl.ds(pl.multiple_of(index * 8, 8), 8)
        sums = [[jnp.zeros((8, 128), jnp.float32) for _ in range(parts)] for _ in range(2)]
        for buf in arrived:
            tag_tile = buf[2 * CAP * parts]
            for rank in range(2 * CAP):
                tag = jnp.broadcast_to(tag_tile[rank : rank + 1, :], (8, 128))
                for bit in range(2):
                    hit = tag == (2 * index + bit) * 1.0
                    for part in range(parts):
                        sums[bit][part] += jnp.where(hit, buf[rank * parts + part], 0.0)
        for part in range(parts):
            cols = slice(part * 128, part * 128 + 128)
            even, odd = sums[0][part], sums[1][part]
            mass[span, cols] = jnp.where(sub < 4, even, turn(odd, 4))
            energy[span, cols] = jnp.where(sub < 4, turn(even, 4), odd)
        return 0

    lax.fori_loop(0, chips, tile_pair, 0, unroll=n <= 8)


def shards(state, order, sweep, owner, slot_target):
    n = lax.axis_size("bis")
    groups = lax.axis_size("grp")
    chips = n // 2
    rows, width = sweep.shape
    parts = width // 128
    f32 = jnp.float32
    params = pltpu.CompilerParams(vmem_limit_bytes=48 * 1024 * 1024)

    def to_sibling(x):
        return lax.ppermute(x, "bis", [(i, i ^ 1) for i in range(n)])

    def to_chip(x, mask):
        return lax.ppermute(x, "bis", [(i, i ^ 2 * mask) for i in range(n)]) if mask else x

    sweep_sib, owner_sib, slot_sib = to_sibling(sweep), to_sibling(owner), to_sibling(slot_target)

    packed = pl.pallas_call(
        functools.partial(pack_kernel, n),
        out_shape=[jax.ShapeDtypeStruct((8 * (NF + 1), width), f32)] * chips
        + [jax.ShapeDtypeStruct((8, width), f32)],
        in_specs=[SMEM, VMEM],
        out_specs=[VMEM] * (chips + 1),
        compiler_params=params,
        name="pack",
    )(order, state)
    links = []
    for grp in range(groups - 1):
        low, high = grp * n + n - 1, (grp + 1) * n
        links += [(low, high), (high, low)]
    across = lax.ppermute(packed[chips], ("grp", "bis"), links)
    mine = [to_chip(packed[mask], mask) for mask in range(chips)]
    theirs = [to_sibling(x) for x in mine]
    across_sib = to_sibling(across)

    stack = (2 * chips + 2) * 8
    send_shape = (2 * CAP * parts + 1, 8, 128)
    out = pl.pallas_call(
        functools.partial(step_kernel, n),
        out_shape=[jax.ShapeDtypeStruct((2, rows, width), f32)]
        + [jax.ShapeDtypeStruct(send_shape, f32)] * chips,
        in_specs=[SMEM] * 4 + [VMEM] * (2 * chips + 4),
        out_specs=[VMEM] * (chips + 1),
        scratch_shapes=[
            pltpu.VMEM((NF, stack, width), f32),
            pltpu.VMEM((2, stack, width), f32),
            pltpu.VMEM((4, stack, width), f32),
            pltpu.VMEM((stack, width), f32),
            pltpu.VMEM((2, chips, 8, width), f32),
            pltpu.VMEM((chips + 1, 2 * CAP, 8, width), f32),
            pltpu.VMEM((chips + 1, 8, 128), f32),
            pltpu.SMEM((chips + 1,), jnp.int32),
        ],
        compiler_params=params,
        name="substeps",
    )(owner, slot_target, owner_sib, slot_sib, *mine, *theirs, across, across_sib, sweep, sweep_sib)
    vel = out[0]
    arrived = [to_chip(out[1 + mask], mask) for mask in range(chips)]
    mass, energy = pl.pallas_call(
        functools.partial(land_kernel, n),
        out_shape=[jax.ShapeDtypeStruct((rows, width), f32)] * 2,
        in_specs=[VMEM] * chips,
        out_specs=[VMEM] * 2,
        compiler_params=params,
        name="land",
    )(*arrived)
    return mass, energy, vel


def solution(mesh):
    placed = (
        P(None, ("grp", "bis"), None),
        P(("grp", "bis"), None),
        P(("grp", "bis"), None),
        P(("grp", "bis"), None),
        P(("grp", "bis")),
    )
    return jax.shard_map(
        shards,
        mesh=mesh,
        in_specs=placed,
        out_specs=(P(("grp", "bis"), None), P(("grp", "bis"), None), P(None, ("grp", "bis"), None)),
        check_vma=False,
    )
```

time: 49.2 us -> 29.5 us (0.60)
  the two profiles are of different devices: /device:TPU:8 before, /device:TPU:0 now
where the time goes in v1:
time: 29.5 us; the launch traced here: 29.4 us
  starting transfers between devices  12.8 us (43%)
  waiting for transfers between devices  10.6 us (36%)
  Pallas kernels  3.58 us (12%)
  local copies, waits for them, and re-layouts  1.71 us (6%)
  between operations  0.7 us (2%)
    ppermute x6, starting transfers between devices, to_chip(): lax.ppermute(x, 'bis', [(i, i ^ 2 * mask) for i in range(n)])  10.2 us
    ppermute x6, waiting for transfers between devices, to_chip(): lax.ppermute(x, 'bis', [(i, i ^ 2 * mask) for i in range(n)])  8.3 us
    ppermute x8, waiting for transfers between devices, to_sibling(): return lax.ppermute(x, 'bis', [(i, i ^ 1) for i in range(n)])  2.29 us
    pallas_call x1, Pallas kernels, shards(): pl.pallas_call(functools.partial(step_kernel, n), out_shape=[jax.ShapeDty...  1.96 us
    ppermute x8, starting transfers between devices, to_sibling(): return lax.ppermute(x, 'bis', [(i, i ^ 1) for i in range(n)])  1.94 us
    unnamed x11, local copies, waits for them, and re-layouts  1.71 us
    pallas_call x1, Pallas kernels, shards(): pl.pallas_call(functools.partial(land_kernel, n), out_shape=[jax.ShapeDty...  0.85 us
    pallas_call x1, Pallas kernels, shards(): pl.pallas_call(functools.partial(pack_kernel, n), out_shape=[jax.ShapeDty...  0.78 us
  transfers between devices with their start and end apart: 15, of which 7 were waited for; matrix products, arithmetic and copies ran while one was open for 0% of the time, Pallas kernels for 0%

profile of v1, /device:TPU:0, one launch (start us, length us, event | category | flops | bytes accessed | tf_op | source)
XLA Modules:
  0.0 29.4 jit_solution(17695822762302707778)
XLA Ops:
  0.6 1.0 %copy-done = f32[5,32,512]{2,1,0:T(8,128)S(1)} copy-done((f32[5,32,512]{2,1,0:T(8,128)S(1)}, f32[5,32,512]{2,1,0:T(8,128)}, u32[]{:S(2)}) %copy-start) | copy-done | bytes 327704
  1.6 0.7 %copy-done.2 = s32[1,8]{1,0:T(1,128)S(1)} copy-done((s32[1,8]{1,0:T(1,128)S(1)}, s32[1,8]{1,0:T(1,128)}, u32[]{:S(2)}) %copy-start.2) | copy-done | bytes 56
  2.3 0.8 %pack.1 = (f32[48,512]{1,0:T(8,128)S(1)}, f32[48,512]{1,0:T(8,128)S(1)}, f32[48,512]{1,0:T(8,128)S(1)}, f32[48,512]{1,0:T(8,128)S(1)}, f32[8,512]{1,0:T(8,128)S(1)}) custom-call(s32[1,8]{1,0:T(1,128)S(1)} %copy-done.2, f32[5,32,512]{2,1,0:T(8,128)S(1)} %copy-done), custom_call_target="tpu_custom_call" | custom-call | tf_op jit(solution)/shard_map/pack/pallas_call | solution.py:267
  3.0 3.0 %collective-permute-start.2 = (f32[48,512]{1,0:T(8,128)S(1)}, f32[48,512]{1,0:T(8,128)S(1)}, u32[]{:S(2)}, u32[]{:S(2)}) collective-permute-start(f32[48,512]{1,0:T(8,128)S(1)} %get-tuple-element.16), channel_id=1, source_target_pairs={{0,2},{1,3},{2,0},{3,1},{4,6},{5,7},{6,4},{7,5},{8,10},{9,11},{10,... | collective-permute-start | bytes 294920 | tf_op jit(solution)/shard_map/ppermute | solution.py:263
  6.1 1.5 %collective-permute-start.3 = (f32[48,512]{1,0:T(8,128)S(1)}, f32[48,512]{1,0:T(8,128)S(1)}, u32[]{:S(2)}, u32[]{:S(2)}) collective-permute-start(f32[48,512]{1,0:T(8,128)S(1)} %get-tuple-element.17), channel_id=1, source_target_pairs={{0,4},{1,5},{2,6},{3,7},{4,0},{5,1},{6,2},{7,3},{8,12},{9,13},{10,... | collective-permute-start | bytes 294920 | tf_op jit(solution)/shard_map/ppermute | solution.py:263
  7.6 0.0 collective-permute-start.4
  7.6 0.0 collective-permute-start.1
  7.6 0.1 copy.9.refs_0_
  7.7 0.5 %collective-permute-start = (s32[8,1]{1,0:T(8,128)S(1)}, s32[8,1]{1,0:T(8,128)S(1)}, u32[]{:S(2)}, u32[]{:S(2)}) collective-permute-start(s32[8,1]{1,0:T(8,128)S(1)} %copy.9.refs_0_), channel_id=1, source_target_pairs={{0,1},{1,0},{2,3},{3,2},{4,5},{5,4},{6,7},{7,6},{8,9},{9,8},{10,11... | collective-permute-start | bytes 104 | tf_op jit(solution)/shard_map/ppermute | solution.py:260
  8.2 0.5 %collective-permute-done.1.refs_3_ = s32[8]{0:T(128)S(1)} collective-permute-done((s32[8]{0:T(128)S(1)}, s32[8]{0:T(128)S(1)}, u32[]{:S(2)}, u32[]{:S(2)}) %collective-permute-start.1) | collective-permute-done | bytes 64 | tf_op jit(solution)/shard_map/ppermute | solution.py:260
  8.7 0.7 %collective-permute-start.9 = (f32[8,512]{1,0:T(8,128)S(1)}, f32[8,512]{1,0:T(8,128)S(1)}, u32[]{:S(2)}, u32[]{:S(2)}) collective-permute-start(f32[8,512]{1,0:T(8,128)S(1)} %get-tuple-element.19), channel_id=1, source_target_pairs={{7,8},{8,7},{15,16},{16,15},{23,24},{24,23}} | collective-permute-start | bytes 49160 | tf_op jit(solution)/shard_map/ppermute | solution.py:280
  9.4 0.0 collective-permute-done.refs_2_
  9.4 0.3 collective-permute-start.5
  9.7 0.0 collective-permute-done.2.refs_5_
  9.7 0.3 %collective-permute-start.6 = (f32[48,512]{1,0:T(8,128)S(1)}, f32[48,512]{1,0:T(8,128)S(1)}, u32[]{:S(2)}, u32[]{:S(2)}) collective-permute-start(f32[48,512]{1,0:T(8,128)S(1)} %collective-permute-done.2.refs_5_), channel_id=1, source_target_pairs={{0,1},{1,0},{2,3},{3,2},{4,5},{5,4},{6,7},{7,6},{8,9},{9,8},{10,11... | collective-permute-start | bytes 294920 | tf_op jit(solution)/shard_map/ppermute | solution.py:260
  10.0 1.7 %collective-permute-done.3.refs_6_ = f32[48,512]{1,0:T(8,128)S(1)} collective-permute-done((f32[48,512]{1,0:T(8,128)S(1)}, f32[48,512]{1,0:T(8,128)S(1)}, u32[]{:S(2)}, u32[]{:S(2)}) %collective-permute-start.3) | collective-permute-done | bytes 98336 | tf_op jit(solution)/shard_map/ppermute | solution.py:263
  11.7 0.0 collective-permute-start.7
  11.7 1.4 %collective-permute-done.4.refs_7_ = f32[48,512]{1,0:T(8,128)S(1)} collective-permute-done((f32[48,512]{1,0:T(8,128)S(1)}, f32[48,512]{1,0:T(8,128)S(1)}, u32[]{:S(2)}, u32[]{:S(2)}) %collective-permute-start.4) | collective-permute-done | bytes 98336 | tf_op jit(solution)/shard_map/ppermute | solution.py:263
  13.1 0.0 collective-permute-start.8
  13.1 0.0 collective-permute-done.9.refs_12_
  13.1 0.5 %collective-permute-start.10 = (f32[8,512]{1,0:T(8,128)S(1)}, f32[8,512]{1,0:T(8,128)S(1)}, u32[]{:S(2)}, u32[]{:S(2)}) collective-permute-start(f32[8,512]{1,0:T(8,128)S(1)} %collective-permute-done.9.refs_12_), channel_id=1, source_target_pairs={{0,1},{1,0},{2,3},{3,2},{4,5},{5,4},{6,7},{7,6},{8,9},{9,8},{10,11... | collective-permute-start | bytes 49160 | tf_op jit(solution)/shard_map/ppermute | solution.py:260
  13.6 0.8 %collective-permute-done.10.refs_13_ = f32[8,512]{1,0:T(8,128)S(1)} collective-permute-done((f32[8,512]{1,0:T(8,128)S(1)}, f32[8,512]{1,0:T(8,128)S(1)}, u32[]{:S(2)}, u32[]{:S(2)}) %collective-permute-start.10) | collective-permute-done | bytes 16416 | tf_op jit(solution)/shard_map/ppermute | solution.py:260
  14.4 0.3 %collective-permute-start.11 = (f32[32,512]{1,0:T(8,128)S(1)}, f32[32,512]{1,0:T(8,128)S(1)}, u32[]{:S(2)}, u32[]{:S(2)}) collective-permute-start(f32[32,512]{1,0:T(8,128)S(1)} %copy-done.1), channel_id=1, source_target_pairs={{0,1},{1,0},{2,3},{3,2},{4,5},{5,4},{6,7},{7,6},{8,9},{9,8},{10,11... | collective-permute-start | bytes 196616 | tf_op jit(solution)/shard_map/ppermute | solution.py:260
  14.8 0.9 %collective-permute-done.11.refs_15_ = f32[32,512]{1,0:T(8,128)S(1)} collective-permute-done((f32[32,512]{1,0:T(8,128)S(1)}, f32[32,512]{1,0:T(8,128)S(1)}, u32[]{:S(2)}, u32[]{:S(2)}) %collective-permute-start.11) | collective-permute-done | bytes 65568 | tf_op jit(solution)/shard_map/ppermute | solution.py:260
  15.7 0.0 collective-permute-done.7.refs_10_
  15.7 0.0 collective-permute-done.8.refs_11_
  15.7 2.0 %substeps.1 = (f32[2,32,512]{2,1,0:T(8,128)}, f32[17,8,128]{2,1,0:T(8,128)S(1)}, f32[17,8,128]{2,1,0:T(8,128)S(1)}, f32[17,8,128]{2,1,0:T(8,128)S(1)}, f32[17,8,128]{2,1,0:T(8,128)S(1)}) custom-call(s32[8,1]{1,0:T(8,128)S(1)} %copy.9.refs_0_, s32[8]{0:T(128)S(1)} %copy-done.3, s32[8,1]{1,0:T(8,128)S(1)} %collective-permute-done.refs_2_, ...), custom_call_target="tpu_custom_call" | custom-call | tf_op jit(solution)/shard_map/substeps/pallas_call | solution.py:287
  17.7 0.6 %collective-permute-start.12 = (f32[17,8,128]{2,1,0:T(8,128)S(1)}, f32[17,8,128]{2,1,0:T(8,128)S(1)}, u32[]{:S(2)}, u32[]{:S(2)}) collective-permute-start(f32[17,8,128]{2,1,0:T(8,128)S(1)} %get-tuple-element.21), channel_id=1, source_target_pairs={{0,2},{1,3},{2,0},{3,1},{4,6},{5,7},{6,4},{7,5},{8,10},{9,11},{10,... | collective-permute-start | bytes 208904 | tf_op jit(solution)/shard_map/ppermute | solution.py:263
  18.3 5.0 %collective-permute-start.13 = (f32[17,8,128]{2,1,0:T(8,128)S(1)}, f32[17,8,128]{2,1,0:T(8,128)S(1)}, u32[]{:S(2)}, u32[]{:S(2)}) collective-permute-start(f32[17,8,128]{2,1,0:T(8,128)S(1)} %get-tuple-element.22), channel_id=1, source_target_pairs={{0,4},{1,5},{2,6},{3,7},{4,0},{5,1},{6,2},{7,3},{8,12},{9,13},{10,... | collective-permute-start | bytes 208904 | tf_op jit(solution)/shard_map/ppermute | solution.py:263
  23.3 3.3 %collective-permute-done.13.refs_2_ = f32[17,8,128]{2,1,0:T(8,128)S(1)} collective-permute-done((f32[17,8,128]{2,1,0:T(8,128)S(1)}, f32[17,8,128]{2,1,0:T(8,128)S(1)}, u32[]{:S(2)}, u32[]{:S(2)}) %collective-permute-start.13) | collective-permute-done | bytes 69664 | tf_op jit(solution)/shard_map/ppermute | solution.py:263
  26.7 1.9 %collective-permute-done.14.refs_3_ = f32[17,8,128]{2,1,0:T(8,128)S(1)} collective-permute-done((f32[17,8,128]{2,1,0:T(8,128)S(1)}, f32[17,8,128]{2,1,0:T(8,128)S(1)}, u32[]{:S(2)}, u32[]{:S(2)}) %collective-permute-start.14) | collective-permute-done | bytes 69664 | tf_op jit(solution)/shard_map/ppermute | solution.py:263
  28.5 0.8 %land.1 = (f32[32,512]{1,0:T(8,128)}, f32[32,512]{1,0:T(8,128)}) custom-call(f32[17,8,128]{2,1,0:T(8,128)S(1)} %get-tuple-element.20.refs_0_, f32[17,8,128]{2,1,0:T(8,128)S(1)} %collective-permute-done.12.refs_1_, f32[17,8,128]{2,1,0:T(8,128)S(1)} %collective-permute-done.13.refs_2_, f32[17,8,128]{2,1,0:T(8,128)S(1)} %collective-permute-done.14.refs_3_), custom_call_target="tpu_custom_call" | custom-call | tf_op jit(solution)/shard_map/land/pallas_call | solution.py:308
  (12 shorter events, 0.0 us)
Async XLA Ops:
  0.6 1.0 %copy-start = (f32[5,32,512]{2,1,0:T(8,128)S(1)}, f32[5,32,512]{2,1,0:T(8,128)}, u32[]{:S(2)}) copy-start(f32[5,32,512]{2,1,0:T(8,128)} %state.1) | copy-start | bytes 983044
  1.6 0.7 %copy-start.2 = (s32[1,8]{1,0:T(1,128)S(1)}, s32[1,8]{1,0:T(1,128)}, u32[]{:S(2)}) copy-start(s32[1,8]{1,0:T(1,128)} %order.1) | copy-start | bytes 100
  2.3 12.2 %copy-start.1 = (f32[32,512]{1,0:T(8,128)S(1)}, f32[32,512]{1,0:T(8,128)}, u32[]{:S(2)}) copy-start(f32[32,512]{1,0:T(8,128)} %refs_14_.1) | copy-start | bytes 196612
  3.0 6.6 %collective-permute-start.2 = (f32[48,512]{1,0:T(8,128)S(1)}, f32[48,512]{1,0:T(8,128)S(1)}, u32[]{:S(2)}, u32[]{:S(2)}) collective-permute-start(f32[48,512]{1,0:T(8,128)S(1)} %get-tuple-element.16), channel_id=1, source_target_pairs={{0,2},{1,3},{2,0},{3,1},{4,6},{5,7},{6,4},{7,5},{8,10},{9,11},{10,... | collective-permute-start | bytes 294920 | tf_op jit(solution)/shard_map/ppermute | solution.py:263
  6.0 1.6 %copy-start.3 = (s32[8]{0:T(128)S(1)}, s32[8]{0:T(128)}, u32[]{:S(2)}) copy-start(s32[8]{0:T(128)} %refs_1_.1) | copy-start | bytes 100
  6.1 1.6 %copy-start.4 = (s32[8,1]{0,1:T(1,128)S(1)}, s32[8,1]{0,1:T(1,128)}, u32[]{:S(2)}) copy-start(s32[8,1]{0,1:T(1,128)} %param.8) | copy-start | bytes 100
  6.1 5.7 %collective-permute-start.3 = (f32[48,512]{1,0:T(8,128)S(1)}, f32[48,512]{1,0:T(8,128)S(1)}, u32[]{:S(2)}, u32[]{:S(2)}) collective-permute-start(f32[48,512]{1,0:T(8,128)S(1)} %get-tuple-element.17), channel_id=1, source_target_pairs={{0,4},{1,5},{2,6},{3,7},{4,0},{5,1},{6,2},{7,3},{8,12},{9,13},{10,... | collective-permute-start | bytes 294920 | tf_op jit(solution)/shard_map/ppermute | solution.py:263
  7.6 5.5 %collective-permute-start.4 = (f32[48,512]{1,0:T(8,128)S(1)}, f32[48,512]{1,0:T(8,128)S(1)}, u32[]{:S(2)}, u32[]{:S(2)}) collective-permute-start(f32[48,512]{1,0:T(8,128)S(1)} %get-tuple-element.18), channel_id=1, source_target_pairs={{0,6},{1,7},{2,4},{3,5},{4,2},{5,3},{6,0},{7,1},{8,14},{9,15},{10,... | collective-permute-start | bytes 294920 | tf_op jit(solution)/shard_map/ppermute | solution.py:263
  7.6 1.1 %collective-permute-start.1 = (s32[8]{0:T(128)S(1)}, s32[8]{0:T(128)S(1)}, u32[]{:S(2)}, u32[]{:S(2)}) collective-permute-start(s32[8]{0:T(128)S(1)} %copy-done.3), channel_id=1, source_target_pairs={{0,1},{1,0},{2,3},{3,2},{4,5},{5,4},{6,7},{7,6},{8,9},{9,8},{10,11... | collective-permute-start | bytes 104 | tf_op jit(solution)/shard_map/ppermute | solution.py:260
  7.7 1.7 %collective-permute-start = (s32[8,1]{1,0:T(8,128)S(1)}, s32[8,1]{1,0:T(8,128)S(1)}, u32[]{:S(2)}, u32[]{:S(2)}) collective-permute-start(s32[8,1]{1,0:T(8,128)S(1)} %copy.9.refs_0_), channel_id=1, source_target_pairs={{0,1},{1,0},{2,3},{3,2},{4,5},{5,4},{6,7},{7,6},{8,9},{9,8},{10,11... | collective-permute-start | bytes 104 | tf_op jit(solution)/shard_map/ppermute | solution.py:260
  8.7 4.4 %collective-permute-start.9 = (f32[8,512]{1,0:T(8,128)S(1)}, f32[8,512]{1,0:T(8,128)S(1)}, u32[]{:S(2)}, u32[]{:S(2)}) collective-permute-start(f32[8,512]{1,0:T(8,128)S(1)} %get-tuple-element.19), channel_id=1, source_target_pairs={{7,8},{8,7},{15,16},{16,15},{23,24},{24,23}} | collective-permute-start | bytes 49160 | tf_op jit(solution)/shard_map/ppermute | solution.py:280
  9.4 6.3 %collective-permute-start.5 = (f32[48,512]{1,0:T(8,128)S(1)}, f32[48,512]{1,0:T(8,128)S(1)}, u32[]{:S(2)}, u32[]{:S(2)}) collective-permute-start(f32[48,512]{1,0:T(8,128)S(1)} %get-tuple-element.15.refs_4_), channel_id=1, source_target_pairs={{0,1},{1,0},{2,3},{3,2},{4,5},{5,4},{6,7},{7,6},{8,9},{9,8},{10,11... | collective-permute-start | bytes 294920 | tf_op jit(solution)/shard_map/ppermute | solution.py:260
  9.7 6.0 %collective-permute-start.6 = (f32[48,512]{1,0:T(8,128)S(1)}, f32[48,512]{1,0:T(8,128)S(1)}, u32[]{:S(2)}, u32[]{:S(2)}) collective-permute-start(f32[48,512]{1,0:T(8,128)S(1)} %collective-permute-done.2.refs_5_), channel_id=1, source_target_pairs={{0,1},{1,0},{2,3},{3,2},{4,5},{5,4},{6,7},{7,6},{8,9},{9,8},{10,11... | collective-permute-start | bytes 294920 | tf_op jit(solution)/shard_map/ppermute | solution.py:260
  11.7 4.0 %collective-permute-start.7 = (f32[48,512]{1,0:T(8,128)S(1)}, f32[48,512]{1,0:T(8,128)S(1)}, u32[]{:S(2)}, u32[]{:S(2)}) collective-permute-start(f32[48,512]{1,0:T(8,128)S(1)} %collective-permute-done.3.refs_6_), channel_id=1, source_target_pairs={{0,1},{1,0},{2,3},{3,2},{4,5},{5,4},{6,7},{7,6},{8,9},{9,8},{10,11... | collective-permute-start | bytes 294920 | tf_op jit(solution)/shard_map/ppermute | solution.py:260
  13.1 2.6 %collective-permute-start.8 = (f32[48,512]{1,0:T(8,128)S(1)}, f32[48,512]{1,0:T(8,128)S(1)}, u32[]{:S(2)}, u32[]{:S(2)}) collective-permute-start(f32[48,512]{1,0:T(8,128)S(1)} %collective-permute-done.4.refs_7_), channel_id=1, source_target_pairs={{0,1},{1,0},{2,3},{3,2},{4,5},{5,4},{6,7},{7,6},{8,9},{9,8},{10,11... | collective-permute-start | bytes 294920 | tf_op jit(solution)/shard_map/ppermute | solution.py:260
  13.1 1.3 %collective-permute-start.10 = (f32[8,512]{1,0:T(8,128)S(1)}, f32[8,512]{1,0:T(8,128)S(1)}, u32[]{:S(2)}, u32[]{:S(2)}) collective-permute-start(f32[8,512]{1,0:T(8,128)S(1)} %collective-permute-done.9.refs_12_), channel_id=1, source_target_pairs={{0,1},{1,0},{2,3},{3,2},{4,5},{5,4},{6,7},{7,6},{8,9},{9,8},{10,11... | collective-permute-start | bytes 49160 | tf_op jit(solution)/shard_map/ppermute | solution.py:260
  14.4 1.3 %collective-permute-start.11 = (f32[32,512]{1,0:T(8,128)S(1)}, f32[32,512]{1,0:T(8,128)S(1)}, u32[]{:S(2)}, u32[]{:S(2)}) collective-permute-start(f32[32,512]{1,0:T(8,128)S(1)} %copy-done.1), channel_id=1, source_target_pairs={{0,1},{1,0},{2,3},{3,2},{4,5},{5,4},{6,7},{7,6},{8,9},{9,8},{10,11... | collective-permute-start | bytes 196616 | tf_op jit(solution)/shard_map/ppermute | solution.py:260
  17.7 5.6 %collective-permute-start.12 = (f32[17,8,128]{2,1,0:T(8,128)S(1)}, f32[17,8,128]{2,1,0:T(8,128)S(1)}, u32[]{:S(2)}, u32[]{:S(2)}) collective-permute-start(f32[17,8,128]{2,1,0:T(8,128)S(1)} %get-tuple-element.21), channel_id=1, source_target_pairs={{0,2},{1,3},{2,0},{3,1},{4,6},{5,7},{6,4},{7,5},{8,10},{9,11},{10,... | collective-permute-start | bytes 208904 | tf_op jit(solution)/shard_map/ppermute | solution.py:263
  18.3 8.3 %collective-permute-start.13 = (f32[17,8,128]{2,1,0:T(8,128)S(1)}, f32[17,8,128]{2,1,0:T(8,128)S(1)}, u32[]{:S(2)}, u32[]{:S(2)}) collective-permute-start(f32[17,8,128]{2,1,0:T(8,128)S(1)} %get-tuple-element.22), channel_id=1, source_target_pairs={{0,4},{1,5},{2,6},{3,7},{4,0},{5,1},{6,2},{7,3},{8,12},{9,13},{10,... | collective-permute-start | bytes 208904 | tf_op jit(solution)/shard_map/ppermute | solution.py:263
  23.3 5.2 %collective-permute-start.14 = (f32[17,8,128]{2,1,0:T(8,128)S(1)}, f32[17,8,128]{2,1,0:T(8,128)S(1)}, u32[]{:S(2)}, u32[]{:S(2)}) collective-permute-start(f32[17,8,128]{2,1,0:T(8,128)S(1)} %get-tuple-element.23), channel_id=1, source_target_pairs={{0,6},{1,7},{2,4},{3,5},{4,2},{5,3},{6,0},{7,1},{8,14},{9,15},{10,... | collective-permute-start | bytes 208904 | tf_op jit(solution)/shard_map/ppermute | solution.py:263

commit v2 on v1

--- a/solution.py
+++ b/solution.py
@@ -29,20 +29,34 @@
     return lax.axis_index("grp"), lax.axis_index("bis")
 
 
-def pack_kernel(n, order, state, *outs):
+def pack_kernel(n, *refs):
     chips = n // 2
+    order_in, owner_in, slot_in, sweep_in, state_in = refs[:5]
+    chip_bufs, across = refs[5 : 5 + chips], refs[5 + chips]
+    order, owner, slot, state, sems = refs[6 + chips :]
     width = state.shape[2]
+    rows = state.shape[1]
+    home = 8 * (NF + 1)
+    copies = [pltpu.make_async_copy(order_in, order, sems.at[0])]
+    copies += [pltpu.make_async_copy(state_in.at[field], state.at[field], sems.at[1 + field]) for field in range(NF)]
+    copies += [
+        pltpu.make_async_copy(owner_in, owner, sems.at[1 + NF]),
+        pltpu.make_async_copy(slot_in, slot, sems.at[2 + NF]),
+        pltpu.make_async_copy(sweep_in, chip_bufs[0].at[home : home + rows, :], sems.at[3 + NF]),
+    ]
+    for copy in copies:
+        copy.start()
     _, me = where_am_i()
     chip = me // 2
     sub = sublane(width)
     first = me == 0
-    chip_bufs, across = outs[:chips], outs[chips]
+    copies[0].wait()
 
     def tile_of(field, block):
         return state[field, pl.ds(pl.multiple_of(block // 2 * 8, 8), 8), :]
 
     def halo(index):
-        block = order[0, index]
+        block = order[index]
         odd = block % 2 * 4
         near = odd + jnp.where(first, 0, BR - 1)
         far = odd + jnp.where(first, 1, BR - 2)
@@ -54,33 +68,44 @@
         out = jnp.where(sub == FAR_P, turn(press, (FAR_P + 8 - far) % 8), out)
         return jnp.where(sub == FAR_U, turn(tiles[VELU], (FAR_U + 8 - far) % 8), out)
 
-    for mask in range(chips):
-        goal = chip ^ mask
-        low = order[0, 2 * goal]
-        high = order[0, 2 * goal + 1]
-        for field in range(NF):
+    for field in range(NF):
+        copies[1 + field].wait()
+        for mask in range(chips):
+            goal = chip ^ mask
+            low = order[2 * goal]
+            high = order[2 * goal + 1]
             even = turn(tile_of(field, low), low % 2 * 4)
             odd = turn(tile_of(field, high), 4 - high % 2 * 4)
             chip_bufs[mask][8 * field : 8 * field + 8, :] = jnp.where(sub < 4, even, odd)
+    for mask in range(chips):
+        goal = chip ^ mask
         beyond = jnp.where(first, jnp.minimum(2 * goal + 2, n - 1), jnp.maximum(2 * goal - 1, 0))
-        chip_bufs[mask][8 * NF :, :] = halo(beyond)
+        chip_bufs[mask][8 * NF : home, :] = halo(beyond)
     across[...] = halo(jnp.where(first, 0, n - 1))
+    for copy in copies[1 + NF :]:
+        copy.wait()
+    lane = lax.broadcasted_iota(jnp.int32, (1, width), 1)
+    for block in range(n):
+        line = jnp.where(lane == 0, owner[block], slot[block])
+        chip_bufs[0][home + rows + block : home + rows + block + 1, :] = line.astype(jnp.float32)
 
 
 def step_kernel(n, *refs):
     chips = n // 2
     refs = list(refs)
     take = lambda count: [refs.pop(0) for _ in range(count)]
-    owner, slot, owner_sib, slot_sib = take(4)
+    owner, slot = take(2)
     mine, theirs = take(chips), take(chips)
-    across, across_sib, sweep, sweep_sib = take(4)
+    across, across_sib, sweep = take(3)
     (vel,) = take(1)
     sends = take(chips)
-    fld, prs, vols, coef, halo, bins, tags, count = take(8)
+    fld, prs, vols, coef, halo, bins, tags, count, named, sem = take(10)
     grp, me = where_am_i()
     chip, core = me // 2, me % 2
     width = sweep.shape[1]
     rows = sweep.shape[0]
+    home = 8 * (NF + 1)
+    sweep_sib = theirs[0].at[home : home + rows, :]
     tiles = 2 * chips
     sub = sublane(width)
     lane = lax.broadcasted_iota(jnp.int32, (8, width), 1)
@@ -91,6 +116,9 @@
 
     def at(tile):
         return pl.ds(pl.multiple_of(tile * 8, 8), 8)
+
+    naming = pltpu.make_async_copy(theirs[0].at[home + rows : home + rows + n, 0:128], named, sem)
+    naming.start()
 
     for mask in range(chips):
         source = chip ^ mask
@@ -99,12 +127,14 @@
             even, odd = pair(mine[mask][span, :], theirs[mask][span, :])
             fld[field, at(1 + source), :] = jnp.where(sub < 4, even, turn(odd, 4))
             fld[field, at(1 + chips + source), :] = jnp.where(sub < 4, turn(even, 4), odd)
-        even, odd = pair(mine[mask][8 * NF :, :], theirs[mask][8 * NF :, :])
+        even, odd = pair(mine[mask][8 * NF : home, :], theirs[mask][8 * NF : home, :])
         halo[0, source] = even
         halo[1, source] = odd
     even, odd = pair(across[...], across_sib[...])
-    top = jnp.where(chip == 0, even, halo[1, chips - 1])
-    bottom = jnp.where(chip == chips - 1, odd, halo[0, 0])
+    inside_top = jnp.logical_or(grp > 0, chip > 0)
+    inside_bottom = jnp.logical_or(grp < lax.axis_size("grp") - 1, chip < chips - 1)
+    top = jnp.where(inside_top, jnp.where(chip == 0, even, halo[1, chips - 1]), 0.0)
+    bottom = jnp.where(inside_bottom, jnp.where(chip == chips - 1, odd, halo[0, 0]), 0.0)
 
     def line(tile, index):
         return jnp.broadcast_to(tile[index : index + 1, :], (8, width))
@@ -153,8 +183,6 @@
         return 0
 
     lax.fori_loop(0, tiles + 2, first, 0, unroll=n <= 8)
-    inside_top = jnp.logical_or(grp > 0, chip > 0)
-    inside_bottom = jnp.logical_or(grp < lax.axis_size("grp") - 1, chip < chips - 1)
     for place, inside in ((0, inside_top), (tiles + 1, inside_bottom)):
         span = at(place)
         prs[1, span, :] = jnp.where(inside, prs[1, span, :], 0.0)
@@ -170,6 +198,7 @@
 
     lax.fori_loop(0, chips, velocity, 0, unroll=n <= 8)
 
+    naming.wait()
     for mask in range(chips + 1):
         count[mask] = 0
         tags[mask] = jnp.full((8, 128), -1.0, jnp.float32)
@@ -184,7 +213,7 @@
         rank = count[mask]
         count[mask] = jnp.where(fits, rank + 1, 0)
         bins[mask, rank] = tile_out
-        tags[mask] = jnp.where(sub128 == rank, where_to.astype(jnp.float32), tags[mask])
+        tags[mask] = jnp.where(sub128 == rank, where_to, tags[mask])
 
     def second(device, index):
         tile = 1 + device * chips + index
@@ -205,8 +234,8 @@
             (1, jnp.where(sub < 4, turn(mass_part, 4), heat_part)),
         ):
             block = 2 * index + bit
-            who = jnp.where(from_own, owner[block, 0], owner_sib[block, 0])
-            where_to = jnp.where(from_own, slot[block], slot_sib[block])
+            who = jnp.where(from_own, owner[block], named[block, 0].astype(jnp.int32))
+            where_to = jnp.where(from_own, slot[block].astype(jnp.float32), named[block, 1])
             place(tile_out, who, where_to)
 
     for device in range(2):
@@ -247,6 +276,20 @@
     lax.fori_loop(0, chips, tile_pair, 0, unroll=n <= 8)
 
 
+def across_links(groups, n):
+    pairs = []
+    for grp in range(groups):
+        base = grp * n
+        pairs += [(base + i, base + i + 1) for i in range(2, n - 2, 2)]
+        if grp + 1 < groups:
+            turn_at = n - 2 if grp % 2 == 0 else 1
+            pairs += [(base + n - 1, base + n), (base + turn_at, base + n + turn_at)]
+    used = {i for pair in pairs for i in pair}
+    left = [i for i in range(groups * n) if i not in used]
+    pairs += [(left[i], left[i + 1]) for i in range(0, len(left), 2)]
+    return [link for low, high in pairs for link in ((low, high), (high, low))]
+
+
 def shards(state, order, sweep, owner, slot_target):
     n = lax.axis_size("bis")
     groups = lax.axis_size("grp")
@@ -262,22 +305,27 @@
     def to_chip(x, mask):
         return lax.ppermute(x, "bis", [(i, i ^ 2 * mask) for i in range(n)]) if mask else x
 
-    sweep_sib, owner_sib, slot_sib = to_sibling(sweep), to_sibling(owner), to_sibling(slot_target)
-
+    owner = owner.reshape(n)
+    extra = -(-(rows + n) // 8) * 8
     packed = pl.pallas_call(
         functools.partial(pack_kernel, n),
-        out_shape=[jax.ShapeDtypeStruct((8 * (NF + 1), width), f32)] * chips
+        out_shape=[
+            jax.ShapeDtypeStruct((8 * (NF + 1) + (0 if mask else extra), width), f32) for mask in range(chips)
+        ]
         + [jax.ShapeDtypeStruct((8, width), f32)],
-        in_specs=[SMEM, VMEM],
+        in_specs=[pl.BlockSpec(memory_space=pl.ANY)] * 5,
         out_specs=[VMEM] * (chips + 1),
+        scratch_shapes=[
+            pltpu.SMEM((n,), jnp.int32),
+            pltpu.SMEM((n,), jnp.int32),
+            pltpu.SMEM((n,), jnp.int32),
+            pltpu.VMEM((NF, rows, width), f32),
+            pltpu.SemaphoreType.DMA((NF + 4,)),
+        ],
         compiler_params=params,
         name="pack",
-    )(order, state)
-    links = []
-    for grp in range(groups - 1):
-        low, high = grp * n + n - 1, (grp + 1) * n
-        links += [(low, high), (high, low)]
-    across = lax.ppermute(packed[chips], ("grp", "bis"), links)
+    )(order.reshape(n), owner, slot_target, sweep, state)
+    across = lax.ppermute(packed[chips], ("grp", "bis"), across_links(groups, n))
     mine = [to_chip(packed[mask], mask) for mask in range(chips)]
     theirs = [to_sibling(x) for x in mine]
     across_sib = to_sibling(across)
@@ -288,7 +336,7 @@
         functools.partial(step_kernel, n),
         out_shape=[jax.ShapeDtypeStruct((2, rows, width), f32)]
         + [jax.ShapeDtypeStruct(send_shape, f32)] * chips,
-        in_specs=[SMEM] * 4 + [VMEM] * (2 * chips + 4),
+        in_specs=[SMEM] * 2 + [VMEM] * (2 * chips + 3),
         out_specs=[VMEM] * (chips + 1),
         scratch_shapes=[
             pltpu.VMEM((NF, stack, width), f32),
@@ -299,10 +347,12 @@
             pltpu.VMEM((chips + 1, 2 * CAP, 8, width), f32),
             pltpu.VMEM((chips + 1, 8, 128), f32),
             pltpu.SMEM((chips + 1,), jnp.int32),
+            pltpu.SMEM((n, 128), f32),
+            pltpu.SemaphoreType.DMA,
         ],
         compiler_params=params,
         name="substeps",
-    )(owner, slot_target, owner_sib, slot_sib, *mine, *theirs, across, across_sib, sweep, sweep_sib)
+    )(owner, slot_target, *mine, *theirs, across, across_sib, sweep)
     vel = out[0]
     arrived = [to_chip(out[1 + mask], mask) for mask in range(chips)]
     mass, energy = pl.pallas_call(

time: 29.5 us -> 30.9 us (1.047)
  starting transfers between devices: 12.8 us -> 10.8 us
  waiting for transfers between devices: 10.6 us -> 12.4 us
  Pallas kernels: 3.58 us -> 4.36 us
  local copies, waits for them, and re-layouts: 1.71 us -> 2.48 us
    ppermute x6, waiting for transfers between devices: 8.3 us -> 10.7 us  [to_chip(): lax.ppermute(x, 'bis', [(i, i ^ 2 * mask) for i in range(n)])]
    ppermute x8 -> x5, starting transfers between devices: 1.94 us -> 0.36 us  [to_sibling(): return lax.ppermute(x, 'bis', [(i, i ^ 1) for i in range(n)])]
    ppermute x8 -> x5, waiting for transfers between devices: 2.29 us -> 0.85 us  [to_sibling(): return lax.ppermute(x, 'bis', [(i, i ^ 1) for i in range(n)])]
    ppermute x1, waiting for transfers between devices: 0.01 us -> 0.84 us  [shards(): lax.ppermute(packed[chips], ('grp', 'bis'), across_links(groups, n))]
    unnamed x11 -> x12, local copies, waits for them, and re-layouts: 1.71 us -> 2.48 us
    pallas_call x1, Pallas kernels: 1.96 us -> 2.38 us  [shards(): pl.pallas_call(functools.partial(step_kernel, n), out_shape=[jax.ShapeDty...]
    pallas_call x1, Pallas kernels: 0.78 us -> 1.13 us  [shards(): pl.pallas_call(functools.partial(pack_kernel, n), out_shape=[jax.ShapeDty...]
  transfers between devices with their start and end apart: 15 -> 12, of which waited for: 7 -> 7; matrix products, arithmetic and copies ran while one was open for 0% -> 0% of each run, Pallas kernels for 0% -> 0%
where the time goes in v2:
time: 30.9 us; the launch traced here: 30.7 us
  waiting for transfers between devices  12.4 us (40%)
  starting transfers between devices  10.8 us (35%)
  Pallas kernels  4.36 us (14%)
  local copies, waits for them, and re-layouts  2.48 us (8%)
  between operations  0.71 us (2%)
    ppermute x6, waiting for transfers between devices, to_chip(): lax.ppermute(x, 'bis', [(i, i ^ 2 * mask) for i in range(n)])  10.7 us
    ppermute x6, starting transfers between devices, to_chip(): lax.ppermute(x, 'bis', [(i, i ^ 2 * mask) for i in range(n)])  9.91 us
    unnamed x12, local copies, waits for them, and re-layouts  2.48 us
    pallas_call x1, Pallas kernels, shards(): pl.pallas_call(functools.partial(step_kernel, n), out_shape=[jax.ShapeDty...  2.38 us
    pallas_call x1, Pallas kernels, shards(): pl.pallas_call(functools.partial(pack_kernel, n), out_shape=[jax.ShapeDty...  1.13 us
    ppermute x5, waiting for transfers between devices, to_sibling(): return lax.ppermute(x, 'bis', [(i, i ^ 1) for i in range(n)])  0.85 us
    pallas_call x1, Pallas kernels, shards(): pl.pallas_call(functools.partial(land_kernel, n), out_shape=[jax.ShapeDty...  0.85 us
    ppermute x1, waiting for transfers between devices, shards(): lax.ppermute(packed[chips], ('grp', 'bis'), across_links(groups, n))  0.84 us
  transfers between devices with their start and end apart: 12, of which 7 were waited for; matrix products, arithmetic and copies ran while one was open for 0% of the time, Pallas kernels for 0%

profile of v2, /device:TPU:0, one launch (start us, length us, event | category | flops | bytes accessed | tf_op | source)
XLA Modules:
  0.0 30.7 jit_solution(5792115698351710622)
XLA Ops:
  0.7 0.6 %copy-done.3 = s32[8,1]{0,1:T(1,128)S(1)} copy-done((s32[8,1]{0,1:T(1,128)S(1)}, s32[8,1]{0,1:T(1,128)}, u32[]{:S(2)}) %copy-start.3) | copy-done | bytes 56
  1.3 0.0 copy-done.4
  1.3 0.0 copy-done.5
  1.3 1.0 %copy-done = f32[5,32,512]{2,1,0:T(8,128)S(1)} copy-done((f32[5,32,512]{2,1,0:T(8,128)S(1)}, f32[5,32,512]{2,1,0:T(8,128)}, u32[]{:S(2)}) %copy-start) | copy-done | bytes 327704
  2.3 0.8 %copy-done.1 = f32[32,512]{1,0:T(8,128)S(1)} copy-done((f32[32,512]{1,0:T(8,128)S(1)}, f32[32,512]{1,0:T(8,128)}, u32[]{:S(2)}) %copy-start.1) | copy-done | bytes 65560
  3.1 1.1 %pack.1 = (f32[88,512]{1,0:T(8,128)S(1)}, f32[48,512]{1,0:T(8,128)S(1)}, f32[48,512]{1,0:T(8,128)S(1)}, f32[48,512]{1,0:T(8,128)S(1)}, f32[8,512]{1,0:T(8,128)S(1)}) custom-call(s32[8]{0:T(128)S(1)} %bitcast.4, s32[8]{0:T(128)S(1)} %bitcast.2, s32[8]{0:T(128)S(1)} %copy-done.4, f32[32,512]{1,0:T(8,128)S(1)} %copy-done.1, f32[5,32,512]{2,1,0:T(8,128)S(1)} %copy-done), custom_call_target="tpu_custom_call" | custom-call | tf_op jit(solution)/shard_map/pack/pallas_call | solution.py:310
  4.3 3.0 %collective-permute-start = (f32[48,512]{1,0:T(8,128)S(1)}, f32[48,512]{1,0:T(8,128)S(1)}, u32[]{:S(2)}, u32[]{:S(2)}) collective-permute-start(f32[48,512]{1,0:T(8,128)S(1)} %get-tuple-element.16), channel_id=1, source_target_pairs={{0,2},{1,3},{2,0},{3,1},{4,6},{5,7},{6,4},{7,5},{8,10},{9,11},{10,... | collective-permute-start | bytes 294920 | tf_op jit(solution)/shard_map/ppermute | solution.py:306
  7.3 1.5 %collective-permute-start.1 = (f32[48,512]{1,0:T(8,128)S(1)}, f32[48,512]{1,0:T(8,128)S(1)}, u32[]{:S(2)}, u32[]{:S(2)}) collective-permute-start(f32[48,512]{1,0:T(8,128)S(1)} %get-tuple-element.17), channel_id=1, source_target_pairs={{0,4},{1,5},{2,6},{3,7},{4,0},{5,1},{6,2},{7,3},{8,12},{9,13},{10,... | collective-permute-start | bytes 294920 | tf_op jit(solution)/shard_map/ppermute | solution.py:306
  8.8 0.0 collective-permute-start.2
  8.8 0.0 collective-permute-start.3
  8.8 1.5 %collective-permute-done.refs_3_ = f32[48,512]{1,0:T(8,128)S(1)} collective-permute-done((f32[48,512]{1,0:T(8,128)S(1)}, f32[48,512]{1,0:T(8,128)S(1)}, u32[]{:S(2)}, u32[]{:S(2)}) %collective-permute-start) | collective-permute-done | bytes 98336 | tf_op jit(solution)/shard_map/ppermute | solution.py:306
  10.3 0.0 collective-permute-start.4
  10.3 2.6 %collective-permute-done.1.refs_4_ = f32[48,512]{1,0:T(8,128)S(1)} collective-permute-done((f32[48,512]{1,0:T(8,128)S(1)}, f32[48,512]{1,0:T(8,128)S(1)}, u32[]{:S(2)}, u32[]{:S(2)}) %collective-permute-start.1) | collective-permute-done | bytes 98336 | tf_op jit(solution)/shard_map/ppermute | solution.py:306
  13.0 0.0 collective-permute-start.5
  13.0 1.4 %collective-permute-done.2.refs_5_ = f32[48,512]{1,0:T(8,128)S(1)} collective-permute-done((f32[48,512]{1,0:T(8,128)S(1)}, f32[48,512]{1,0:T(8,128)S(1)}, u32[]{:S(2)}, u32[]{:S(2)}) %collective-permute-start.2) | collective-permute-done | bytes 98336 | tf_op jit(solution)/shard_map/ppermute | solution.py:306
  14.3 0.0 collective-permute-start.6
  14.3 0.5 %collective-permute-start.7 = (f32[8,512]{1,0:T(8,128)S(1)}, f32[8,512]{1,0:T(8,128)S(1)}, u32[]{:S(2)}, u32[]{:S(2)}) collective-permute-start(f32[8,512]{1,0:T(8,128)S(1)} %get-tuple-element.19), channel_id=1, source_target_pairs={{2,3},{3,2},{4,5},{5,4},{7,8},{8,7},{6,14},{14,6},{10,11},{11,10},... | collective-permute-start | bytes 49160 | tf_op jit(solution)/shard_map/ppermute | solution.py:328
  14.8 0.8 %collective-permute-done.7.refs_10_ = f32[8,512]{1,0:T(8,128)S(1)} collective-permute-done((f32[8,512]{1,0:T(8,128)S(1)}, f32[8,512]{1,0:T(8,128)S(1)}, u32[]{:S(2)}, u32[]{:S(2)}) %collective-permute-start.7) | collective-permute-done | bytes 16416 | tf_op jit(solution)/shard_map/ppermute | solution.py:328
  15.7 0.3 %collective-permute-start.8 = (f32[8,512]{1,0:T(8,128)S(1)}, f32[8,512]{1,0:T(8,128)S(1)}, u32[]{:S(2)}, u32[]{:S(2)}) collective-permute-start(f32[8,512]{1,0:T(8,128)S(1)} %collective-permute-done.7.refs_10_), channel_id=1, source_target_pairs={{0,1},{1,0},{2,3},{3,2},{4,5},{5,4},{6,7},{7,6},{8,9},{9,8},{10,11... | collective-permute-start | bytes 49160 | tf_op jit(solution)/shard_map/ppermute | solution.py:303
  16.0 0.8 %collective-permute-done.8.refs_11_ = f32[8,512]{1,0:T(8,128)S(1)} collective-permute-done((f32[8,512]{1,0:T(8,128)S(1)}, f32[8,512]{1,0:T(8,128)S(1)}, u32[]{:S(2)}, u32[]{:S(2)}) %collective-permute-start.8) | collective-permute-done | bytes 16416 | tf_op jit(solution)/shard_map/ppermute | solution.py:303
  16.9 0.0 collective-permute-done.3.refs_6_
  16.9 0.0 collective-permute-done.4.refs_7_
  16.9 0.0 collective-permute-done.5.refs_8_
  16.9 0.0 collective-permute-done.6.refs_9_
  16.9 2.4 %substeps.1 = (f32[2,32,512]{2,1,0:T(8,128)}, f32[17,8,128]{2,1,0:T(8,128)S(1)}, f32[17,8,128]{2,1,0:T(8,128)S(1)}, f32[17,8,128]{2,1,0:T(8,128)S(1)}, f32[17,8,128]{2,1,0:T(8,128)S(1)}) custom-call(s32[8]{0:T(128)S(1)} %bitcast.3, s32[8]{0:T(128)S(1)} %copy-done.4, f32[88,512]{1,0:T(8,128)S(1)} %get-tuple-element.15.refs_2_, ...), custom_call_target="tpu_custom_call" | custom-call | tf_op jit(solution)/shard_map/substeps/pallas_call | solution.py:335
  19.3 0.7 %collective-permute-start.9 = (f32[17,8,128]{2,1,0:T(8,128)S(1)}, f32[17,8,128]{2,1,0:T(8,128)S(1)}, u32[]{:S(2)}, u32[]{:S(2)}) collective-permute-start(f32[17,8,128]{2,1,0:T(8,128)S(1)} %get-tuple-element.21), channel_id=1, source_target_pairs={{0,2},{1,3},{2,0},{3,1},{4,6},{5,7},{6,4},{7,5},{8,10},{9,11},{10,... | collective-permute-start | bytes 208904 | tf_op jit(solution)/shard_map/ppermute | solution.py:306
  20.0 4.7 %collective-permute-start.10 = (f32[17,8,128]{2,1,0:T(8,128)S(1)}, f32[17,8,128]{2,1,0:T(8,128)S(1)}, u32[]{:S(2)}, u32[]{:S(2)}) collective-permute-start(f32[17,8,128]{2,1,0:T(8,128)S(1)} %get-tuple-element.22), channel_id=1, source_target_pairs={{0,4},{1,5},{2,6},{3,7},{4,0},{5,1},{6,2},{7,3},{8,12},{9,13},{10,... | collective-permute-start | bytes 208904 | tf_op jit(solution)/shard_map/ppermute | solution.py:306
  24.6 0.0 collective-permute-start.11
  24.6 0.0 collective-permute-done.9.refs_1_
  24.6 3.3 %collective-permute-done.10.refs_2_ = f32[17,8,128]{2,1,0:T(8,128)S(1)} collective-permute-done((f32[17,8,128]{2,1,0:T(8,128)S(1)}, f32[17,8,128]{2,1,0:T(8,128)S(1)}, u32[]{:S(2)}, u32[]{:S(2)}) %collective-permute-start.10) | collective-permute-done | bytes 69664 | tf_op jit(solution)/shard_map/ppermute | solution.py:306
  28.0 1.9 %collective-permute-done.11.refs_3_ = f32[17,8,128]{2,1,0:T(8,128)S(1)} collective-permute-done((f32[17,8,128]{2,1,0:T(8,128)S(1)}, f32[17,8,128]{2,1,0:T(8,128)S(1)}, u32[]{:S(2)}, u32[]{:S(2)}) %collective-permute-start.11) | collective-permute-done | bytes 69664 | tf_op jit(solution)/shard_map/ppermute | solution.py:306
  29.8 0.8 %land.1 = (f32[32,512]{1,0:T(8,128)}, f32[32,512]{1,0:T(8,128)}) custom-call(f32[17,8,128]{2,1,0:T(8,128)S(1)} %get-tuple-element.20.refs_0_, f32[17,8,128]{2,1,0:T(8,128)S(1)} %collective-permute-done.9.refs_1_, f32[17,8,128]{2,1,0:T(8,128)S(1)} %collective-permute-done.10.refs_2_, f32[17,8,128]{2,1,0:T(8,128)S(1)} %collective-permute-done.11.refs_3_), custom_call_target="tpu_custom_call" | custom-call | tf_op jit(solution)/shard_map/land/pallas_call | solution.py:358
  (7 shorter events, 0.0 us)
Async XLA Ops:
  0.6 0.7 %copy-start.3 = (s32[8,1]{0,1:T(1,128)S(1)}, s32[8,1]{0,1:T(1,128)}, u32[]{:S(2)}) copy-start(s32[8,1]{0,1:T(1,128)} %param.8) | copy-start | bytes 100
  0.6 0.7 %copy-start.4 = (s32[8]{0:T(128)S(1)}, s32[8]{0:T(128)}, u32[]{:S(2)}) copy-start(s32[8]{0:T(128)} %refs_1_.1) | copy-start | bytes 100
  0.7 0.7 %copy-start.5 = (s32[1,8]{1,0:T(1,128)S(1)}, s32[1,8]{1,0:T(1,128)}, u32[]{:S(2)}) copy-start(s32[1,8]{1,0:T(1,128)} %param.6) | copy-start | bytes 100
  1.3 1.0 %copy-start = (f32[5,32,512]{2,1,0:T(8,128)S(1)}, f32[5,32,512]{2,1,0:T(8,128)}, u32[]{:S(2)}) copy-start(f32[5,32,512]{2,1,0:T(8,128)} %refs_4_.1) | copy-start | bytes 983044
  2.3 0.8 %copy-start.1 = (f32[32,512]{1,0:T(8,128)S(1)}, f32[32,512]{1,0:T(8,128)}, u32[]{:S(2)}) copy-start(f32[32,512]{1,0:T(8,128)} %refs_12_.1) | copy-start | bytes 196612
  3.1 13.7 %copy-start.2 = (f32[32,512]{1,0:T(8,128)S(1)}, f32[32,512]{1,0:T(8,128)}, u32[]{:S(2)}) copy-start(f32[32,512]{1,0:T(8,128)} %refs_12_.1) | copy-start | bytes 196612
  4.3 6.1 %collective-permute-start = (f32[48,512]{1,0:T(8,128)S(1)}, f32[48,512]{1,0:T(8,128)S(1)}, u32[]{:S(2)}, u32[]{:S(2)}) collective-permute-start(f32[48,512]{1,0:T(8,128)S(1)} %get-tuple-element.16), channel_id=1, source_target_pairs={{0,2},{1,3},{2,0},{3,1},{4,6},{5,7},{6,4},{7,5},{8,10},{9,11},{10,... | collective-permute-start | bytes 294920 | tf_op jit(solution)/shard_map/ppermute | solution.py:306
  7.3 5.7 %collective-permute-start.1 = (f32[48,512]{1,0:T(8,128)S(1)}, f32[48,512]{1,0:T(8,128)S(1)}, u32[]{:S(2)}, u32[]{:S(2)}) collective-permute-start(f32[48,512]{1,0:T(8,128)S(1)} %get-tuple-element.17), channel_id=1, source_target_pairs={{0,4},{1,5},{2,6},{3,7},{4,0},{5,1},{6,2},{7,3},{8,12},{9,13},{10,... | collective-permute-start | bytes 294920 | tf_op jit(solution)/shard_map/ppermute | solution.py:306
  8.8 5.5 %collective-permute-start.2 = (f32[48,512]{1,0:T(8,128)S(1)}, f32[48,512]{1,0:T(8,128)S(1)}, u32[]{:S(2)}, u32[]{:S(2)}) collective-permute-start(f32[48,512]{1,0:T(8,128)S(1)} %get-tuple-element.18), channel_id=1, source_target_pairs={{0,6},{1,7},{2,4},{3,5},{4,2},{5,3},{6,0},{7,1},{8,14},{9,15},{10,... | collective-permute-start | bytes 294920 | tf_op jit(solution)/shard_map/ppermute | solution.py:306
  8.8 8.0 %collective-permute-start.3 = (f32[88,512]{1,0:T(8,128)S(1)}, f32[88,512]{1,0:T(8,128)S(1)}, u32[]{:S(2)}, u32[]{:S(2)}) collective-permute-start(f32[88,512]{1,0:T(8,128)S(1)} %get-tuple-element.15.refs_2_), channel_id=1, source_target_pairs={{0,1},{1,0},{2,3},{3,2},{4,5},{5,4},{6,7},{7,6},{8,9},{9,8},{10,11... | collective-permute-start | bytes 540680 | tf_op jit(solution)/shard_map/ppermute | solution.py:303
  10.3 6.5 %collective-permute-start.4 = (f32[48,512]{1,0:T(8,128)S(1)}, f32[48,512]{1,0:T(8,128)S(1)}, u32[]{:S(2)}, u32[]{:S(2)}) collective-permute-start(f32[48,512]{1,0:T(8,128)S(1)} %collective-permute-done.refs_3_), channel_id=1, source_target_pairs={{0,1},{1,0},{2,3},{3,2},{4,5},{5,4},{6,7},{7,6},{8,9},{9,8},{10,11... | collective-permute-start | bytes 294920 | tf_op jit(solution)/shard_map/ppermute | solution.py:303
  13.0 3.9 %collective-permute-start.5 = (f32[48,512]{1,0:T(8,128)S(1)}, f32[48,512]{1,0:T(8,128)S(1)}, u32[]{:S(2)}, u32[]{:S(2)}) collective-permute-start(f32[48,512]{1,0:T(8,128)S(1)} %collective-permute-done.1.refs_4_), channel_id=1, source_target_pairs={{0,1},{1,0},{2,3},{3,2},{4,5},{5,4},{6,7},{7,6},{8,9},{9,8},{10,11... | collective-permute-start | bytes 294920 | tf_op jit(solution)/shard_map/ppermute | solution.py:303
  14.3 2.6 %collective-permute-start.6 = (f32[48,512]{1,0:T(8,128)S(1)}, f32[48,512]{1,0:T(8,128)S(1)}, u32[]{:S(2)}, u32[]{:S(2)}) collective-permute-start(f32[48,512]{1,0:T(8,128)S(1)} %collective-permute-done.2.refs_5_), channel_id=1, source_target_pairs={{0,1},{1,0},{2,3},{3,2},{4,5},{5,4},{6,7},{7,6},{8,9},{9,8},{10,11... | collective-permute-start | bytes 294920 | tf_op jit(solution)/shard_map/ppermute | solution.py:303
  14.3 1.3 %collective-permute-start.7 = (f32[8,512]{1,0:T(8,128)S(1)}, f32[8,512]{1,0:T(8,128)S(1)}, u32[]{:S(2)}, u32[]{:S(2)}) collective-permute-start(f32[8,512]{1,0:T(8,128)S(1)} %get-tuple-element.19), channel_id=1, source_target_pairs={{2,3},{3,2},{4,5},{5,4},{7,8},{8,7},{6,14},{14,6},{10,11},{11,10},... | collective-permute-start | bytes 49160 | tf_op jit(solution)/shard_map/ppermute | solution.py:328
  15.7 1.2 %collective-permute-start.8 = (f32[8,512]{1,0:T(8,128)S(1)}, f32[8,512]{1,0:T(8,128)S(1)}, u32[]{:S(2)}, u32[]{:S(2)}) collective-permute-start(f32[8,512]{1,0:T(8,128)S(1)} %collective-permute-done.7.refs_10_), channel_id=1, source_target_pairs={{0,1},{1,0},{2,3},{3,2},{4,5},{5,4},{6,7},{7,6},{8,9},{9,8},{10,11... | collective-permute-start | bytes 49160 | tf_op jit(solution)/shard_map/ppermute | solution.py:303
  19.3 5.4 %collective-permute-start.9 = (f32[17,8,128]{2,1,0:T(8,128)S(1)}, f32[17,8,128]{2,1,0:T(8,128)S(1)}, u32[]{:S(2)}, u32[]{:S(2)}) collective-permute-start(f32[17,8,128]{2,1,0:T(8,128)S(1)} %get-tuple-element.21), channel_id=1, source_target_pairs={{0,2},{1,3},{2,0},{3,1},{4,6},{5,7},{6,4},{7,5},{8,10},{9,11},{10,... | collective-permute-start | bytes 208904 | tf_op jit(solution)/shard_map/ppermute | solution.py:306
  20.0 8.0 %collective-permute-start.10 = (f32[17,8,128]{2,1,0:T(8,128)S(1)}, f32[17,8,128]{2,1,0:T(8,128)S(1)}, u32[]{:S(2)}, u32[]{:S(2)}) collective-permute-start(f32[17,8,128]{2,1,0:T(8,128)S(1)} %get-tuple-element.22), channel_id=1, source_target_pairs={{0,4},{1,5},{2,6},{3,7},{4,0},{5,1},{6,2},{7,3},{8,12},{9,13},{10,... | collective-permute-start | bytes 208904 | tf_op jit(solution)/shard_map/ppermute | solution.py:306
  24.6 5.2 %collective-permute-start.11 = (f32[17,8,128]{2,1,0:T(8,128)S(1)}, f32[17,8,128]{2,1,0:T(8,128)S(1)}, u32[]{:S(2)}, u32[]{:S(2)}) collective-permute-start(f32[17,8,128]{2,1,0:T(8,128)S(1)} %get-tuple-element.23), channel_id=1, source_target_pairs={{0,6},{1,7},{2,4},{3,5},{4,2},{5,3},{6,0},{7,1},{8,14},{9,15},{10,... | collective-permute-start | bytes 208904 | tf_op jit(solution)/shard_map/ppermute | solution.py:306

commit v3 on v2

--- a/solution.py
+++ b/solution.py
@@ -9,6 +9,7 @@
 
 BR = 4
 CAP = 2
+ZR = 48
 HALF_DT = 0.075
 NF = 5
 RHO, ENE, VELU, VELV, GAM = range(NF)
@@ -81,7 +82,7 @@
         goal = chip ^ mask
         beyond = jnp.where(first, jnp.minimum(2 * goal + 2, n - 1), jnp.maximum(2 * goal - 1, 0))
         chip_bufs[mask][8 * NF : home, :] = halo(beyond)
-    across[...] = halo(jnp.where(first, 0, n - 1))
+    across[0:8, :] = halo(jnp.where(first, 0, n - 1))
     for copy in copies[1 + NF :]:
         copy.wait()
     lane = lax.broadcasted_iota(jnp.int32, (1, width), 1)
@@ -99,7 +100,7 @@
     across, across_sib, sweep = take(3)
     (vel,) = take(1)
     sends = take(chips)
-    fld, prs, vols, coef, halo, bins, tags, count, named, sem = take(10)
+    fld, prs, vols, coef, halo, bins, tags, count, staged, named, sem = take(11)
     grp, me = where_am_i()
     chip, core = me // 2, me % 2
     width = sweep.shape[1]
@@ -117,7 +118,8 @@
     def at(tile):
         return pl.ds(pl.multiple_of(tile * 8, 8), 8)
 
-    naming = pltpu.make_async_copy(theirs[0].at[home + rows : home + rows + n, 0:128], named, sem)
+    staged[...] = theirs[0][home + rows : home + rows + n, 0:128].astype(jnp.int32)
+    naming = pltpu.make_async_copy(staged, named, sem)
     naming.start()
 
     for mask in range(chips):
@@ -130,7 +132,7 @@
         even, odd = pair(mine[mask][8 * NF : home, :], theirs[mask][8 * NF : home, :])
         halo[0, source] = even
         halo[1, source] = odd
-    even, odd = pair(across[...], across_sib[...])
+    even, odd = pair(across[0:8, :], across_sib[0:8, :])
     inside_top = jnp.logical_or(grp > 0, chip > 0)
     inside_bottom = jnp.logical_or(grp < lax.axis_size("grp") - 1, chip < chips - 1)
     top = jnp.where(inside_top, jnp.where(chip == 0, even, halo[1, chips - 1]), 0.0)
@@ -213,7 +215,7 @@
         rank = count[mask]
         count[mask] = jnp.where(fits, rank + 1, 0)
         bins[mask, rank] = tile_out
-        tags[mask] = jnp.where(sub128 == rank, where_to, tags[mask])
+        tags[mask] = jnp.where(sub128 == rank, jnp.full((8, 128), where_to).astype(jnp.float32), tags[mask])
 
     def second(device, index):
         tile = 1 + device * chips + index
@@ -234,8 +236,8 @@
             (1, jnp.where(sub < 4, turn(mass_part, 4), heat_part)),
         ):
             block = 2 * index + bit
-            who = jnp.where(from_own, owner[block], named[block, 0].astype(jnp.int32))
-            where_to = jnp.where(from_own, slot[block].astype(jnp.float32), named[block, 1])
+            who = jnp.where(from_own, owner[block], named[block, 0])
+            where_to = jnp.where(from_own, slot[block], named[block, 1])
             place(tile_out, who, where_to)
 
     for device in range(2):
@@ -312,7 +314,7 @@
         out_shape=[
             jax.ShapeDtypeStruct((8 * (NF + 1) + (0 if mask else extra), width), f32) for mask in range(chips)
         ]
-        + [jax.ShapeDtypeStruct((8, width), f32)],
+        + [jax.ShapeDtypeStruct((ZR, width), f32)],
         in_specs=[pl.BlockSpec(memory_space=pl.ANY)] * 5,
         out_specs=[VMEM] * (chips + 1),
         scratch_shapes=[
@@ -324,7 +326,7 @@
         ],
         compiler_params=params,
         name="pack",
-    )(order.reshape(n), owner, slot_target, sweep, state)
+    )(*[pltpu.with_memory_space_constraint(x, pltpu.HBM) for x in (order.reshape(n), owner, slot_target, sweep, state)])
     across = lax.ppermute(packed[chips], ("grp", "bis"), across_links(groups, n))
     mine = [to_chip(packed[mask], mask) for mask in range(chips)]
     theirs = [to_sibling(x) for x in mine]
@@ -347,7 +349,8 @@
             pltpu.VMEM((chips + 1, 2 * CAP, 8, width), f32),
             pltpu.VMEM((chips + 1, 8, 128), f32),
             pltpu.SMEM((chips + 1,), jnp.int32),
-            pltpu.SMEM((n, 128), f32),
+            pltpu.VMEM((n, 128), jnp.int32),
+            pltpu.SMEM((n, 128), jnp.int32),
             pltpu.SemaphoreType.DMA,
         ],
         compiler_params=params,

time: 30.9 us -> 24.7 us (0.80)
  local copies, waits for them, and re-layouts: 2.48 us -> 0.01 us
  waiting for transfers between devices: 12.4 us -> 10.1 us
  starting transfers between devices: 10.8 us -> 9.14 us
  Pallas kernels: 4.36 us -> 4.68 us
    unnamed x12 -> x6, local copies, waits for them, and re-layouts: 2.48 us -> 0.01 us
    ppermute x6, starting transfers between devices: 9.91 us -> 8.11 us  [to_chip(): lax.ppermute(x, 'bis', [(i, i ^ 2 * mask) for i in range(n)])]
    ppermute x6, waiting for transfers between devices: 10.7 us -> 9.12 us  [to_chip(): lax.ppermute(x, 'bis', [(i, i ^ 2 * mask) for i in range(n)])]
    ppermute x1, waiting for transfers between devices: 0.84 us -> 0.01 us  [shards(): lax.ppermute(packed[chips], ('grp', 'bis'), across_links(groups, n))]
    ppermute x5, starting transfers between devices: 0.36 us -> 1.02 us  [to_sibling(): return lax.ppermute(x, 'bis', [(i, i ^ 1) for i in range(n)])]
    ppermute x1, starting transfers between devices: 0.51 us -> 0.01 us  [shards(): lax.ppermute(packed[chips], ('grp', 'bis'), across_links(groups, n))]
  transfers between devices with their start and end apart: 12 -> 12, of which waited for: 7 -> 8; matrix products, arithmetic and copies ran while one was open for 0% -> 0% of each run, Pallas kernels for 0% -> 0%
where the time goes in v3:
time: 24.7 us; the launch traced here: 24.6 us
  waiting for transfers between devices  10.1 us (41%)
  starting transfers between devices  9.14 us (37%)
  Pallas kernels  4.68 us (19%)
  between operations  0.67 us (3%)
    ppermute x6, waiting for transfers between devices, to_chip(): lax.ppermute(x, 'bis', [(i, i ^ 2 * mask) for i in range(n)])  9.12 us
    ppermute x6, starting transfers between devices, to_chip(): lax.ppermute(x, 'bis', [(i, i ^ 2 * mask) for i in range(n)])  8.11 us
    pallas_call x1, Pallas kernels, shards(): pl.pallas_call(functools.partial(step_kernel, n), out_shape=[jax.ShapeDty...  2.4 us
    pallas_call x1, Pallas kernels, shards(): pl.pallas_call(functools.partial(pack_kernel, n), out_shape=[jax.ShapeDty...  1.44 us
    ppermute x5, starting transfers between devices, to_sibling(): return lax.ppermute(x, 'bis', [(i, i ^ 1) for i in range(n)])  1.02 us
    ppermute x5, waiting for transfers between devices, to_sibling(): return lax.ppermute(x, 'bis', [(i, i ^ 1) for i in range(n)])  0.94 us
    pallas_call x1, Pallas kernels, shards(): pl.pallas_call(functools.partial(land_kernel, n), out_shape=[jax.ShapeDty...  0.85 us
  transfers between devices with their start and end apart: 12, of which 8 were waited for; matrix products, arithmetic and copies ran while one was open for 0% of the time, Pallas kernels for 0%

profile of v3, /device:TPU:0, one launch (start us, length us, event | category | flops | bytes accessed | tf_op | source)
XLA Modules:
  0.0 24.6 jit_solution(17988986779689773365)
XLA Ops:
  0.6 0.0 copy-start
  0.6 1.4 %pack.1 = (f32[88,512]{1,0:T(8,128)S(1)}, f32[48,512]{1,0:T(8,128)S(1)}, f32[48,512]{1,0:T(8,128)S(1)}, f32[48,512]{1,0:T(8,128)S(1)}, f32[48,512]{1,0:T(8,128)S(1)}) custom-call(s32[8]{0:T(128)} %bitcast.4, s32[8]{0:T(128)} %bitcast.2, s32[8]{0:T(128)} %refs_1_.1, f32[32,512]{1,0:T(8,128)} %refs_12_.1, f32[5,32,512]{2,1,0:T(8,128)} %refs_4_.1), custom_call_target="tpu_custom_call" | custom-call | tf_op jit(solution)/shard_map/pack/pallas_call | solution.py:312
  2.1 3.0 %collective-permute-start = (f32[48,512]{1,0:T(8,128)S(1)}, f32[48,512]{1,0:T(8,128)S(1)}, u32[]{:S(2)}, u32[]{:S(2)}) collective-permute-start(f32[48,512]{1,0:T(8,128)S(1)} %get-tuple-element.16), channel_id=1, source_target_pairs={{0,2},{1,3},{2,0},{3,1},{4,6},{5,7},{6,4},{7,5},{8,10},{9,11},{10,... | collective-permute-start | bytes 294920 | tf_op jit(solution)/shard_map/ppermute | solution.py:308
  5.1 1.5 %collective-permute-start.1 = (f32[48,512]{1,0:T(8,128)S(1)}, f32[48,512]{1,0:T(8,128)S(1)}, u32[]{:S(2)}, u32[]{:S(2)}) collective-permute-start(f32[48,512]{1,0:T(8,128)S(1)} %get-tuple-element.17), channel_id=1, source_target_pairs={{0,4},{1,5},{2,6},{3,7},{4,0},{5,1},{6,2},{7,3},{8,12},{9,13},{10,... | collective-permute-start | bytes 294920 | tf_op jit(solution)/shard_map/ppermute | solution.py:308
  6.6 0.0 collective-permute-start.2
  6.6 0.0 copy-start.1
  6.6 0.0 collective-permute-start.7
  6.6 0.5 %collective-permute-start.3 = (f32[88,512]{1,0:T(8,128)S(1)}, f32[88,512]{1,0:T(8,128)S(1)}, u32[]{:S(2)}, u32[]{:S(2)}) collective-permute-start(f32[88,512]{1,0:T(8,128)S(1)} %get-tuple-element.15.refs_2_), channel_id=1, source_target_pairs={{0,1},{1,0},{2,3},{3,2},{4,5},{5,4},{6,7},{7,6},{8,9},{9,8},{10,11... | collective-permute-start | bytes 540680 | tf_op jit(solution)/shard_map/ppermute | solution.py:305
  7.1 1.0 %collective-permute-done.refs_3_ = f32[48,512]{1,0:T(8,128)S(1)} collective-permute-done((f32[48,512]{1,0:T(8,128)S(1)}, f32[48,512]{1,0:T(8,128)S(1)}, u32[]{:S(2)}, u32[]{:S(2)}) %collective-permute-start) | collective-permute-done | bytes 98336 | tf_op jit(solution)/shard_map/ppermute | solution.py:308
  8.1 0.0 collective-permute-start.4
  8.2 2.6 %collective-permute-done.1.refs_4_ = f32[48,512]{1,0:T(8,128)S(1)} collective-permute-done((f32[48,512]{1,0:T(8,128)S(1)}, f32[48,512]{1,0:T(8,128)S(1)}, u32[]{:S(2)}, u32[]{:S(2)}) %collective-permute-start.1) | collective-permute-done | bytes 98336 | tf_op jit(solution)/shard_map/ppermute | solution.py:308
  10.8 0.0 collective-permute-start.5
  10.8 1.4 %collective-permute-done.2.refs_5_ = f32[48,512]{1,0:T(8,128)S(1)} collective-permute-done((f32[48,512]{1,0:T(8,128)S(1)}, f32[48,512]{1,0:T(8,128)S(1)}, u32[]{:S(2)}, u32[]{:S(2)}) %collective-permute-start.2) | collective-permute-done | bytes 98336 | tf_op jit(solution)/shard_map/ppermute | solution.py:308
  12.1 0.0 collective-permute-start.6
  12.1 0.0 collective-permute-done.7.refs_10_
  12.1 0.5 %collective-permute-start.8 = (f32[48,512]{1,0:T(8,128)S(1)}, f32[48,512]{1,0:T(8,128)S(1)}, u32[]{:S(2)}, u32[]{:S(2)}) collective-permute-start(f32[48,512]{1,0:T(8,128)S(1)} %collective-permute-done.7.refs_10_), channel_id=1, source_target_pairs={{0,1},{1,0},{2,3},{3,2},{4,5},{5,4},{6,7},{7,6},{8,9},{9,8},{10,11... | collective-permute-start | bytes 294920 | tf_op jit(solution)/shard_map/ppermute | solution.py:305
  12.6 0.0 collective-permute-done.3.refs_6_
  12.6 0.0 collective-permute-done.4.refs_7_
  12.6 0.0 collective-permute-done.5.refs_8_
  12.7 0.8 %collective-permute-done.6.refs_9_ = f32[48,512]{1,0:T(8,128)S(1)} collective-permute-done((f32[48,512]{1,0:T(8,128)S(1)}, f32[48,512]{1,0:T(8,128)S(1)}, u32[]{:S(2)}, u32[]{:S(2)}) %collective-permute-start.6) | collective-permute-done | bytes 98336 | tf_op jit(solution)/shard_map/ppermute | solution.py:305
  13.4 0.2 collective-permute-done.8.refs_11_
  13.6 0.0 copy-done
  13.6 0.0 copy-done.1
  13.6 0.0 copy-done.2
  13.6 2.4 %substeps.1 = (f32[2,32,512]{2,1,0:T(8,128)}, f32[17,8,128]{2,1,0:T(8,128)S(1)}, f32[17,8,128]{2,1,0:T(8,128)S(1)}, f32[17,8,128]{2,1,0:T(8,128)S(1)}, f32[17,8,128]{2,1,0:T(8,128)S(1)}) custom-call(s32[8]{0:T(128)S(1)} %bitcast.3, s32[8]{0:T(128)S(1)} %copy-done.2, f32[88,512]{1,0:T(8,128)S(1)} %get-tuple-element.15.refs_2_, ...), custom_call_target="tpu_custom_call" | custom-call | tf_op jit(solution)/shard_map/substeps/pallas_call | solution.py:337
  16.0 0.7 %collective-permute-start.9 = (f32[17,8,128]{2,1,0:T(8,128)S(1)}, f32[17,8,128]{2,1,0:T(8,128)S(1)}, u32[]{:S(2)}, u32[]{:S(2)}) collective-permute-start(f32[17,8,128]{2,1,0:T(8,128)S(1)} %get-tuple-element.21), channel_id=1, source_target_pairs={{0,2},{1,3},{2,0},{3,1},{4,6},{5,7},{6,4},{7,5},{8,10},{9,11},{10,... | collective-permute-start | bytes 208904 | tf_op jit(solution)/shard_map/ppermute | solution.py:308
  16.7 1.8 %collective-permute-start.10 = (f32[17,8,128]{2,1,0:T(8,128)S(1)}, f32[17,8,128]{2,1,0:T(8,128)S(1)}, u32[]{:S(2)}, u32[]{:S(2)}) collective-permute-start(f32[17,8,128]{2,1,0:T(8,128)S(1)} %get-tuple-element.22), channel_id=1, source_target_pairs={{0,4},{1,5},{2,6},{3,7},{4,0},{5,1},{6,2},{7,3},{8,12},{9,13},{10,... | collective-permute-start | bytes 208904 | tf_op jit(solution)/shard_map/ppermute | solution.py:308
  18.5 1.1 %collective-permute-start.11 = (f32[17,8,128]{2,1,0:T(8,128)S(1)}, f32[17,8,128]{2,1,0:T(8,128)S(1)}, u32[]{:S(2)}, u32[]{:S(2)}) collective-permute-start(f32[17,8,128]{2,1,0:T(8,128)S(1)} %get-tuple-element.23), channel_id=1, source_target_pairs={{0,6},{1,7},{2,4},{3,5},{4,2},{5,3},{6,0},{7,1},{8,14},{9,15},{10,... | collective-permute-start | bytes 208904 | tf_op jit(solution)/shard_map/ppermute | solution.py:308
  19.6 0.9 %collective-permute-done.9.refs_1_ = f32[17,8,128]{2,1,0:T(8,128)S(1)} collective-permute-done((f32[17,8,128]{2,1,0:T(8,128)S(1)}, f32[17,8,128]{2,1,0:T(8,128)S(1)}, u32[]{:S(2)}, u32[]{:S(2)}) %collective-permute-start.9) | collective-permute-done | bytes 69664 | tf_op jit(solution)/shard_map/ppermute | solution.py:308
  20.5 1.3 %collective-permute-done.10.refs_2_ = f32[17,8,128]{2,1,0:T(8,128)S(1)} collective-permute-done((f32[17,8,128]{2,1,0:T(8,128)S(1)}, f32[17,8,128]{2,1,0:T(8,128)S(1)}, u32[]{:S(2)}, u32[]{:S(2)}) %collective-permute-start.10) | collective-permute-done | bytes 69664 | tf_op jit(solution)/shard_map/ppermute | solution.py:308
  21.8 1.9 %collective-permute-done.11.refs_3_ = f32[17,8,128]{2,1,0:T(8,128)S(1)} collective-permute-done((f32[17,8,128]{2,1,0:T(8,128)S(1)}, f32[17,8,128]{2,1,0:T(8,128)S(1)}, u32[]{:S(2)}, u32[]{:S(2)}) %collective-permute-start.11) | collective-permute-done | bytes 69664 | tf_op jit(solution)/shard_map/ppermute | solution.py:308
  23.7 0.8 %land.1 = (f32[32,512]{1,0:T(8,128)}, f32[32,512]{1,0:T(8,128)}) custom-call(f32[17,8,128]{2,1,0:T(8,128)S(1)} %get-tuple-element.20.refs_0_, f32[17,8,128]{2,1,0:T(8,128)S(1)} %collective-permute-done.9.refs_1_, f32[17,8,128]{2,1,0:T(8,128)S(1)} %collective-permute-done.10.refs_2_, f32[17,8,128]{2,1,0:T(8,128)S(1)} %collective-permute-done.11.refs_3_), custom_call_target="tpu_custom_call" | custom-call | tf_op jit(solution)/shard_map/land/pallas_call | solution.py:361
  (1 shorter events, 0.0 us)
Async XLA Ops:
  0.6 13.0 %copy-start = (f32[32,512]{1,0:T(8,128)S(1)}, f32[32,512]{1,0:T(8,128)}, u32[]{:S(2)}) copy-start(f32[32,512]{1,0:T(8,128)} %refs_12_.1) | copy-start | bytes 196612
  2.1 6.1 %collective-permute-start = (f32[48,512]{1,0:T(8,128)S(1)}, f32[48,512]{1,0:T(8,128)S(1)}, u32[]{:S(2)}, u32[]{:S(2)}) collective-permute-start(f32[48,512]{1,0:T(8,128)S(1)} %get-tuple-element.16), channel_id=1, source_target_pairs={{0,2},{1,3},{2,0},{3,1},{4,6},{5,7},{6,4},{7,5},{8,10},{9,11},{10,... | collective-permute-start | bytes 294920 | tf_op jit(solution)/shard_map/ppermute | solution.py:308
  5.1 5.7 %collective-permute-start.1 = (f32[48,512]{1,0:T(8,128)S(1)}, f32[48,512]{1,0:T(8,128)S(1)}, u32[]{:S(2)}, u32[]{:S(2)}) collective-permute-start(f32[48,512]{1,0:T(8,128)S(1)} %get-tuple-element.17), channel_id=1, source_target_pairs={{0,4},{1,5},{2,6},{3,7},{4,0},{5,1},{6,2},{7,3},{8,12},{9,13},{10,... | collective-permute-start | bytes 294920 | tf_op jit(solution)/shard_map/ppermute | solution.py:308
  6.6 5.5 %collective-permute-start.2 = (f32[48,512]{1,0:T(8,128)S(1)}, f32[48,512]{1,0:T(8,128)S(1)}, u32[]{:S(2)}, u32[]{:S(2)}) collective-permute-start(f32[48,512]{1,0:T(8,128)S(1)} %get-tuple-element.18), channel_id=1, source_target_pairs={{0,6},{1,7},{2,4},{3,5},{4,2},{5,3},{6,0},{7,1},{8,14},{9,15},{10,... | collective-permute-start | bytes 294920 | tf_op jit(solution)/shard_map/ppermute | solution.py:308
  6.6 7.0 %copy-start.1 = (s32[8,1]{0,1:T(1,128)S(1)}, s32[8,1]{0,1:T(1,128)}, u32[]{:S(2)}) copy-start(s32[8,1]{0,1:T(1,128)} %param.8) | copy-start | bytes 100
  6.6 7.0 %copy-start.2 = (s32[8]{0:T(128)S(1)}, s32[8]{0:T(128)}, u32[]{:S(2)}) copy-start(s32[8]{0:T(128)} %refs_1_.1) | copy-start | bytes 100
  6.6 5.5 %collective-permute-start.7 = (f32[48,512]{1,0:T(8,128)S(1)}, f32[48,512]{1,0:T(8,128)S(1)}, u32[]{:S(2)}, u32[]{:S(2)}) collective-permute-start(f32[48,512]{1,0:T(8,128)S(1)} %get-tuple-element.19), channel_id=1, source_target_pairs={{2,3},{3,2},{4,5},{5,4},{7,8},{8,7},{6,14},{14,6},{10,11},{11,10},... | collective-permute-start | bytes 294920 | tf_op jit(solution)/shard_map/ppermute | solution.py:330
  6.6 6.0 %collective-permute-start.3 = (f32[88,512]{1,0:T(8,128)S(1)}, f32[88,512]{1,0:T(8,128)S(1)}, u32[]{:S(2)}, u32[]{:S(2)}) collective-permute-start(f32[88,512]{1,0:T(8,128)S(1)} %get-tuple-element.15.refs_2_), channel_id=1, source_target_pairs={{0,1},{1,0},{2,3},{3,2},{4,5},{5,4},{6,7},{7,6},{8,9},{9,8},{10,11... | collective-permute-start | bytes 540680 | tf_op jit(solution)/shard_map/ppermute | solution.py:305
  8.1 4.5 %collective-permute-start.4 = (f32[48,512]{1,0:T(8,128)S(1)}, f32[48,512]{1,0:T(8,128)S(1)}, u32[]{:S(2)}, u32[]{:S(2)}) collective-permute-start(f32[48,512]{1,0:T(8,128)S(1)} %collective-permute-done.refs_3_), channel_id=1, source_target_pairs={{0,1},{1,0},{2,3},{3,2},{4,5},{5,4},{6,7},{7,6},{8,9},{9,8},{10,11... | collective-permute-start | bytes 294920 | tf_op jit(solution)/shard_map/ppermute | solution.py:305
  10.8 1.9 %collective-permute-start.5 = (f32[48,512]{1,0:T(8,128)S(1)}, f32[48,512]{1,0:T(8,128)S(1)}, u32[]{:S(2)}, u32[]{:S(2)}) collective-permute-start(f32[48,512]{1,0:T(8,128)S(1)} %collective-permute-done.1.refs_4_), channel_id=1, source_target_pairs={{0,1},{1,0},{2,3},{3,2},{4,5},{5,4},{6,7},{7,6},{8,9},{9,8},{10,11... | collective-permute-start | bytes 294920 | tf_op jit(solution)/shard_map/ppermute | solution.py:305
  12.1 1.3 %collective-permute-start.6 = (f32[48,512]{1,0:T(8,128)S(1)}, f32[48,512]{1,0:T(8,128)S(1)}, u32[]{:S(2)}, u32[]{:S(2)}) collective-permute-start(f32[48,512]{1,0:T(8,128)S(1)} %collective-permute-done.2.refs_5_), channel_id=1, source_target_pairs={{0,1},{1,0},{2,3},{3,2},{4,5},{5,4},{6,7},{7,6},{8,9},{9,8},{10,11... | collective-permute-start | bytes 294920 | tf_op jit(solution)/shard_map/ppermute | solution.py:305
  12.1 1.5 %collective-permute-start.8 = (f32[48,512]{1,0:T(8,128)S(1)}, f32[48,512]{1,0:T(8,128)S(1)}, u32[]{:S(2)}, u32[]{:S(2)}) collective-permute-start(f32[48,512]{1,0:T(8,128)S(1)} %collective-permute-done.7.refs_10_), channel_id=1, source_target_pairs={{0,1},{1,0},{2,3},{3,2},{4,5},{5,4},{6,7},{7,6},{8,9},{9,8},{10,11... | collective-permute-start | bytes 294920 | tf_op jit(solution)/shard_map/ppermute | solution.py:305
  16.0 4.5 %collective-permute-start.9 = (f32[17,8,128]{2,1,0:T(8,128)S(1)}, f32[17,8,128]{2,1,0:T(8,128)S(1)}, u32[]{:S(2)}, u32[]{:S(2)}) collective-permute-start(f32[17,8,128]{2,1,0:T(8,128)S(1)} %get-tuple-element.21), channel_id=1, source_target_pairs={{0,2},{1,3},{2,0},{3,1},{4,6},{5,7},{6,4},{7,5},{8,10},{9,11},{10,... | collective-permute-start | bytes 208904 | tf_op jit(solution)/shard_map/ppermute | solution.py:308
  16.7 5.1 %collective-permute-start.10 = (f32[17,8,128]{2,1,0:T(8,128)S(1)}, f32[17,8,128]{2,1,0:T(8,128)S(1)}, u32[]{:S(2)}, u32[]{:S(2)}) collective-permute-start(f32[17,8,128]{2,1,0:T(8,128)S(1)} %get-tuple-element.22), channel_id=1, source_target_pairs={{0,4},{1,5},{2,6},{3,7},{4,0},{5,1},{6,2},{7,3},{8,12},{9,13},{10,... | collective-permute-start | bytes 208904 | tf_op jit(solution)/shard_map/ppermute | solution.py:308
  18.5 5.2 %collective-permute-start.11 = (f32[17,8,128]{2,1,0:T(8,128)S(1)}, f32[17,8,128]{2,1,0:T(8,128)S(1)}, u32[]{:S(2)}, u32[]{:S(2)}) collective-permute-start(f32[17,8,128]{2,1,0:T(8,128)S(1)} %get-tuple-element.23), channel_id=1, source_target_pairs={{0,6},{1,7},{2,4},{3,5},{4,2},{5,3},{6,0},{7,1},{8,14},{9,15},{10,... | collective-permute-start | bytes 208904 | tf_op jit(solution)/shard_map/ppermute | solution.py:308

commit v4 on v3

--- a/solution.py
+++ b/solution.py
@@ -28,6 +28,18 @@
 
 def where_am_i():
     return lax.axis_index("grp"), lax.axis_index("bis")
+
+
+def routes(chips):
+    bits = chips.bit_length() - 1
+    half = bits // 2 if bits % 2 == 0 else 0
+    swap = lambda mask: (mask << half | mask >> bits - half) & chips - 1
+    masks = sorted(range(1, chips), key=lambda mask: (-mask.bit_count(), mask))
+    return [(0, 0)] + [(mask, swap(mask)) for mask in masks]
+
+
+def reached(route, core):
+    return route[0] if route[0] == route[1] else jnp.where(core == 0, route[0], route[1])
 
 
 def pack_kernel(n, *refs):
@@ -48,9 +60,10 @@
     for copy in copies:
         copy.start()
     _, me = where_am_i()
-    chip = me // 2
+    chip, core = me // 2, me % 2
     sub = sublane(width)
     first = me == 0
+    goals = [chip ^ reached(route, core) for route in routes(chips)]
     copies[0].wait()
 
     def tile_of(field, block):
@@ -71,17 +84,15 @@
 
     for field in range(NF):
         copies[1 + field].wait()
-        for mask in range(chips):
-            goal = chip ^ mask
+        for buf, goal in zip(chip_bufs, goals):
             low = order[2 * goal]
             high = order[2 * goal + 1]
             even = turn(tile_of(field, low), low % 2 * 4)
             odd = turn(tile_of(field, high), 4 - high % 2 * 4)
-            chip_bufs[mask][8 * field : 8 * field + 8, :] = jnp.where(sub < 4, even, odd)
-    for mask in range(chips):
-        goal = chip ^ mask
+            buf[8 * field : 8 * field + 8, :] = jnp.where(sub < 4, even, odd)
+    for buf, goal in zip(chip_bufs, goals):
         beyond = jnp.where(first, jnp.minimum(2 * goal + 2, n - 1), jnp.maximum(2 * goal - 1, 0))
-        chip_bufs[mask][8 * NF : home, :] = halo(beyond)
+        buf[8 * NF : home, :] = halo(beyond)
     across[0:8, :] = halo(jnp.where(first, 0, n - 1))
     for copy in copies[1 + NF :]:
         copy.wait()
@@ -122,14 +133,16 @@
     naming = pltpu.make_async_copy(staged, named, sem)
     naming.start()
 
-    for mask in range(chips):
-        source = chip ^ mask
+    paths = routes(chips)
+    for index, path in enumerate(paths):
+        source = chip ^ reached(path, core)
+        own, sib = mine[index], theirs[paths.index((path[1], path[0]))]
         for field in range(NF):
             span = pl.ds(8 * field, 8)
-            even, odd = pair(mine[mask][span, :], theirs[mask][span, :])
+            even, odd = pair(own[span, :], sib[span, :])
             fld[field, at(1 + source), :] = jnp.where(sub < 4, even, turn(odd, 4))
             fld[field, at(1 + chips + source), :] = jnp.where(sub < 4, turn(even, 4), odd)
-        even, odd = pair(mine[mask][8 * NF : home, :], theirs[mask][8 * NF : home, :])
+        even, odd = pair(own[8 * NF : home, :], sib[8 * NF : home, :])
         halo[0, source] = even
         halo[1, source] = odd
     even, odd = pair(across[0:8, :], across_sib[0:8, :])
@@ -243,11 +256,12 @@
     for device in range(2):
         lax.fori_loop(0, chips, lambda index, _, device=device: (second(device, index), 0)[1], 0, unroll=n <= 8)
 
-    for mask in range(chips):
+    for send, path in zip(sends, paths):
+        mask = reached(path, core)
         for rank in range(2 * CAP):
             for part in range(width // 128):
-                sends[mask][rank * (width // 128) + part] = bins[mask, rank, :, part * 128 : part * 128 + 128]
-        sends[mask][2 * CAP * (width // 128)] = tags[mask]
+                send[rank * (width // 128) + part] = bins[mask, rank, :, part * 128 : part * 128 + 128]
+        send[2 * CAP * (width // 128)] = tags[mask]
 
 
 def land_kernel(n, *refs):
@@ -304,8 +318,10 @@
     def to_sibling(x):
         return lax.ppermute(x, "bis", [(i, i ^ 1) for i in range(n)])
 
-    def to_chip(x, mask):
-        return lax.ppermute(x, "bis", [(i, i ^ 2 * mask) for i in range(n)]) if mask else x
+    def to_chip(x, path):
+        return lax.ppermute(x, "bis", [(i, i ^ 2 * path[i % 2]) for i in range(n)]) if path[0] else x
+
+    paths = routes(chips)
 
     owner = owner.reshape(n)
     extra = -(-(rows + n) // 8) * 8
@@ -328,7 +344,7 @@
         name="pack",
     )(*[pltpu.with_memory_space_constraint(x, pltpu.HBM) for x in (order.reshape(n), owner, slot_target, sweep, state)])
     across = lax.ppermute(packed[chips], ("grp", "bis"), across_links(groups, n))
-    mine = [to_chip(packed[mask], mask) for mask in range(chips)]
+    mine = [to_chip(x, path) for x, path in zip(packed, paths)]
     theirs = [to_sibling(x) for x in mine]
     across_sib = to_sibling(across)
 
@@ -357,7 +373,7 @@
         name="substeps",
     )(owner, slot_target, *mine, *theirs, across, across_sib, sweep)
     vel = out[0]
-    arrived = [to_chip(out[1 + mask], mask) for mask in range(chips)]
+    arrived = [to_chip(x, path) for x, path in zip(out[1:], paths)]
     mass, energy = pl.pallas_call(
         functools.partial(land_kernel, n),
         out_shape=[jax.ShapeDtypeStruct((rows, width), f32)] * 2,

time: 24.7 us -> 23.8 us (0.964)
  waiting for transfers between devices: 10.1 us -> 8.52 us
  starting transfers between devices: 9.14 us -> 9.73 us
    ppermute x6, waiting for transfers between devices: 9.12 us -> 7.29 us  [to_chip(): lax.ppermute(x, 'bis', [(i, i ^ 2 * path[i % 2]) for i in range(n)])]
    ppermute x6, starting transfers between devices: 8.11 us -> 8.64 us  [to_chip(): lax.ppermute(x, 'bis', [(i, i ^ 2 * path[i % 2]) for i in range(n)])]
    ppermute x5, waiting for transfers between devices: 0.94 us -> 1.23 us  [to_sibling(): return lax.ppermute(x, 'bis', [(i, i ^ 1) for i in range(n)])]
  transfers between devices with their start and end apart: 12 -> 12, of which waited for: 8 -> 7; matrix products, arithmetic and copies ran while one was open for 0% -> 0% of each run, Pallas kernels for 0% -> 0%
where the time goes in v4:
time: 23.8 us; the launch traced here: 23.6 us
  starting transfers between devices  9.73 us (41%)
  waiting for transfers between devices  8.52 us (36%)
  Pallas kernels  4.69 us (20%)
  between operations  0.67 us (3%)
    ppermute x6, starting transfers between devices, to_chip(): lax.ppermute(x, 'bis', [(i, i ^ 2 * path[i % 2]) for i in range(n)])  8.64 us
    ppermute x6, waiting for transfers between devices, to_chip(): lax.ppermute(x, 'bis', [(i, i ^ 2 * path[i % 2]) for i in range(n)])  7.29 us
    pallas_call x1, Pallas kernels, shards(): pl.pallas_call(functools.partial(step_kernel, n), out_shape=[jax.ShapeDty...  2.4 us
    pallas_call x1, Pallas kernels, shards(): pl.pallas_call(functools.partial(pack_kernel, n), out_shape=[jax.ShapeDty...  1.44 us
    ppermute x5, waiting for transfers between devices, to_sibling(): return lax.ppermute(x, 'bis', [(i, i ^ 1) for i in range(n)])  1.23 us
    ppermute x5, starting transfers between devices, to_sibling(): return lax.ppermute(x, 'bis', [(i, i ^ 1) for i in range(n)])  1.09 us
    pallas_call x1, Pallas kernels, shards(): pl.pallas_call(functools.partial(land_kernel, n), out_shape=[jax.ShapeDty...  0.85 us
  transfers between devices with their start and end apart: 12, of which 7 were waited for; matrix products, arithmetic and copies ran while one was open for 0% of the time, Pallas kernels for 0%

profile of v4, /device:TPU:0, one launch (start us, length us, event | category | flops | bytes accessed | tf_op | source)
XLA Modules:
  0.0 23.6 jit_solution(2989722998600587125)
XLA Ops:
  0.6 0.0 copy-start
  0.6 1.4 %pack.1 = (f32[88,512]{1,0:T(8,128)S(1)}, f32[48,512]{1,0:T(8,128)S(1)}, f32[48,512]{1,0:T(8,128)S(1)}, f32[48,512]{1,0:T(8,128)S(1)}, f32[48,512]{1,0:T(8,128)S(1)}) custom-call(s32[8]{0:T(128)} %bitcast.4, s32[8]{0:T(128)} %bitcast.2, s32[8]{0:T(128)} %refs_1_.1, f32[32,512]{1,0:T(8,128)} %refs_12_.1, f32[5,32,512]{2,1,0:T(8,128)} %refs_4_.1), custom_call_target="tpu_custom_call" | custom-call | tf_op jit(solution)/shard_map/pack/pallas_call | solution.py:328
  2.1 4.0 %collective-permute-start = (f32[48,512]{1,0:T(8,128)S(1)}, f32[48,512]{1,0:T(8,128)S(1)}, u32[]{:S(2)}, u32[]{:S(2)}) collective-permute-start(f32[48,512]{1,0:T(8,128)S(1)} %get-tuple-element.16), channel_id=1, source_target_pairs={{0,6},{1,7},{2,4},{3,5},{4,2},{5,3},{6,0},{7,1},{8,14},{9,15},{10,... | collective-permute-start | bytes 294920 | tf_op jit(solution)/shard_map/ppermute | solution.py:322
  6.0 0.5 %collective-permute-start.1 = (f32[48,512]{1,0:T(8,128)S(1)}, f32[48,512]{1,0:T(8,128)S(1)}, u32[]{:S(2)}, u32[]{:S(2)}) collective-permute-start(f32[48,512]{1,0:T(8,128)S(1)} %get-tuple-element.17), channel_id=1, source_target_pairs={{0,2},{1,5},{2,0},{3,7},{4,6},{5,1},{6,4},{7,3},{8,10},{9,13},{10,... | collective-permute-start | bytes 294920 | tf_op jit(solution)/shard_map/ppermute | solution.py:322
  6.6 0.1 collective-permute-start.2
  6.7 0.0 copy-start.1
  6.7 0.0 collective-permute-start.7
  6.7 0.5 %collective-permute-start.3 = (f32[88,512]{1,0:T(8,128)S(1)}, f32[88,512]{1,0:T(8,128)S(1)}, u32[]{:S(2)}, u32[]{:S(2)}) collective-permute-start(f32[88,512]{1,0:T(8,128)S(1)} %get-tuple-element.15.refs_2_), channel_id=1, source_target_pairs={{0,1},{1,0},{2,3},{3,2},{4,5},{5,4},{6,7},{7,6},{8,9},{9,8},{10,11... | collective-permute-start | bytes 540680 | tf_op jit(solution)/shard_map/ppermute | solution.py:319
  7.2 2.0 %collective-permute-done.refs_3_ = f32[48,512]{1,0:T(8,128)S(1)} collective-permute-done((f32[48,512]{1,0:T(8,128)S(1)}, f32[48,512]{1,0:T(8,128)S(1)}, u32[]{:S(2)}, u32[]{:S(2)}) %collective-permute-start) | collective-permute-done | bytes 98336 | tf_op jit(solution)/shard_map/ppermute | solution.py:322
  9.2 0.0 collective-permute-start.4
  9.2 2.0 %collective-permute-done.1.refs_4_ = f32[48,512]{1,0:T(8,128)S(1)} collective-permute-done((f32[48,512]{1,0:T(8,128)S(1)}, f32[48,512]{1,0:T(8,128)S(1)}, u32[]{:S(2)}, u32[]{:S(2)}) %collective-permute-start.1) | collective-permute-done | bytes 98336 | tf_op jit(solution)/shard_map/ppermute | solution.py:322
  11.3 0.0 collective-permute-start.5
  11.3 0.0 collective-permute-done.2.refs_5_
  11.3 0.5 %collective-permute-start.6 = (f32[48,512]{1,0:T(8,128)S(1)}, f32[48,512]{1,0:T(8,128)S(1)}, u32[]{:S(2)}, u32[]{:S(2)}) collective-permute-start(f32[48,512]{1,0:T(8,128)S(1)} %collective-permute-done.2.refs_5_), channel_id=1, source_target_pairs={{0,1},{1,0},{2,3},{3,2},{4,5},{5,4},{6,7},{7,6},{8,9},{9,8},{10,11... | collective-permute-start | bytes 294920 | tf_op jit(solution)/shard_map/ppermute | solution.py:319
  11.8 0.0 collective-permute-done.7.refs_10_
  11.8 0.1 collective-permute-start.8
  11.9 0.0 collective-permute-done.3.refs_6_
  11.9 0.0 collective-permute-done.4.refs_7_
  11.9 0.7 %collective-permute-done.5.refs_8_ = f32[48,512]{1,0:T(8,128)S(1)} collective-permute-done((f32[48,512]{1,0:T(8,128)S(1)}, f32[48,512]{1,0:T(8,128)S(1)}, u32[]{:S(2)}, u32[]{:S(2)}) %collective-permute-start.5) | collective-permute-done | bytes 98336 | tf_op jit(solution)/shard_map/ppermute | solution.py:319
  12.6 0.2 collective-permute-done.6.refs_9_
  12.7 0.4 %collective-permute-done.8.refs_11_ = f32[48,512]{1,0:T(8,128)S(1)} collective-permute-done((f32[48,512]{1,0:T(8,128)S(1)}, f32[48,512]{1,0:T(8,128)S(1)}, u32[]{:S(2)}, u32[]{:S(2)}) %collective-permute-start.8) | collective-permute-done | bytes 98336 | tf_op jit(solution)/shard_map/ppermute | solution.py:319
  13.1 0.0 copy-done
  13.1 0.0 copy-done.1
  13.1 0.0 copy-done.2
  13.1 2.4 %substeps.1 = (f32[2,32,512]{2,1,0:T(8,128)}, f32[17,8,128]{2,1,0:T(8,128)S(1)}, f32[17,8,128]{2,1,0:T(8,128)S(1)}, f32[17,8,128]{2,1,0:T(8,128)S(1)}, f32[17,8,128]{2,1,0:T(8,128)S(1)}) custom-call(s32[8]{0:T(128)S(1)} %bitcast.3, s32[8]{0:T(128)S(1)} %copy-done.2, f32[88,512]{1,0:T(8,128)S(1)} %get-tuple-element.15.refs_2_, ...), custom_call_target="tpu_custom_call" | custom-call | tf_op jit(solution)/shard_map/substeps/pallas_call | solution.py:353
  15.5 2.4 %collective-permute-start.9 = (f32[17,8,128]{2,1,0:T(8,128)S(1)}, f32[17,8,128]{2,1,0:T(8,128)S(1)}, u32[]{:S(2)}, u32[]{:S(2)}) collective-permute-start(f32[17,8,128]{2,1,0:T(8,128)S(1)} %get-tuple-element.21), channel_id=1, source_target_pairs={{0,6},{1,7},{2,4},{3,5},{4,2},{5,3},{6,0},{7,1},{8,14},{9,15},{10,... | collective-permute-start | bytes 208904 | tf_op jit(solution)/shard_map/ppermute | solution.py:322
  17.9 0.2 collective-permute-start.10
  18.2 1.4 %collective-permute-start.11 = (f32[17,8,128]{2,1,0:T(8,128)S(1)}, f32[17,8,128]{2,1,0:T(8,128)S(1)}, u32[]{:S(2)}, u32[]{:S(2)}) collective-permute-start(f32[17,8,128]{2,1,0:T(8,128)S(1)} %get-tuple-element.23), channel_id=1, source_target_pairs={{0,4},{1,3},{2,6},{3,1},{4,0},{5,7},{6,2},{7,5},{8,12},{9,11},{10,... | collective-permute-start | bytes 208904 | tf_op jit(solution)/shard_map/ppermute | solution.py:322
  19.6 1.3 %collective-permute-done.9.refs_1_ = f32[17,8,128]{2,1,0:T(8,128)S(1)} collective-permute-done((f32[17,8,128]{2,1,0:T(8,128)S(1)}, f32[17,8,128]{2,1,0:T(8,128)S(1)}, u32[]{:S(2)}, u32[]{:S(2)}) %collective-permute-start.9) | collective-permute-done | bytes 69664 | tf_op jit(solution)/shard_map/ppermute | solution.py:322
  20.8 2.0 %collective-permute-done.10.refs_2_ = f32[17,8,128]{2,1,0:T(8,128)S(1)} collective-permute-done((f32[17,8,128]{2,1,0:T(8,128)S(1)}, f32[17,8,128]{2,1,0:T(8,128)S(1)}, u32[]{:S(2)}, u32[]{:S(2)}) %collective-permute-start.10) | collective-permute-done | bytes 69664 | tf_op jit(solution)/shard_map/ppermute | solution.py:322
  22.8 0.0 collective-permute-done.11.refs_3_
  22.8 0.8 %land.1 = (f32[32,512]{1,0:T(8,128)}, f32[32,512]{1,0:T(8,128)}) custom-call(f32[17,8,128]{2,1,0:T(8,128)S(1)} %get-tuple-element.20.refs_0_, f32[17,8,128]{2,1,0:T(8,128)S(1)} %collective-permute-done.9.refs_1_, f32[17,8,128]{2,1,0:T(8,128)S(1)} %collective-permute-done.10.refs_2_, f32[17,8,128]{2,1,0:T(8,128)S(1)} %collective-permute-done.11.refs_3_), custom_call_target="tpu_custom_call" | custom-call | tf_op jit(solution)/shard_map/land/pallas_call | solution.py:377
  (1 shorter events, 0.0 us)
Async XLA Ops:
  0.6 12.5 %copy-start = (f32[32,512]{1,0:T(8,128)S(1)}, f32[32,512]{1,0:T(8,128)}, u32[]{:S(2)}) copy-start(f32[32,512]{1,0:T(8,128)} %refs_12_.1) | copy-start | bytes 196612
  2.1 7.1 %collective-permute-start = (f32[48,512]{1,0:T(8,128)S(1)}, f32[48,512]{1,0:T(8,128)S(1)}, u32[]{:S(2)}, u32[]{:S(2)}) collective-permute-start(f32[48,512]{1,0:T(8,128)S(1)} %get-tuple-element.16), channel_id=1, source_target_pairs={{0,6},{1,7},{2,4},{3,5},{4,2},{5,3},{6,0},{7,1},{8,14},{9,15},{10,... | collective-permute-start | bytes 294920 | tf_op jit(solution)/shard_map/ppermute | solution.py:322
  6.0 5.2 %collective-permute-start.1 = (f32[48,512]{1,0:T(8,128)S(1)}, f32[48,512]{1,0:T(8,128)S(1)}, u32[]{:S(2)}, u32[]{:S(2)}) collective-permute-start(f32[48,512]{1,0:T(8,128)S(1)} %get-tuple-element.17), channel_id=1, source_target_pairs={{0,2},{1,5},{2,0},{3,7},{4,6},{5,1},{6,4},{7,3},{8,10},{9,13},{10,... | collective-permute-start | bytes 294920 | tf_op jit(solution)/shard_map/ppermute | solution.py:322
  6.6 4.7 %collective-permute-start.2 = (f32[48,512]{1,0:T(8,128)S(1)}, f32[48,512]{1,0:T(8,128)S(1)}, u32[]{:S(2)}, u32[]{:S(2)}) collective-permute-start(f32[48,512]{1,0:T(8,128)S(1)} %get-tuple-element.18), channel_id=1, source_target_pairs={{0,4},{1,3},{2,6},{3,1},{4,0},{5,7},{6,2},{7,5},{8,12},{9,11},{10,... | collective-permute-start | bytes 294920 | tf_op jit(solution)/shard_map/ppermute | solution.py:322
  6.7 6.4 %copy-start.1 = (s32[8,1]{0,1:T(1,128)S(1)}, s32[8,1]{0,1:T(1,128)}, u32[]{:S(2)}) copy-start(s32[8,1]{0,1:T(1,128)} %param.8) | copy-start | bytes 100
  6.7 6.4 %copy-start.2 = (s32[8]{0:T(128)S(1)}, s32[8]{0:T(128)}, u32[]{:S(2)}) copy-start(s32[8]{0:T(128)} %refs_1_.1) | copy-start | bytes 100
  6.7 5.1 %collective-permute-start.7 = (f32[48,512]{1,0:T(8,128)S(1)}, f32[48,512]{1,0:T(8,128)S(1)}, u32[]{:S(2)}, u32[]{:S(2)}) collective-permute-start(f32[48,512]{1,0:T(8,128)S(1)} %get-tuple-element.19), channel_id=1, source_target_pairs={{2,3},{3,2},{4,5},{5,4},{7,8},{8,7},{6,14},{14,6},{10,11},{11,10},... | collective-permute-start | bytes 294920 | tf_op jit(solution)/shard_map/ppermute | solution.py:346
  6.7 5.2 %collective-permute-start.3 = (f32[88,512]{1,0:T(8,128)S(1)}, f32[88,512]{1,0:T(8,128)S(1)}, u32[]{:S(2)}, u32[]{:S(2)}) collective-permute-start(f32[88,512]{1,0:T(8,128)S(1)} %get-tuple-element.15.refs_2_), channel_id=1, source_target_pairs={{0,1},{1,0},{2,3},{3,2},{4,5},{5,4},{6,7},{7,6},{8,9},{9,8},{10,11... | collective-permute-start | bytes 540680 | tf_op jit(solution)/shard_map/ppermute | solution.py:319
  9.2 2.6 %collective-permute-start.4 = (f32[48,512]{1,0:T(8,128)S(1)}, f32[48,512]{1,0:T(8,128)S(1)}, u32[]{:S(2)}, u32[]{:S(2)}) collective-permute-start(f32[48,512]{1,0:T(8,128)S(1)} %collective-permute-done.refs_3_), channel_id=1, source_target_pairs={{0,1},{1,0},{2,3},{3,2},{4,5},{5,4},{6,7},{7,6},{8,9},{9,8},{10,11... | collective-permute-start | bytes 294920 | tf_op jit(solution)/shard_map/ppermute | solution.py:319
  11.3 1.3 %collective-permute-start.5 = (f32[48,512]{1,0:T(8,128)S(1)}, f32[48,512]{1,0:T(8,128)S(1)}, u32[]{:S(2)}, u32[]{:S(2)}) collective-permute-start(f32[48,512]{1,0:T(8,128)S(1)} %collective-permute-done.1.refs_4_), channel_id=1, source_target_pairs={{0,1},{1,0},{2,3},{3,2},{4,5},{5,4},{6,7},{7,6},{8,9},{9,8},{10,11... | collective-permute-start | bytes 294920 | tf_op jit(solution)/shard_map/ppermute | solution.py:319
  11.3 1.5 %collective-permute-start.6 = (f32[48,512]{1,0:T(8,128)S(1)}, f32[48,512]{1,0:T(8,128)S(1)}, u32[]{:S(2)}, u32[]{:S(2)}) collective-permute-start(f32[48,512]{1,0:T(8,128)S(1)} %collective-permute-done.2.refs_5_), channel_id=1, source_target_pairs={{0,1},{1,0},{2,3},{3,2},{4,5},{5,4},{6,7},{7,6},{8,9},{9,8},{10,11... | collective-permute-start | bytes 294920 | tf_op jit(solution)/shard_map/ppermute | solution.py:319
  11.8 1.3 %collective-permute-start.8 = (f32[48,512]{1,0:T(8,128)S(1)}, f32[48,512]{1,0:T(8,128)S(1)}, u32[]{:S(2)}, u32[]{:S(2)}) collective-permute-start(f32[48,512]{1,0:T(8,128)S(1)} %collective-permute-done.7.refs_10_), channel_id=1, source_target_pairs={{0,1},{1,0},{2,3},{3,2},{4,5},{5,4},{6,7},{7,6},{8,9},{9,8},{10,11... | collective-permute-start | bytes 294920 | tf_op jit(solution)/shard_map/ppermute | solution.py:319
  15.5 5.3 %collective-permute-start.9 = (f32[17,8,128]{2,1,0:T(8,128)S(1)}, f32[17,8,128]{2,1,0:T(8,128)S(1)}, u32[]{:S(2)}, u32[]{:S(2)}) collective-permute-start(f32[17,8,128]{2,1,0:T(8,128)S(1)} %get-tuple-element.21), channel_id=1, source_target_pairs={{0,6},{1,7},{2,4},{3,5},{4,2},{5,3},{6,0},{7,1},{8,14},{9,15},{10,... | collective-permute-start | bytes 208904 | tf_op jit(solution)/shard_map/ppermute | solution.py:322
  17.9 4.8 %collective-permute-start.10 = (f32[17,8,128]{2,1,0:T(8,128)S(1)}, f32[17,8,128]{2,1,0:T(8,128)S(1)}, u32[]{:S(2)}, u32[]{:S(2)}) collective-permute-start(f32[17,8,128]{2,1,0:T(8,128)S(1)} %get-tuple-element.22), channel_id=1, source_target_pairs={{0,2},{1,5},{2,0},{3,7},{4,6},{5,1},{6,4},{7,3},{8,10},{9,13},{10,... | collective-permute-start | bytes 208904 | tf_op jit(solution)/shard_map/ppermute | solution.py:322
  18.2 4.6 %collective-permute-start.11 = (f32[17,8,128]{2,1,0:T(8,128)S(1)}, f32[17,8,128]{2,1,0:T(8,128)S(1)}, u32[]{:S(2)}, u32[]{:S(2)}) collective-permute-start(f32[17,8,128]{2,1,0:T(8,128)S(1)} %get-tuple-element.23), channel_id=1, source_target_pairs={{0,4},{1,3},{2,6},{3,1},{4,0},{5,7},{6,2},{7,5},{8,12},{9,11},{10,... | collective-permute-start | bytes 208904 | tf_op jit(solution)/shard_map/ppermute | solution.py:322

commit v5 on v4

--- a/solution.py
+++ b/solution.py
@@ -24,6 +24,25 @@
 
 def turn(tile, shift):
     return pltpu.roll(tile, shift, 0)
+
+
+def left_right(x):
+    width = x.shape[1]
+    lane = lax.broadcasted_iota(jnp.int32, x.shape, 1)
+    left = jnp.where(lane == 0, 0.0, pltpu.roll(x, 1, 1))
+    right = jnp.where(lane == width - 1, 0.0, pltpu.roll(x, width - 1, 1))
+    return right - left
+
+
+def at(tile):
+    return pl.ds(pl.multiple_of(tile * 8, 8), 8)
+
+
+def down_up(ref, tile, x, clip=None):
+    sub = sublane(x.shape[1])
+    before = ref[at(tile - 1 if clip is None else jnp.maximum(tile - 1, 0)), :]
+    after = ref[at(tile + 1 if clip is None else jnp.minimum(tile + 1, clip)), :]
+    return turn(jnp.where(sub == 0, after, x), 7) - turn(jnp.where(sub == 7, before, x), 1)
 
 
 def where_am_i():
@@ -98,20 +117,51 @@
         copy.wait()
     lane = lax.broadcasted_iota(jnp.int32, (1, width), 1)
     for block in range(n):
-        line = jnp.where(lane == 0, owner[block], slot[block])
+        line = jnp.where(lane < width // 2, owner[block], slot[block])
         chip_bufs[0][home + rows + block : home + rows + block + 1, :] = line.astype(jnp.float32)
+
+
+def tag_kernel(n, rows, own_home, sib_home, code, tags):
+    chips = n // 2
+    width = own_home.shape[1]
+    _, me = where_am_i()
+    chip, core = me // 2, me % 2
+    span = pl.ds(8 * (NF + 1) + rows, n)
+    own, sib = own_home[span, :].astype(jnp.int32), sib_home[span, :].astype(jnp.int32)
+    both = (jnp.where(core == 0, own, sib), jnp.where(core == 0, sib, own))
+    line_id = lax.broadcasted_iota(jnp.int32, (n, 128), 0)
+    sub = sublane(128)
+    slots = []
+    for device, info in enumerate(both):
+        owner = info[:, 0:128]
+        rank = jnp.zeros((n, 128), jnp.int32)
+        for block in range(n):
+            same = jnp.logical_and(owner == owner[block : block + 1, :], line_id > block)
+            rank = jnp.where(same, rank + 1, rank)
+        mine = (owner & 1) == core
+        place = ((owner >> 1) ^ chip) * (2 * CAP) + (device * CAP) + rank
+        slots.append(jnp.where(mine, place, -1))
+        code[device] = slots[device]
+    for index, path in enumerate(routes(chips)):
+        want = sub + reached(path, core) * (2 * CAP)
+        tile = jnp.full((8, 128), -1, jnp.int32)
+        for device, info in enumerate(both):
+            for block in range(n):
+                hit = jnp.logical_and(want == slots[device][block : block + 1, :], sub < 2 * CAP)
+                tile = jnp.where(hit, info[block : block + 1, width - 128 :], tile)
+        tags[index] = tile.astype(jnp.float32)
 
 
 def step_kernel(n, *refs):
     chips = n // 2
     refs = list(refs)
     take = lambda count: [refs.pop(0) for _ in range(count)]
-    owner, slot = take(2)
+    code, tags = take(2)
     mine, theirs = take(chips), take(chips)
     across, across_sib, sweep = take(3)
-    (vel,) = take(1)
+    nxt_prs, nxt_u, nxt_v, coef = take(4)
     sends = take(chips)
-    fld, prs, vols, coef, halo, bins, tags, count, staged, named, sem = take(11)
+    fld, prs, vols, halo, parts = take(5)
     grp, me = where_am_i()
     chip, core = me // 2, me % 2
     width = sweep.shape[1]
@@ -120,18 +170,10 @@
     sweep_sib = theirs[0].at[home : home + rows, :]
     tiles = 2 * chips
     sub = sublane(width)
-    lane = lax.broadcasted_iota(jnp.int32, (8, width), 1)
     is_low = core == 0
 
     def pair(own, sib):
         return jnp.where(is_low, own, sib), jnp.where(is_low, sib, own)
-
-    def at(tile):
-        return pl.ds(pl.multiple_of(tile * 8, 8), 8)
-
-    staged[...] = theirs[0][home + rows : home + rows + n, 0:128].astype(jnp.int32)
-    naming = pltpu.make_async_copy(staged, named, sem)
-    naming.start()
 
     paths = routes(chips)
     for index, path in enumerate(paths):
@@ -160,82 +202,45 @@
             fld[field, span, :] = line(tile, field)
         fld[VELU, span, :] = jnp.where(sub == near, line(tile, VELU), line(tile, FAR_U))
         press = (line(tile, GAM) - 1.0) * line(tile, RHO) * line(tile, ENE)
-        prs[0, span, :] = jnp.where(sub == near, press, line(tile, FAR_P))
-
-    def left_right(x):
-        left = jnp.where(lane == 0, 0.0, pltpu.roll(x, 1, 1))
-        right = jnp.where(lane == width - 1, 0.0, pltpu.roll(x, width - 1, 1))
-        return right - left
-
-    def down_up(ref, index, tile, x, clip=False):
-        before = ref[index, at(jnp.maximum(tile - 1, 0) if clip else tile - 1), :]
-        after = ref[index, at(jnp.minimum(tile + 1, tiles + 1) if clip else tile + 1), :]
-        return turn(jnp.where(sub == 0, after, x), 7) - turn(jnp.where(sub == 7, before, x), 1)
+        prs[span, :] = jnp.where(sub == near, press, line(tile, FAR_P))
 
     def pressure(tile, _):
         span = at(tile)
-        prs[0, span, :] = (fld[GAM, span, :] - 1.0) * fld[RHO, span, :] * fld[ENE, span, :]
+        prs[span, :] = (fld[GAM, span, :] - 1.0) * fld[RHO, span, :] * fld[ENE, span, :]
         return 0
 
     lax.fori_loop(1, tiles + 1, pressure, 0, unroll=n <= 8)
 
     def first(tile, _):
         span = at(tile)
-        velu, velv, press = fld[VELU, span, :], fld[VELV, span, :], prs[0, span, :]
-        push = HALF_DT * (down_up(fld, VELU, tile, velu, True) + left_right(velv))
+        velu, velv, press = fld[VELU, span, :], fld[VELV, span, :], prs[span, :]
+        push = HALF_DT * (down_up(fld.at[VELU], tile, velu, tiles + 1) + left_right(velv))
         grow = 1.0 + push
         scale = HALF_DT / fld[RHO, span, :]
         keep = 1.0 - (fld[GAM, span, :] - 1.0) * push
-        nxt_p = press * keep / grow
-        nxt_u = velu - down_up(prs, 0, tile, press, True) * scale
-        nxt_v = velv - left_right(press) * scale
-        prs[1, span, :] = nxt_p
-        vols[0, span, :] = nxt_u
-        vols[1, span, :] = nxt_v
-        vols[2, span, :] = grow
-        vols[3, span, :] = fld[ENE, span, :] * keep
+        nxt_prs[span, :] = press * keep / grow
+        nxt_u[span, :] = velu - down_up(prs, tile, press, tiles + 1) * scale
+        nxt_v[span, :] = velv - left_right(press) * scale
         coef[span, :] = scale * grow
+        vols[0, span, :] = grow
+        vols[1, span, :] = fld[ENE, span, :] * keep
         return 0
 
     lax.fori_loop(0, tiles + 2, first, 0, unroll=n <= 8)
     for place, inside in ((0, inside_top), (tiles + 1, inside_bottom)):
         span = at(place)
-        prs[1, span, :] = jnp.where(inside, prs[1, span, :], 0.0)
-        vols[0, span, :] = jnp.where(inside, vols[0, span, :], 0.0)
-
-    def velocity(index, _):
-        tile = 1 + core * chips + index
-        span, dest = at(tile), at(index)
-        press, scale = prs[1, span, :], coef[span, :]
-        vel[0, dest, :] = vols[0, span, :] - down_up(prs, 1, tile, press) * scale
-        vel[1, dest, :] = vols[1, span, :] - left_right(press) * scale
-        return 0
-
-    lax.fori_loop(0, chips, velocity, 0, unroll=n <= 8)
-
-    naming.wait()
-    for mask in range(chips + 1):
-        count[mask] = 0
-        tags[mask] = jnp.full((8, 128), -1.0, jnp.float32)
-    sub128 = sublane(128)
+        nxt_prs[span, :] = jnp.where(inside, nxt_prs[span, :], 0.0)
+        nxt_u[span, :] = jnp.where(inside, nxt_u[span, :], 0.0)
 
     def cyclic(x):
         return jnp.where(sub % BR == 0, turn(x, 8 - (BR - 1)), turn(x, 1))
-
-    def place(tile_out, who, where_to):
-        fits = who % 2 == core
-        mask = jnp.where(fits, (who // 2) ^ chip, chips)
-        rank = count[mask]
-        count[mask] = jnp.where(fits, rank + 1, 0)
-        bins[mask, rank] = tile_out
-        tags[mask] = jnp.where(sub128 == rank, jnp.full((8, 128), where_to).astype(jnp.float32), tags[mask])
 
     def second(device, index):
         tile = 1 + device * chips + index
         span = at(tile)
-        push = HALF_DT * (down_up(vols, 0, tile, vols[0, span, :]) + left_right(vols[1, span, :]))
-        volume = vols[2, span, :] * (1.0 + push)
-        heat_e = vols[3, span, :] * (1.0 - (fld[GAM, span, :] - 1.0) * push)
+        push = HALF_DT * (down_up(nxt_u, tile, nxt_u[span, :]) + left_right(nxt_v[span, :]))
+        volume = vols[0, span, :] * (1.0 + push)
+        heat_e = vols[1, span, :] * (1.0 - (fld[GAM, span, :] - 1.0) * push)
         mass = fld[RHO, span, :]
         heat = mass * heat_e
         from_own = (core == 0) if device == 0 else (core == 1)
@@ -244,32 +249,55 @@
         mass_go, heat_go = frac * mass, frac * heat
         mass_part = mass - mass_go + cyclic(mass_go)
         heat_part = heat - heat_go + cyclic(heat_go)
-        for bit, tile_out in (
-            (0, jnp.where(sub < 4, mass_part, turn(heat_part, 4))),
-            (1, jnp.where(sub < 4, turn(mass_part, 4), heat_part)),
-        ):
-            block = 2 * index + bit
-            who = jnp.where(from_own, owner[block], named[block, 0])
-            where_to = jnp.where(from_own, slot[block], named[block, 1])
-            place(tile_out, who, where_to)
+        parts[device, 2 * index] = jnp.where(sub < 4, mass_part, turn(heat_part, 4))
+        parts[device, 2 * index + 1] = jnp.where(sub < 4, turn(mass_part, 4), heat_part)
 
     for device in range(2):
         lax.fori_loop(0, chips, lambda index, _, device=device: (second(device, index), 0)[1], 0, unroll=n <= 8)
 
-    for send, path in zip(sends, paths):
-        mask = reached(path, core)
-        for rank in range(2 * CAP):
-            for part in range(width // 128):
-                send[rank * (width // 128) + part] = bins[mask, rank, :, part * 128 : part * 128 + 128]
-        send[2 * CAP * (width // 128)] = tags[mask]
+    pieces = width // 128
+    for index, (send, path) in enumerate(zip(sends, paths)):
+        base = reached(path, core) * (2 * CAP)
+        for device in range(2):
+            for turn_of in range(CAP):
+                rank = device * CAP + turn_of
+                found = [jnp.zeros((8, 128), jnp.float32)] * pieces
+                for block in range(n):
+                    hit = jnp.broadcast_to(code[device, block : block + 1, :], (8, 128)) == base + rank
+                    found = [
+                        jnp.where(hit, parts[device, block, :, piece * 128 : piece * 128 + 128], found[piece])
+                        for piece in range(pieces)
+                    ]
+                for piece in range(pieces):
+                    send[rank * pieces + piece] = found[piece]
+        send[2 * CAP * pieces] = tags[index]
+
+
+def velocity_kernel(n, prs, velu, velv, coef, vel):
+    chips = n // 2
+    _, me = where_am_i()
+
+    def one(index, _):
+        tile = 1 + me % 2 * chips + index
+        span, dest = at(tile), at(index)
+        press, scale = prs[span, :], coef[span, :]
+        vel[0, dest, :] = velu[span, :] - down_up(prs, tile, press) * scale
+        vel[1, dest, :] = velv[span, :] - left_right(press) * scale
+        return 0
+
+    lax.fori_loop(0, chips, one, 0, unroll=n <= 8)
 
 
 def land_kernel(n, *refs):
     chips = n // 2
     arrived = refs[:chips]
-    mass, energy = refs[chips:]
+    mass_out, energy_out, mass, energy, sems = refs[chips:]
     parts = mass.shape[1] // 128
     sub = sublane(128)
+
+    def send(source, target, which, index):
+        span = pl.ds(pl.multiple_of(index * 8, 8), 8)
+        return pltpu.make_async_copy(source.at[span, :], target.at[span, :], sems.at[which, index])
 
     def tile_pair(index, _):
         span = pl.ds(pl.multiple_of(index * 8, 8), 8)
@@ -287,9 +315,14 @@
             even, odd = sums[0][part], sums[1][part]
             mass[span, cols] = jnp.where(sub < 4, even, turn(odd, 4))
             energy[span, cols] = jnp.where(sub < 4, turn(even, 4), odd)
+        send(mass, mass_out, 0, index).start()
+        send(energy, energy_out, 1, index).start()
         return 0
 
     lax.fori_loop(0, chips, tile_pair, 0, unroll=n <= 8)
+    for index in range(chips):
+        send(mass, mass_out, 0, index).wait()
+        send(energy, energy_out, 1, index).wait()
 
 
 def across_links(groups, n):
@@ -348,37 +381,55 @@
     theirs = [to_sibling(x) for x in mine]
     across_sib = to_sibling(across)
 
+    code, tags = pl.pallas_call(
+        functools.partial(tag_kernel, n, rows),
+        out_shape=[
+            jax.ShapeDtypeStruct((2, n, 128), jnp.int32),
+            jax.ShapeDtypeStruct((chips, 8, 128), f32),
+        ],
+        in_specs=[VMEM] * 2,
+        out_specs=[VMEM] * 2,
+        compiler_params=params,
+        name="tags",
+    )(mine[0], theirs[0])
+
     stack = (2 * chips + 2) * 8
     send_shape = (2 * CAP * parts + 1, 8, 128)
     out = pl.pallas_call(
         functools.partial(step_kernel, n),
-        out_shape=[jax.ShapeDtypeStruct((2, rows, width), f32)]
+        out_shape=[jax.ShapeDtypeStruct((stack, width), f32)] * 4
         + [jax.ShapeDtypeStruct(send_shape, f32)] * chips,
-        in_specs=[SMEM] * 2 + [VMEM] * (2 * chips + 3),
-        out_specs=[VMEM] * (chips + 1),
+        in_specs=[VMEM] * (2 * chips + 5),
+        out_specs=[VMEM] * (chips + 4),
         scratch_shapes=[
             pltpu.VMEM((NF, stack, width), f32),
+            pltpu.VMEM((stack, width), f32),
             pltpu.VMEM((2, stack, width), f32),
-            pltpu.VMEM((4, stack, width), f32),
-            pltpu.VMEM((stack, width), f32),
             pltpu.VMEM((2, chips, 8, width), f32),
-            pltpu.VMEM((chips + 1, 2 * CAP, 8, width), f32),
-            pltpu.VMEM((chips + 1, 8, 128), f32),
-            pltpu.SMEM((chips + 1,), jnp.int32),
-            pltpu.VMEM((n, 128), jnp.int32),
-            pltpu.SMEM((n, 128), jnp.int32),
-            pltpu.SemaphoreType.DMA,
+            pltpu.VMEM((2, n, 8, width), f32),
         ],
         compiler_params=params,
         name="substeps",
-    )(owner, slot_target, *mine, *theirs, across, across_sib, sweep)
-    vel = out[0]
-    arrived = [to_chip(x, path) for x, path in zip(out[1:], paths)]
+    )(code, tags, *mine, *theirs, across, across_sib, sweep)
+    arrived = [to_chip(x, path) for x, path in zip(out[4:], paths)]
+    vel = pl.pallas_call(
+        functools.partial(velocity_kernel, n),
+        out_shape=jax.ShapeDtypeStruct((2, rows, width), f32),
+        in_specs=[VMEM] * 4,
+        out_specs=VMEM,
+        compiler_params=params,
+        name="velocities",
+    )(*out[:4])
     mass, energy = pl.pallas_call(
         functools.partial(land_kernel, n),
         out_shape=[jax.ShapeDtypeStruct((rows, width), f32)] * 2,
         in_specs=[VMEM] * chips,
-        out_specs=[VMEM] * 2,
+        out_specs=[pl.BlockSpec(memory_space=pl.ANY)] * 2,
+        scratch_shapes=[
+            pltpu.VMEM((rows, width), f32),
+            pltpu.VMEM((rows, width), f32),
+            pltpu.SemaphoreType.DMA((2, chips)),
+        ],
         compiler_params=params,
         name="land",
     )(*arrived)

time: 23.8 us -> 22 us (0.924)
  Pallas kernels: 4.69 us -> 3.76 us
  waiting for transfers between devices: 8.52 us -> 7.67 us
    pallas_call x1, Pallas kernels: 2.4 us -> 0.66 us  [shards(): pl.pallas_call(functools.partial(step_kernel, n), out_shape=[jax.ShapeDty...]
    pallas_call x0 -> x2, Pallas kernels: none -> 0.82 us  [the longest x1 0.76 us: shards(): pl.pallas_call(functools.partial(velocity_kernel, n), out_shape=jax.Shape...]
    ppermute x6, waiting for transfers between devices: 7.29 us -> 6.51 us  [to_chip(): lax.ppermute(x, 'bis', [(i, i ^ 2 * path[i % 2]) for i in range(n)])]
  transfers between devices with their start and end apart: 12 -> 12, of which waited for: 7 -> 7; matrix products, arithmetic and copies ran while one was open for 0% -> 0% of each run, Pallas kernels for 0% -> 4%
where the time goes in v5:
time: 22 us; the launch traced here: 21.8 us
  starting transfers between devices  9.73 us (44%)
  waiting for transfers between devices  7.67 us (35%)
  Pallas kernels  3.76 us (17%)
  between operations  0.67 us (3%)
    ppermute x6, starting transfers between devices, to_chip(): lax.ppermute(x, 'bis', [(i, i ^ 2 * path[i % 2]) for i in range(n)])  8.64 us
    ppermute x6, waiting for transfers between devices, to_chip(): lax.ppermute(x, 'bis', [(i, i ^ 2 * path[i % 2]) for i in range(n)])  6.51 us
    pallas_call x1, Pallas kernels, shards(): pl.pallas_call(functools.partial(pack_kernel, n), out_shape=[jax.ShapeDty...  1.4 us
    ppermute x5, waiting for transfers between devices, to_sibling(): return lax.ppermute(x, 'bis', [(i, i ^ 1) for i in range(n)])  1.16 us
    ppermute x5, starting transfers between devices, to_sibling(): return lax.ppermute(x, 'bis', [(i, i ^ 1) for i in range(n)])  1.09 us
    pallas_call x1, Pallas kernels, shards(): pl.pallas_call(functools.partial(land_kernel, n), out_shape=[jax.ShapeDty...  0.88 us
    pallas_call x1, Pallas kernels, shards(): pl.pallas_call(functools.partial(velocity_kernel, n), out_shape=jax.Shape...  0.76 us
    pallas_call x1, Pallas kernels, shards(): pl.pallas_call(functools.partial(step_kernel, n), out_shape=[jax.ShapeDty...  0.66 us
  transfers between devices with their start and end apart: 12, of which 7 were waited for; matrix products, arithmetic and copies ran while one was open for 0% of the time, Pallas kernels for 4%

profile of v5, /device:TPU:0, one launch (start us, length us, event | category | flops | bytes accessed | tf_op | source)
XLA Modules:
  0.0 21.8 jit_solution(598081444460825795)
XLA Ops:
  0.6 1.4 %pack.1 = (f32[88,512]{1,0:T(8,128)S(1)}, f32[48,512]{1,0:T(8,128)S(1)}, f32[48,512]{1,0:T(8,128)S(1)}, f32[48,512]{1,0:T(8,128)S(1)}, f32[48,512]{1,0:T(8,128)S(1)}) custom-call(s32[8]{0:T(128)} %bitcast.2, s32[8]{0:T(128)} %bitcast.3, s32[8]{0:T(128)} %refs_2_.1, f32[32,512]{1,0:T(8,128)} %refs_12_.1, f32[5,32,512]{2,1,0:T(8,128)} %refs_4_.1), custom_call_target="tpu_custom_call" | custom-call | tf_op jit(solution)/shard_map/pack/pallas_call | solution.py:361
  2.0 4.0 %collective-permute-start.1 = (f32[48,512]{1,0:T(8,128)S(1)}, f32[48,512]{1,0:T(8,128)S(1)}, u32[]{:S(2)}, u32[]{:S(2)}) collective-permute-start(f32[48,512]{1,0:T(8,128)S(1)} %get-tuple-element.23), channel_id=1, source_target_pairs={{0,6},{1,7},{2,4},{3,5},{4,2},{5,3},{6,0},{7,1},{8,14},{9,15},{10,... | collective-permute-start | bytes 294920 | tf_op jit(solution)/shard_map/ppermute | solution.py:355
  6.0 0.5 %collective-permute-start.2 = (f32[48,512]{1,0:T(8,128)S(1)}, f32[48,512]{1,0:T(8,128)S(1)}, u32[]{:S(2)}, u32[]{:S(2)}) collective-permute-start(f32[48,512]{1,0:T(8,128)S(1)} %get-tuple-element.24), channel_id=1, source_target_pairs={{0,2},{1,5},{2,0},{3,7},{4,6},{5,1},{6,4},{7,3},{8,10},{9,13},{10,... | collective-permute-start | bytes 294920 | tf_op jit(solution)/shard_map/ppermute | solution.py:355
  6.5 0.1 collective-permute-start.3
  6.6 0.0 collective-permute-start.7
  6.7 0.0 copy-start
  6.7 0.5 %collective-permute-start = (f32[88,512]{1,0:T(8,128)S(1)}, f32[88,512]{1,0:T(8,128)S(1)}, u32[]{:S(2)}, u32[]{:S(2)}) collective-permute-start(f32[88,512]{1,0:T(8,128)S(1)} %get-tuple-element.20.own_home.refs_2_), channel_id=1, source_target_pairs={{0,1},{1,0},{2,3},{3,2},{4,5},{5,4},{6,7},{7,6},{8,9},{9,8},{10,11... | collective-permute-start | bytes 540680 | tf_op jit(solution)/shard_map/ppermute | solution.py:352
  7.2 2.0 %collective-permute-done.1.refs_3_ = f32[48,512]{1,0:T(8,128)S(1)} collective-permute-done((f32[48,512]{1,0:T(8,128)S(1)}, f32[48,512]{1,0:T(8,128)S(1)}, u32[]{:S(2)}, u32[]{:S(2)}) %collective-permute-start.1) | collective-permute-done | bytes 98336 | tf_op jit(solution)/shard_map/ppermute | solution.py:355
  9.2 0.0 collective-permute-start.4
  9.2 2.0 %collective-permute-done.2.refs_4_ = f32[48,512]{1,0:T(8,128)S(1)} collective-permute-done((f32[48,512]{1,0:T(8,128)S(1)}, f32[48,512]{1,0:T(8,128)S(1)}, u32[]{:S(2)}, u32[]{:S(2)}) %collective-permute-start.2) | collective-permute-done | bytes 98336 | tf_op jit(solution)/shard_map/ppermute | solution.py:355
  11.2 0.0 collective-permute-start.5
  11.2 0.0 collective-permute-done.3.refs_5_
  11.2 0.5 %collective-permute-start.6 = (f32[48,512]{1,0:T(8,128)S(1)}, f32[48,512]{1,0:T(8,128)S(1)}, u32[]{:S(2)}, u32[]{:S(2)}) collective-permute-start(f32[48,512]{1,0:T(8,128)S(1)} %collective-permute-done.3.refs_5_), channel_id=1, source_target_pairs={{0,1},{1,0},{2,3},{3,2},{4,5},{5,4},{6,7},{7,6},{8,9},{9,8},{10,11... | collective-permute-start | bytes 294920 | tf_op jit(solution)/shard_map/ppermute | solution.py:352
  11.8 0.0 collective-permute-done.7.refs_10_
  11.8 0.1 collective-permute-start.8
  11.8 0.0 collective-permute-done.sib_home.refs_6_
  11.8 0.1 tags.1
  11.9 0.0 collective-permute-done.4.refs_7_
  11.9 0.6 %collective-permute-done.5.refs_8_ = f32[48,512]{1,0:T(8,128)S(1)} collective-permute-done((f32[48,512]{1,0:T(8,128)S(1)}, f32[48,512]{1,0:T(8,128)S(1)}, u32[]{:S(2)}, u32[]{:S(2)}) %collective-permute-start.5) | collective-permute-done | bytes 98336 | tf_op jit(solution)/shard_map/ppermute | solution.py:352
  12.5 0.2 collective-permute-done.6.refs_9_
  12.7 0.4 %collective-permute-done.8.refs_11_ = f32[48,512]{1,0:T(8,128)S(1)} collective-permute-done((f32[48,512]{1,0:T(8,128)S(1)}, f32[48,512]{1,0:T(8,128)S(1)}, u32[]{:S(2)}, u32[]{:S(2)}) %collective-permute-start.8) | collective-permute-done | bytes 98336 | tf_op jit(solution)/shard_map/ppermute | solution.py:352
  13.1 0.0 copy-done
  13.1 0.7 %substeps.1 = (f32[80,512]{1,0:T(8,128)S(1)}, f32[80,512]{1,0:T(8,128)S(1)}, f32[80,512]{1,0:T(8,128)S(1)}, f32[80,512]{1,0:T(8,128)S(1)}, f32[17,8,128]{2,1,0:T...) custom-call(s32[2,8,128]{2,1,0:T(8,128)S(1)} %get-tuple-element.21.refs_0_, ...), custom_call_target="tpu_custom_call" | custom-call | tf_op jit(solution)/shard_map/substeps/pallas_call | solution.py:398
  13.7 2.4 %collective-permute-start.9 = (f32[17,8,128]{2,1,0:T(8,128)S(1)}, f32[17,8,128]{2,1,0:T(8,128)S(1)}, u32[]{:S(2)}, u32[]{:S(2)}) collective-permute-start(f32[17,8,128]{2,1,0:T(8,128)S(1)} %get-tuple-element.28), channel_id=1, source_target_pairs={{0,6},{1,7},{2,4},{3,5},{4,2},{5,3},{6,0},{7,1},{8,14},{9,15},{10,... | collective-permute-start | bytes 208904 | tf_op jit(solution)/shard_map/ppermute | solution.py:355
  16.1 0.2 %collective-permute-start.10 = (f32[17,8,128]{2,1,0:T(8,128)S(1)}, f32[17,8,128]{2,1,0:T(8,128)S(1)}, u32[]{:S(2)}, u32[]{:S(2)}) collective-permute-start(f32[17,8,128]{2,1,0:T(8,128)S(1)} %get-tuple-element.29), channel_id=1, source_target_pairs={{0,2},{1,5},{2,0},{3,7},{4,6},{5,1},{6,4},{7,3},{8,10},{9,13},{10,... | collective-permute-start | bytes 208904 | tf_op jit(solution)/shard_map/ppermute | solution.py:355
  16.4 1.4 %collective-permute-start.11 = (f32[17,8,128]{2,1,0:T(8,128)S(1)}, f32[17,8,128]{2,1,0:T(8,128)S(1)}, u32[]{:S(2)}, u32[]{:S(2)}) collective-permute-start(f32[17,8,128]{2,1,0:T(8,128)S(1)} %get-tuple-element.30), channel_id=1, source_target_pairs={{0,4},{1,3},{2,6},{3,1},{4,0},{5,7},{6,2},{7,5},{8,12},{9,11},{10,... | collective-permute-start | bytes 208904 | tf_op jit(solution)/shard_map/ppermute | solution.py:355
  17.8 0.8 %velocities.1 = f32[2,32,512]{2,1,0:T(8,128)} custom-call(f32[80,512]{1,0:T(8,128)S(1)} %get-tuple-element.33.prs, f32[80,512]{1,0:T(8,128)S(1)} %get-tuple-element.34.velu, f32[80,512]{1,0:T(8,128)S(1)} %get-tuple-element.35.velv, f32[80,512]{1,0:T(8,128)S(1)} %get-tuple-element.36.coef), custom_call_target="tpu_custom_call" | custom-call | tf_op jit(solution)/shard_map/velocities/pallas_call | solution.py:415
  18.5 0.5 %collective-permute-done.9.refs_1_ = f32[17,8,128]{2,1,0:T(8,128)S(1)} collective-permute-done((f32[17,8,128]{2,1,0:T(8,128)S(1)}, f32[17,8,128]{2,1,0:T(8,128)S(1)}, u32[]{:S(2)}, u32[]{:S(2)}) %collective-permute-start.9) | collective-permute-done | bytes 69664 | tf_op jit(solution)/shard_map/ppermute | solution.py:355
  19.0 1.9 %collective-permute-done.10.refs_2_ = f32[17,8,128]{2,1,0:T(8,128)S(1)} collective-permute-done((f32[17,8,128]{2,1,0:T(8,128)S(1)}, f32[17,8,128]{2,1,0:T(8,128)S(1)}, u32[]{:S(2)}, u32[]{:S(2)}) %collective-permute-start.10) | collective-permute-done | bytes 69664 | tf_op jit(solution)/shard_map/ppermute | solution.py:355
  21.0 0.0 collective-permute-done.11.refs_3_
  21.0 0.9 %land.1 = (f32[32,512]{1,0:T(8,128)}, f32[32,512]{1,0:T(8,128)}) custom-call(f32[17,8,128]{2,1,0:T(8,128)S(1)} %get-tuple-element.27.refs_0_, f32[17,8,128]{2,1,0:T(8,128)S(1)} %collective-permute-done.9.refs_1_, f32[17,8,128]{2,1,0:T(8,128)S(1)} %collective-permute-done.10.refs_2_, f32[17,8,128]{2,1,0:T(8,128)S(1)} %collective-permute-done.11.refs_3_), custom_call_target="tpu_custom_call" | custom-call | tf_op jit(solution)/shard_map/land/pallas_call | solution.py:423
Async XLA Ops:
  2.0 7.1 %collective-permute-start.1 = (f32[48,512]{1,0:T(8,128)S(1)}, f32[48,512]{1,0:T(8,128)S(1)}, u32[]{:S(2)}, u32[]{:S(2)}) collective-permute-start(f32[48,512]{1,0:T(8,128)S(1)} %get-tuple-element.23), channel_id=1, source_target_pairs={{0,6},{1,7},{2,4},{3,5},{4,2},{5,3},{6,0},{7,1},{8,14},{9,15},{10,... | collective-permute-start | bytes 294920 | tf_op jit(solution)/shard_map/ppermute | solution.py:355
  6.0 5.2 %collective-permute-start.2 = (f32[48,512]{1,0:T(8,128)S(1)}, f32[48,512]{1,0:T(8,128)S(1)}, u32[]{:S(2)}, u32[]{:S(2)}) collective-permute-start(f32[48,512]{1,0:T(8,128)S(1)} %get-tuple-element.24), channel_id=1, source_target_pairs={{0,2},{1,5},{2,0},{3,7},{4,6},{5,1},{6,4},{7,3},{8,10},{9,13},{10,... | collective-permute-start | bytes 294920 | tf_op jit(solution)/shard_map/ppermute | solution.py:355
  6.5 4.7 %collective-permute-start.3 = (f32[48,512]{1,0:T(8,128)S(1)}, f32[48,512]{1,0:T(8,128)S(1)}, u32[]{:S(2)}, u32[]{:S(2)}) collective-permute-start(f32[48,512]{1,0:T(8,128)S(1)} %get-tuple-element.25), channel_id=1, source_target_pairs={{0,4},{1,3},{2,6},{3,1},{4,0},{5,7},{6,2},{7,5},{8,12},{9,11},{10,... | collective-permute-start | bytes 294920 | tf_op jit(solution)/shard_map/ppermute | solution.py:355
  6.6 5.1 %collective-permute-start.7 = (f32[48,512]{1,0:T(8,128)S(1)}, f32[48,512]{1,0:T(8,128)S(1)}, u32[]{:S(2)}, u32[]{:S(2)}) collective-permute-start(f32[48,512]{1,0:T(8,128)S(1)} %get-tuple-element.26), channel_id=1, source_target_pairs={{2,3},{3,2},{4,5},{5,4},{7,8},{8,7},{6,14},{14,6},{10,11},{11,10},... | collective-permute-start | bytes 294920 | tf_op jit(solution)/shard_map/ppermute | solution.py:379
  6.7 6.4 %copy-start = (f32[32,512]{1,0:T(8,128)S(1)}, f32[32,512]{1,0:T(8,128)}, u32[]{:S(2)}) copy-start(f32[32,512]{1,0:T(8,128)} %refs_12_.1) | copy-start | bytes 196612
  6.7 5.2 %collective-permute-start = (f32[88,512]{1,0:T(8,128)S(1)}, f32[88,512]{1,0:T(8,128)S(1)}, u32[]{:S(2)}, u32[]{:S(2)}) collective-permute-start(f32[88,512]{1,0:T(8,128)S(1)} %get-tuple-element.20.own_home.refs_2_), channel_id=1, source_target_pairs={{0,1},{1,0},{2,3},{3,2},{4,5},{5,4},{6,7},{7,6},{8,9},{9,8},{10,11... | collective-permute-start | bytes 540680 | tf_op jit(solution)/shard_map/ppermute | solution.py:352
  9.2 2.7 %collective-permute-start.4 = (f32[48,512]{1,0:T(8,128)S(1)}, f32[48,512]{1,0:T(8,128)S(1)}, u32[]{:S(2)}, u32[]{:S(2)}) collective-permute-start(f32[48,512]{1,0:T(8,128)S(1)} %collective-permute-done.1.refs_3_), channel_id=1, source_target_pairs={{0,1},{1,0},{2,3},{3,2},{4,5},{5,4},{6,7},{7,6},{8,9},{9,8},{10,11... | collective-permute-start | bytes 294920 | tf_op jit(solution)/shard_map/ppermute | solution.py:352
  11.2 1.3 %collective-permute-start.5 = (f32[48,512]{1,0:T(8,128)S(1)}, f32[48,512]{1,0:T(8,128)S(1)}, u32[]{:S(2)}, u32[]{:S(2)}) collective-permute-start(f32[48,512]{1,0:T(8,128)S(1)} %collective-permute-done.2.refs_4_), channel_id=1, source_target_pairs={{0,1},{1,0},{2,3},{3,2},{4,5},{5,4},{6,7},{7,6},{8,9},{9,8},{10,11... | collective-permute-start | bytes 294920 | tf_op jit(solution)/shard_map/ppermute | solution.py:352
  11.2 1.5 %collective-permute-start.6 = (f32[48,512]{1,0:T(8,128)S(1)}, f32[48,512]{1,0:T(8,128)S(1)}, u32[]{:S(2)}, u32[]{:S(2)}) collective-permute-start(f32[48,512]{1,0:T(8,128)S(1)} %collective-permute-done.3.refs_5_), channel_id=1, source_target_pairs={{0,1},{1,0},{2,3},{3,2},{4,5},{5,4},{6,7},{7,6},{8,9},{9,8},{10,11... | collective-permute-start | bytes 294920 | tf_op jit(solution)/shard_map/ppermute | solution.py:352
  11.8 1.3 %collective-permute-start.8 = (f32[48,512]{1,0:T(8,128)S(1)}, f32[48,512]{1,0:T(8,128)S(1)}, u32[]{:S(2)}, u32[]{:S(2)}) collective-permute-start(f32[48,512]{1,0:T(8,128)S(1)} %collective-permute-done.7.refs_10_), channel_id=1, source_target_pairs={{0,1},{1,0},{2,3},{3,2},{4,5},{5,4},{6,7},{7,6},{8,9},{9,8},{10,11... | collective-permute-start | bytes 294920 | tf_op jit(solution)/shard_map/ppermute | solution.py:352
  13.7 5.3 %collective-permute-start.9 = (f32[17,8,128]{2,1,0:T(8,128)S(1)}, f32[17,8,128]{2,1,0:T(8,128)S(1)}, u32[]{:S(2)}, u32[]{:S(2)}) collective-permute-start(f32[17,8,128]{2,1,0:T(8,128)S(1)} %get-tuple-element.28), channel_id=1, source_target_pairs={{0,6},{1,7},{2,4},{3,5},{4,2},{5,3},{6,0},{7,1},{8,14},{9,15},{10,... | collective-permute-start | bytes 208904 | tf_op jit(solution)/shard_map/ppermute | solution.py:355
  16.1 4.8 %collective-permute-start.10 = (f32[17,8,128]{2,1,0:T(8,128)S(1)}, f32[17,8,128]{2,1,0:T(8,128)S(1)}, u32[]{:S(2)}, u32[]{:S(2)}) collective-permute-start(f32[17,8,128]{2,1,0:T(8,128)S(1)} %get-tuple-element.29), channel_id=1, source_target_pairs={{0,2},{1,5},{2,0},{3,7},{4,6},{5,1},{6,4},{7,3},{8,10},{9,13},{10,... | collective-permute-start | bytes 208904 | tf_op jit(solution)/shard_map/ppermute | solution.py:355
  16.4 4.6 %collective-permute-start.11 = (f32[17,8,128]{2,1,0:T(8,128)S(1)}, f32[17,8,128]{2,1,0:T(8,128)S(1)}, u32[]{:S(2)}, u32[]{:S(2)}) collective-permute-start(f32[17,8,128]{2,1,0:T(8,128)S(1)} %get-tuple-element.30), channel_id=1, source_target_pairs={{0,4},{1,3},{2,6},{3,1},{4,0},{5,7},{6,2},{7,5},{8,12},{9,11},{10,... | collective-permute-start | bytes 208904 | tf_op jit(solution)/shard_map/ppermute | solution.py:355

commit v6 on v5

--- a/solution.py
+++ b/solution.py
@@ -9,7 +9,7 @@
 
 BR = 4
 CAP = 2
-ZR = 48
+ZR = 8
 HALF_DT = 0.075
 NF = 5
 RHO, ENE, VELU, VELV, GAM = range(NF)
@@ -88,31 +88,28 @@
     def tile_of(field, block):
         return state[field, pl.ds(pl.multiple_of(block // 2 * 8, 8), 8), :]
 
-    def halo(index):
+    def halo(buf, base, index):
         block = order[index]
-        odd = block % 2 * 4
-        near = odd + jnp.where(first, 0, BR - 1)
-        far = odd + jnp.where(first, 1, BR - 2)
-        tiles = [tile_of(field, block) for field in range(NF)]
-        press = (tiles[GAM] - 1.0) * tiles[RHO] * tiles[ENE]
-        out = turn(tiles[0], (8 - near) % 8)
-        for field in range(1, NF):
-            out = jnp.where(sub == field, turn(tiles[field], (field + 8 - near) % 8), out)
-        out = jnp.where(sub == FAR_P, turn(press, (FAR_P + 8 - far) % 8), out)
-        return jnp.where(sub == FAR_U, turn(tiles[VELU], (FAR_U + 8 - far) % 8), out)
+        near = block * 4 + jnp.where(first, 0, BR - 1)
+        far = block * 4 + jnp.where(first, 1, BR - 2)
+        for field in range(NF):
+            buf[base + field : base + field + 1, :] = state[field, pl.ds(near, 1), :]
+        line = lambda field: state[field, pl.ds(far, 1), :]
+        buf[base + FAR_P : base + FAR_P + 1, :] = (line(GAM) - 1.0) * line(RHO) * line(ENE)
+        buf[base + FAR_U : base + FAR_U + 1, :] = line(VELU)
 
     for field in range(NF):
         copies[1 + field].wait()
         for buf, goal in zip(chip_bufs, goals):
             low = order[2 * goal]
             high = order[2 * goal + 1]
-            even = turn(tile_of(field, low), low % 2 * 4)
-            odd = turn(tile_of(field, high), 4 - high % 2 * 4)
-            buf[8 * field : 8 * field + 8, :] = jnp.where(sub < 4, even, odd)
+            for line in range(BR):
+                buf[8 * field + line : 8 * field + line + 1, :] = state[field, pl.ds(low * BR + line, 1), :]
+                buf[8 * field + BR + line : 8 * field + BR + line + 1, :] = state[field, pl.ds(high * BR + line, 1), :]
     for buf, goal in zip(chip_bufs, goals):
         beyond = jnp.where(first, jnp.minimum(2 * goal + 2, n - 1), jnp.maximum(2 * goal - 1, 0))
-        buf[8 * NF : home, :] = halo(beyond)
-    across[0:8, :] = halo(jnp.where(first, 0, n - 1))
+        halo(buf, 8 * NF, beyond)
+    halo(across, 0, jnp.where(first, 0, n - 1))
     for copy in copies[1 + NF :]:
         copy.wait()
     lane = lax.broadcasted_iota(jnp.int32, (1, width), 1)
@@ -379,7 +376,7 @@
     across = lax.ppermute(packed[chips], ("grp", "bis"), across_links(groups, n))
     mine = [to_chip(x, path) for x, path in zip(packed, paths)]
     theirs = [to_sibling(x) for x in mine]
-    across_sib = to_sibling(across)
+    across_sib = to_sibling(jnp.concatenate([across] + [x[0:8] for x in mine[1:]]))
 
     code, tags = pl.pallas_call(
         functools.partial(tag_kernel, n, rows),

time: 22 us -> 21.6 us (0.982)
  starting transfers between devices: 9.73 us -> 9.31 us
    ppermute x6, starting transfers between devices: 8.64 us -> 8.16 us  [to_chip(): lax.ppermute(x, 'bis', [(i, i ^ 2 * path[i % 2]) for i in range(n)])]
  transfers between devices with their start and end apart: 12 -> 12, of which waited for: 7 -> 6; matrix products, arithmetic and copies ran while one was open for 0% -> 0% of each run, Pallas kernels for 4% -> 4%
where the time goes in v6:
time: 21.6 us; the launch traced here: 21.4 us
  starting transfers between devices  9.31 us (43%)
  waiting for transfers between devices  7.74 us (36%)
  Pallas kernels  3.65 us (17%)
  between operations  0.7 us (3%)
    ppermute x6, starting transfers between devices, to_chip(): lax.ppermute(x, 'bis', [(i, i ^ 2 * path[i % 2]) for i in range(n)])  8.16 us
    ppermute x6, waiting for transfers between devices, to_chip(): lax.ppermute(x, 'bis', [(i, i ^ 2 * path[i % 2]) for i in range(n)])  6.62 us
    pallas_call x1, Pallas kernels, shards(): pl.pallas_call(functools.partial(pack_kernel, n), out_shape=[jax.ShapeDty...  1.28 us
    ppermute x5, starting transfers between devices, to_sibling(): return lax.ppermute(x, 'bis', [(i, i ^ 1) for i in range(n)])  1.15 us
    ppermute x5, waiting for transfers between devices, to_sibling(): return lax.ppermute(x, 'bis', [(i, i ^ 1) for i in range(n)])  1.12 us
    pallas_call x1, Pallas kernels, shards(): pl.pallas_call(functools.partial(land_kernel, n), out_shape=[jax.ShapeDty...  0.88 us
    pallas_call x1, Pallas kernels, shards(): pl.pallas_call(functools.partial(velocity_kernel, n), out_shape=jax.Shape...  0.76 us
    pallas_call x1, Pallas kernels, shards(): pl.pallas_call(functools.partial(step_kernel, n), out_shape=[jax.ShapeDty...  0.68 us
  transfers between devices with their start and end apart: 12, of which 6 were waited for; matrix products, arithmetic and copies ran while one was open for 0% of the time, Pallas kernels for 4%

profile of v6, /device:TPU:0, one launch (start us, length us, event | category | flops | bytes accessed | tf_op | source)
XLA Modules:
  0.0 21.4 jit_solution(12432032117789179623)
XLA Ops:
  0.6 1.3 %pack.1 = (f32[88,512]{1,0:T(8,128)S(1)}, f32[48,512]{1,0:T(8,128)S(1)}, f32[48,512]{1,0:T(8,128)S(1)}, f32[48,512]{1,0:T(8,128)S(1)}, f32[8,512]{1,0:T(8,128)S(1)}) custom-call(s32[8]{0:T(128)} %bitcast.2, s32[8]{0:T(128)} %bitcast.3, s32[8]{0:T(128)} %refs_2_.1, f32[32,512]{1,0:T(8,128)} %refs_12_.1, f32[5,32,512]{2,1,0:T(8,128)} %refs_4_.1), custom_call_target="tpu_custom_call" | custom-call | tf_op jit(solution)/shard_map/pack/pallas_call | solution.py:358
  1.9 4.0 %collective-permute-start.1 = (f32[48,512]{1,0:T(8,128)S(1)}, f32[48,512]{1,0:T(8,128)S(1)}, u32[]{:S(2)}, u32[]{:S(2)}) collective-permute-start(f32[48,512]{1,0:T(8,128)S(1)} %get-tuple-element.23), channel_id=1, source_target_pairs={{0,6},{1,7},{2,4},{3,5},{4,2},{5,3},{6,0},{7,1},{8,14},{9,15},{10,... | collective-permute-start | bytes 294920 | tf_op jit(solution)/shard_map/ppermute | solution.py:352
  5.9 0.5 %collective-permute-start.2 = (f32[48,512]{1,0:T(8,128)S(1)}, f32[48,512]{1,0:T(8,128)S(1)}, u32[]{:S(2)}, u32[]{:S(2)}) collective-permute-start(f32[48,512]{1,0:T(8,128)S(1)} %get-tuple-element.24), channel_id=1, source_target_pairs={{0,2},{1,5},{2,0},{3,7},{4,6},{5,1},{6,4},{7,3},{8,10},{9,13},{10,... | collective-permute-start | bytes 294920 | tf_op jit(solution)/shard_map/ppermute | solution.py:352
  6.4 0.1 collective-permute-start.3
  6.5 0.0 collective-permute-start.7
  6.5 0.5 %collective-permute-start = (f32[88,512]{1,0:T(8,128)S(1)}, f32[88,512]{1,0:T(8,128)S(1)}, u32[]{:S(2)}, u32[]{:S(2)}) collective-permute-start(f32[88,512]{1,0:T(8,128)S(1)} %get-tuple-element.20.own_home.refs_2_), channel_id=1, source_target_pairs={{0,1},{1,0},{2,3},{3,2},{4,5},{5,4},{6,7},{7,6},{8,9},{9,8},{10,11... | collective-permute-start | bytes 540680 | tf_op jit(solution)/shard_map/ppermute | solution.py:349
  7.0 2.0 %collective-permute-done.1.refs_3_ = f32[48,512]{1,0:T(8,128)S(1)} collective-permute-done((f32[48,512]{1,0:T(8,128)S(1)}, f32[48,512]{1,0:T(8,128)S(1)}, u32[]{:S(2)}, u32[]{:S(2)}) %collective-permute-start.1) | collective-permute-done | bytes 98336 | tf_op jit(solution)/shard_map/ppermute | solution.py:352
  9.1 0.0 collective-permute-start.4
  9.1 2.0 %collective-permute-done.2.refs_4_ = f32[48,512]{1,0:T(8,128)S(1)} collective-permute-done((f32[48,512]{1,0:T(8,128)S(1)}, f32[48,512]{1,0:T(8,128)S(1)}, u32[]{:S(2)}, u32[]{:S(2)}) %collective-permute-start.2) | collective-permute-done | bytes 98336 | tf_op jit(solution)/shard_map/ppermute | solution.py:352
  11.1 0.0 collective-permute-start.5
  11.1 0.0 collective-permute-done.3.refs_5_
  11.1 0.5 %collective-permute-start.6 = (f32[48,512]{1,0:T(8,128)S(1)}, f32[48,512]{1,0:T(8,128)S(1)}, u32[]{:S(2)}, u32[]{:S(2)}) collective-permute-start(f32[48,512]{1,0:T(8,128)S(1)} %collective-permute-done.3.refs_5_), channel_id=1, source_target_pairs={{0,1},{1,0},{2,3},{3,2},{4,5},{5,4},{6,7},{7,6},{8,9},{9,8},{10,11... | collective-permute-start | bytes 294920 | tf_op jit(solution)/shard_map/ppermute | solution.py:349
  11.6 0.0 collective-permute-done.7.refs_10_
  11.6 0.0 copy-start
  11.7 0.1 collective-permute-start.8
  11.8 0.0 collective-permute-done.sib_home.refs_6_
  11.8 0.1 tags.1
  11.9 1.1 %collective-permute-done.8.refs_11_ = f32[32,512]{1,0:T(8,128)S(1)} collective-permute-done((f32[32,512]{1,0:T(8,128)S(1)}, f32[32,512]{1,0:T(8,128)S(1)}, u32[]{:S(2)}, u32[]{:S(2)}) %collective-permute-start.8) | collective-permute-done | bytes 65568 | tf_op jit(solution)/shard_map/ppermute | solution.py:349
  13.0 0.0 collective-permute-done.4.refs_7_
  13.0 0.0 collective-permute-done.5.refs_8_
  13.0 0.0 collective-permute-done.6.refs_9_
  13.0 0.0 copy-done
  13.0 0.7 %substeps.1 = (f32[80,512]{1,0:T(8,128)S(1)}, f32[80,512]{1,0:T(8,128)S(1)}, f32[80,512]{1,0:T(8,128)S(1)}, f32[80,512]{1,0:T(8,128)S(1)}, f32[17,8,128]{2,1,0:T...) custom-call(s32[2,8,128]{2,1,0:T(8,128)S(1)} %get-tuple-element.21.refs_0_, ...), custom_call_target="tpu_custom_call" | custom-call | tf_op jit(solution)/shard_map/substeps/pallas_call | solution.py:395
  13.7 1.6 %collective-permute-start.9 = (f32[17,8,128]{2,1,0:T(8,128)S(1)}, f32[17,8,128]{2,1,0:T(8,128)S(1)}, u32[]{:S(2)}, u32[]{:S(2)}) collective-permute-start(f32[17,8,128]{2,1,0:T(8,128)S(1)} %get-tuple-element.28), channel_id=1, source_target_pairs={{0,6},{1,7},{2,4},{3,5},{4,2},{5,3},{6,0},{7,1},{8,14},{9,15},{10,... | collective-permute-start | bytes 208904 | tf_op jit(solution)/shard_map/ppermute | solution.py:352
  15.3 1.0 %collective-permute-start.10 = (f32[17,8,128]{2,1,0:T(8,128)S(1)}, f32[17,8,128]{2,1,0:T(8,128)S(1)}, u32[]{:S(2)}, u32[]{:S(2)}) collective-permute-start(f32[17,8,128]{2,1,0:T(8,128)S(1)} %get-tuple-element.29), channel_id=1, source_target_pairs={{0,2},{1,5},{2,0},{3,7},{4,6},{5,1},{6,4},{7,3},{8,10},{9,13},{10,... | collective-permute-start | bytes 208904 | tf_op jit(solution)/shard_map/ppermute | solution.py:352
  16.2 1.0 %collective-permute-start.11 = (f32[17,8,128]{2,1,0:T(8,128)S(1)}, f32[17,8,128]{2,1,0:T(8,128)S(1)}, u32[]{:S(2)}, u32[]{:S(2)}) collective-permute-start(f32[17,8,128]{2,1,0:T(8,128)S(1)} %get-tuple-element.30), channel_id=1, source_target_pairs={{0,4},{1,3},{2,6},{3,1},{4,0},{5,7},{6,2},{7,5},{8,12},{9,11},{10,... | collective-permute-start | bytes 208904 | tf_op jit(solution)/shard_map/ppermute | solution.py:352
  17.2 0.8 %velocities.1 = f32[2,32,512]{2,1,0:T(8,128)} custom-call(f32[80,512]{1,0:T(8,128)S(1)} %get-tuple-element.33.prs, f32[80,512]{1,0:T(8,128)S(1)} %get-tuple-element.34.velu, f32[80,512]{1,0:T(8,128)S(1)} %get-tuple-element.35.velv, f32[80,512]{1,0:T(8,128)S(1)} %get-tuple-element.36.coef), custom_call_target="tpu_custom_call" | custom-call | tf_op jit(solution)/shard_map/velocities/pallas_call | solution.py:412
  18.0 1.0 %collective-permute-done.9.refs_1_ = f32[17,8,128]{2,1,0:T(8,128)S(1)} collective-permute-done((f32[17,8,128]{2,1,0:T(8,128)S(1)}, f32[17,8,128]{2,1,0:T(8,128)S(1)}, u32[]{:S(2)}, u32[]{:S(2)}) %collective-permute-start.9) | collective-permute-done | bytes 69664 | tf_op jit(solution)/shard_map/ppermute | solution.py:352
  19.0 1.1 %collective-permute-done.10.refs_2_ = f32[17,8,128]{2,1,0:T(8,128)S(1)} collective-permute-done((f32[17,8,128]{2,1,0:T(8,128)S(1)}, f32[17,8,128]{2,1,0:T(8,128)S(1)}, u32[]{:S(2)}, u32[]{:S(2)}) %collective-permute-start.10) | collective-permute-done | bytes 69664 | tf_op jit(solution)/shard_map/ppermute | solution.py:352
  20.1 0.4 %collective-permute-done.11.refs_3_ = f32[17,8,128]{2,1,0:T(8,128)S(1)} collective-permute-done((f32[17,8,128]{2,1,0:T(8,128)S(1)}, f32[17,8,128]{2,1,0:T(8,128)S(1)}, u32[]{:S(2)}, u32[]{:S(2)}) %collective-permute-start.11) | collective-permute-done | bytes 69664 | tf_op jit(solution)/shard_map/ppermute | solution.py:352
  20.5 0.9 %land.1 = (f32[32,512]{1,0:T(8,128)}, f32[32,512]{1,0:T(8,128)}) custom-call(f32[17,8,128]{2,1,0:T(8,128)S(1)} %get-tuple-element.27.refs_0_, f32[17,8,128]{2,1,0:T(8,128)S(1)} %collective-permute-done.9.refs_1_, f32[17,8,128]{2,1,0:T(8,128)S(1)} %collective-permute-done.10.refs_2_, f32[17,8,128]{2,1,0:T(8,128)S(1)} %collective-permute-done.11.refs_3_), custom_call_target="tpu_custom_call" | custom-call | tf_op jit(solution)/shard_map/land/pallas_call | solution.py:420
  (4 shorter events, 0.0 us)
Async XLA Ops:
  1.9 7.1 %collective-permute-start.1 = (f32[48,512]{1,0:T(8,128)S(1)}, f32[48,512]{1,0:T(8,128)S(1)}, u32[]{:S(2)}, u32[]{:S(2)}) collective-permute-start(f32[48,512]{1,0:T(8,128)S(1)} %get-tuple-element.23), channel_id=1, source_target_pairs={{0,6},{1,7},{2,4},{3,5},{4,2},{5,3},{6,0},{7,1},{8,14},{9,15},{10,... | collective-permute-start | bytes 294920 | tf_op jit(solution)/shard_map/ppermute | solution.py:352
  5.9 5.2 %collective-permute-start.2 = (f32[48,512]{1,0:T(8,128)S(1)}, f32[48,512]{1,0:T(8,128)S(1)}, u32[]{:S(2)}, u32[]{:S(2)}) collective-permute-start(f32[48,512]{1,0:T(8,128)S(1)} %get-tuple-element.24), channel_id=1, source_target_pairs={{0,2},{1,5},{2,0},{3,7},{4,6},{5,1},{6,4},{7,3},{8,10},{9,13},{10,... | collective-permute-start | bytes 294920 | tf_op jit(solution)/shard_map/ppermute | solution.py:352
  6.4 4.7 %collective-permute-start.3 = (f32[48,512]{1,0:T(8,128)S(1)}, f32[48,512]{1,0:T(8,128)S(1)}, u32[]{:S(2)}, u32[]{:S(2)}) collective-permute-start(f32[48,512]{1,0:T(8,128)S(1)} %get-tuple-element.25), channel_id=1, source_target_pairs={{0,4},{1,3},{2,6},{3,1},{4,0},{5,7},{6,2},{7,5},{8,12},{9,11},{10,... | collective-permute-start | bytes 294920 | tf_op jit(solution)/shard_map/ppermute | solution.py:352
  6.5 5.1 %collective-permute-start.7 = (f32[8,512]{1,0:T(8,128)S(1)}, f32[8,512]{1,0:T(8,128)S(1)}, u32[]{:S(2)}, u32[]{:S(2)}) collective-permute-start(f32[8,512]{1,0:T(8,128)S(1)} %get-tuple-element.26), channel_id=1, source_target_pairs={{2,3},{3,2},{4,5},{5,4},{7,8},{8,7},{6,14},{14,6},{10,11},{11,10},... | collective-permute-start | bytes 49160 | tf_op jit(solution)/shard_map/ppermute | solution.py:376
  6.5 5.3 %collective-permute-start = (f32[88,512]{1,0:T(8,128)S(1)}, f32[88,512]{1,0:T(8,128)S(1)}, u32[]{:S(2)}, u32[]{:S(2)}) collective-permute-start(f32[88,512]{1,0:T(8,128)S(1)} %get-tuple-element.20.own_home.refs_2_), channel_id=1, source_target_pairs={{0,1},{1,0},{2,3},{3,2},{4,5},{5,4},{6,7},{7,6},{8,9},{9,8},{10,11... | collective-permute-start | bytes 540680 | tf_op jit(solution)/shard_map/ppermute | solution.py:349
  9.1 3.9 %collective-permute-start.4 = (f32[48,512]{1,0:T(8,128)S(1)}, f32[48,512]{1,0:T(8,128)S(1)}, u32[]{:S(2)}, u32[]{:S(2)}) collective-permute-start(f32[48,512]{1,0:T(8,128)S(1)} %collective-permute-done.1.refs_3_), channel_id=1, source_target_pairs={{0,1},{1,0},{2,3},{3,2},{4,5},{5,4},{6,7},{7,6},{8,9},{9,8},{10,11... | collective-permute-start | bytes 294920 | tf_op jit(solution)/shard_map/ppermute | solution.py:349
  11.1 1.9 %collective-permute-start.5 = (f32[48,512]{1,0:T(8,128)S(1)}, f32[48,512]{1,0:T(8,128)S(1)}, u32[]{:S(2)}, u32[]{:S(2)}) collective-permute-start(f32[48,512]{1,0:T(8,128)S(1)} %collective-permute-done.2.refs_4_), channel_id=1, source_target_pairs={{0,1},{1,0},{2,3},{3,2},{4,5},{5,4},{6,7},{7,6},{8,9},{9,8},{10,11... | collective-permute-start | bytes 294920 | tf_op jit(solution)/shard_map/ppermute | solution.py:349
  11.1 1.9 %collective-permute-start.6 = (f32[48,512]{1,0:T(8,128)S(1)}, f32[48,512]{1,0:T(8,128)S(1)}, u32[]{:S(2)}, u32[]{:S(2)}) collective-permute-start(f32[48,512]{1,0:T(8,128)S(1)} %collective-permute-done.3.refs_5_), channel_id=1, source_target_pairs={{0,1},{1,0},{2,3},{3,2},{4,5},{5,4},{6,7},{7,6},{8,9},{9,8},{10,11... | collective-permute-start | bytes 294920 | tf_op jit(solution)/shard_map/ppermute | solution.py:349
  11.6 1.3 %copy-start = (f32[32,512]{1,0:T(8,128)S(1)}, f32[32,512]{1,0:T(8,128)}, u32[]{:S(2)}) copy-start(f32[32,512]{1,0:T(8,128)} %refs_12_.1) | copy-start | bytes 196612
  11.7 1.3 %collective-permute-start.8 = (f32[32,512]{1,0:T(8,128)S(1)}, f32[32,512]{1,0:T(8,128)S(1)}, u32[]{:S(2)}, u32[]{:S(2)}) collective-permute-start(f32[32,512]{1,0:T(8,128)S(1)} %pad_maximum_fusion), channel_id=1, source_target_pairs={{0,1},{1,0},{2,3},{3,2},{4,5},{5,4},{6,7},{7,6},{8,9},{9,8},{10,11... | collective-permute-start | bytes 196616 | tf_op jit(solution)/shard_map/ppermute | solution.py:349
  13.7 5.3 %collective-permute-start.9 = (f32[17,8,128]{2,1,0:T(8,128)S(1)}, f32[17,8,128]{2,1,0:T(8,128)S(1)}, u32[]{:S(2)}, u32[]{:S(2)}) collective-permute-start(f32[17,8,128]{2,1,0:T(8,128)S(1)} %get-tuple-element.28), channel_id=1, source_target_pairs={{0,6},{1,7},{2,4},{3,5},{4,2},{5,3},{6,0},{7,1},{8,14},{9,15},{10,... | collective-permute-start | bytes 208904 | tf_op jit(solution)/shard_map/ppermute | solution.py:352
  15.3 4.9 %collective-permute-start.10 = (f32[17,8,128]{2,1,0:T(8,128)S(1)}, f32[17,8,128]{2,1,0:T(8,128)S(1)}, u32[]{:S(2)}, u32[]{:S(2)}) collective-permute-start(f32[17,8,128]{2,1,0:T(8,128)S(1)} %get-tuple-element.29), channel_id=1, source_target_pairs={{0,2},{1,5},{2,0},{3,7},{4,6},{5,1},{6,4},{7,3},{8,10},{9,13},{10,... | collective-permute-start | bytes 208904 | tf_op jit(solution)/shard_map/ppermute | solution.py:352
  16.2 4.3 %collective-permute-start.11 = (f32[17,8,128]{2,1,0:T(8,128)S(1)}, f32[17,8,128]{2,1,0:T(8,128)S(1)}, u32[]{:S(2)}, u32[]{:S(2)}) collective-permute-start(f32[17,8,128]{2,1,0:T(8,128)S(1)} %get-tuple-element.30), channel_id=1, source_target_pairs={{0,4},{1,3},{2,6},{3,1},{4,0},{5,7},{6,2},{7,5},{8,12},{9,11},{10,... | collective-permute-start | bytes 208904 | tf_op jit(solution)/shard_map/ppermute | solution.py:352

commit v7 on v6

--- a/solution.py
+++ b/solution.py
@@ -9,6 +9,8 @@
 
 BR = 4
 CAP = 2
+SWAP1, CROSS1 = 1, 0
+SWAP2, CROSS2 = 0, 1
 ZR = 8
 HALF_DT = 0.075
 NF = 5
@@ -45,13 +47,17 @@
     return turn(jnp.where(sub == 0, after, x), 7) - turn(jnp.where(sub == 7, before, x), 1)
 
 
+def target(path, core):
+    return 2 * reached(path, core) + (1 if CROSS2 and path[0] else 0)
+
+
 def where_am_i():
     return lax.axis_index("grp"), lax.axis_index("bis")
 
 
-def routes(chips):
+def routes(chips, swapped):
     bits = chips.bit_length() - 1
-    half = bits // 2 if bits % 2 == 0 else 0
+    half = bits // 2 if swapped and bits % 2 == 0 else 0
     swap = lambda mask: (mask << half | mask >> bits - half) & chips - 1
     masks = sorted(range(1, chips), key=lambda mask: (-mask.bit_count(), mask))
     return [(0, 0)] + [(mask, swap(mask)) for mask in masks]
@@ -82,7 +88,7 @@
     chip, core = me // 2, me % 2
     sub = sublane(width)
     first = me == 0
-    goals = [chip ^ reached(route, core) for route in routes(chips)]
+    goals = [chip ^ reached(route, core) for route in routes(chips, SWAP1)]
     copies[0].wait()
 
     def tile_of(field, block):
@@ -135,12 +141,10 @@
         for block in range(n):
             same = jnp.logical_and(owner == owner[block : block + 1, :], line_id > block)
             rank = jnp.where(same, rank + 1, rank)
-        mine = (owner & 1) == core
-        place = ((owner >> 1) ^ chip) * (2 * CAP) + (device * CAP) + rank
-        slots.append(jnp.where(mine, place, -1))
+        slots.append((owner ^ me) * (2 * CAP) + (device * CAP) + rank)
         code[device] = slots[device]
-    for index, path in enumerate(routes(chips)):
-        want = sub + reached(path, core) * (2 * CAP)
+    for index, path in enumerate(routes(chips, SWAP2)):
+        want = sub + target(path, core) * (2 * CAP)
         tile = jnp.full((8, 128), -1, jnp.int32)
         for device, info in enumerate(both):
             for block in range(n):
@@ -149,6 +153,27 @@
         tags[index] = tile.astype(jnp.float32)
 
 
+def pack_partials(n, paths, core, code, tags, parts, sends):
+    width = parts.shape[3]
+    pieces = width // 128
+    lanes = [slice(piece * 128, piece * 128 + 128) for piece in range(pieces)]
+    for device in range(2):
+        wants = [target(path, core) * (2 * CAP) + device * CAP + again for path in paths for again in range(CAP)]
+        found = [[jnp.zeros((8, 128), jnp.float32)] * pieces for _ in wants]
+        for block in range(n):
+            taken = jnp.broadcast_to(code[device, block : block + 1, :], (8, 128))
+            tile = [parts[device, block, :, lane] for lane in lanes]
+            for index, want in enumerate(wants):
+                hit = taken == want
+                found[index] = [jnp.where(hit, new, old) for new, old in zip(tile, found[index])]
+        for index in range(len(wants)):
+            rank = device * CAP + index % CAP
+            for piece in range(pieces):
+                sends[index // CAP][rank * pieces + piece] = found[index][piece]
+    for send, tag in zip(sends, tags):
+        send[2 * CAP * pieces] = tag[...]
+
+
 def step_kernel(n, *refs):
     chips = n // 2
     refs = list(refs)
@@ -157,8 +182,9 @@
     mine, theirs = take(chips), take(chips)
     across, across_sib, sweep = take(3)
     nxt_prs, nxt_u, nxt_v, coef = take(4)
-    sends = take(chips)
-    fld, prs, vols, halo, parts = take(5)
+    (parts,) = take(1)
+    sends = take(chips - 1)
+    fld, prs, vols, halo = take(4)
     grp, me = where_am_i()
     chip, core = me // 2, me % 2
     width = sweep.shape[1]
@@ -172,10 +198,11 @@
     def pair(own, sib):
         return jnp.where(is_low, own, sib), jnp.where(is_low, sib, own)
 
-    paths = routes(chips)
-    for index, path in enumerate(paths):
+    for index, path in enumerate(routes(chips, SWAP1)):
         source = chip ^ reached(path, core)
-        own, sib = mine[index], theirs[paths.index((path[1], path[0]))]
+        own, sib = mine[index], theirs[routes(chips, SWAP1).index((path[1], path[0]))]
+        if CROSS1 and path[0]:
+            own, sib = sib, own
         for field in range(NF):
             span = pl.ds(8 * field, 8)
             even, odd = pair(own[span, :], sib[span, :])
@@ -252,27 +279,13 @@
     for device in range(2):
         lax.fori_loop(0, chips, lambda index, _, device=device: (second(device, index), 0)[1], 0, unroll=n <= 8)
 
-    pieces = width // 128
-    for index, (send, path) in enumerate(zip(sends, paths)):
-        base = reached(path, core) * (2 * CAP)
-        for device in range(2):
-            for turn_of in range(CAP):
-                rank = device * CAP + turn_of
-                found = [jnp.zeros((8, 128), jnp.float32)] * pieces
-                for block in range(n):
-                    hit = jnp.broadcast_to(code[device, block : block + 1, :], (8, 128)) == base + rank
-                    found = [
-                        jnp.where(hit, parts[device, block, :, piece * 128 : piece * 128 + 128], found[piece])
-                        for piece in range(pieces)
-                    ]
-                for piece in range(pieces):
-                    send[rank * pieces + piece] = found[piece]
-        send[2 * CAP * pieces] = tags[index]
-
-
-def velocity_kernel(n, prs, velu, velv, coef, vel):
+    pack_partials(n, routes(chips, SWAP2)[1:], core, code, [tags.at[1 + i] for i in range(chips - 1)], parts, sends)
+
+
+def side_kernel(n, prs, velu, velv, coef, parts, code, tags, vel, home):
     chips = n // 2
     _, me = where_am_i()
+    pack_partials(n, routes(chips, SWAP2)[:1], me % 2, code, [tags.at[0]], parts, [home])
 
     def one(index, _):
         tile = 1 + me % 2 * chips + index
@@ -285,16 +298,21 @@
     lax.fori_loop(0, chips, one, 0, unroll=n <= 8)
 
 
-def land_kernel(n, *refs):
-    chips = n // 2
-    arrived = refs[:chips]
-    mass_out, energy_out, mass, energy, sems = refs[chips:]
-    parts = mass.shape[1] // 128
+def land_kernel(n, final, *refs):
+    chips = n // 2
+    refs = list(refs)
+    if final:
+        mass_out, energy_out, sums_out, sems = refs[-4:]
+        sums_in, arrived = refs[0], refs[1:-4]
+    else:
+        sums_in, arrived, sums_out = None, refs[:-1], refs[-1]
+    parts = sums_out.shape[2] // 128
     sub = sublane(128)
 
-    def send(source, target, which, index):
+    def send(which, index):
         span = pl.ds(pl.multiple_of(index * 8, 8), 8)
-        return pltpu.make_async_copy(source.at[span, :], target.at[span, :], sems.at[which, index])
+        target_ref = energy_out if which else mass_out
+        return pltpu.make_async_copy(sums_out.at[which, span, :], target_ref.at[span, :], sems.at[which, index])
 
     def tile_pair(index, _):
         span = pl.ds(pl.multiple_of(index * 8, 8), 8)
@@ -310,16 +328,21 @@
         for part in range(parts):
             cols = slice(part * 128, part * 128 + 128)
             even, odd = sums[0][part], sums[1][part]
-            mass[span, cols] = jnp.where(sub < 4, even, turn(odd, 4))
-            energy[span, cols] = jnp.where(sub < 4, turn(even, 4), odd)
-        send(mass, mass_out, 0, index).start()
-        send(energy, energy_out, 1, index).start()
+            mass, energy = jnp.where(sub < 4, even, turn(odd, 4)), jnp.where(sub < 4, turn(even, 4), odd)
+            if final:
+                mass, energy = mass + sums_in[0, span, cols], energy + sums_in[1, span, cols]
+            sums_out[0, span, cols] = mass
+            sums_out[1, span, cols] = energy
+        if final:
+            send(0, index).start()
+            send(1, index).start()
         return 0
 
     lax.fori_loop(0, chips, tile_pair, 0, unroll=n <= 8)
-    for index in range(chips):
-        send(mass, mass_out, 0, index).wait()
-        send(energy, energy_out, 1, index).wait()
+    if final:
+        for index in range(chips):
+            send(0, index).wait()
+            send(1, index).wait()
 
 
 def across_links(groups, n):
@@ -348,10 +371,11 @@
     def to_sibling(x):
         return lax.ppermute(x, "bis", [(i, i ^ 1) for i in range(n)])
 
-    def to_chip(x, path):
-        return lax.ppermute(x, "bis", [(i, i ^ 2 * path[i % 2]) for i in range(n)]) if path[0] else x
-
-    paths = routes(chips)
+    def to_chip(x, path, cross):
+        links = [(i, i ^ 2 * path[i % 2] ^ cross) for i in range(n)]
+        return lax.ppermute(x, "bis", links) if path[0] else x
+
+    paths = routes(chips, SWAP1)
 
     owner = owner.reshape(n)
     extra = -(-(rows + n) // 8) * 8
@@ -374,7 +398,7 @@
         name="pack",
     )(*[pltpu.with_memory_space_constraint(x, pltpu.HBM) for x in (order.reshape(n), owner, slot_target, sweep, state)])
     across = lax.ppermute(packed[chips], ("grp", "bis"), across_links(groups, n))
-    mine = [to_chip(x, path) for x, path in zip(packed, paths)]
+    mine = [to_chip(x, path, CROSS1) for x, path in zip(packed, paths)]
     theirs = [to_sibling(x) for x in mine]
     across_sib = to_sibling(jnp.concatenate([across] + [x[0:8] for x in mine[1:]]))
 
@@ -395,7 +419,8 @@
     out = pl.pallas_call(
         functools.partial(step_kernel, n),
         out_shape=[jax.ShapeDtypeStruct((stack, width), f32)] * 4
-        + [jax.ShapeDtypeStruct(send_shape, f32)] * chips,
+        + [jax.ShapeDtypeStruct((2, n, 8, width), f32)]
+        + [jax.ShapeDtypeStruct(send_shape, f32)] * (chips - 1),
         in_specs=[VMEM] * (2 * chips + 5),
         out_specs=[VMEM] * (chips + 4),
         scratch_shapes=[
@@ -403,33 +428,38 @@
             pltpu.VMEM((stack, width), f32),
             pltpu.VMEM((2, stack, width), f32),
             pltpu.VMEM((2, chips, 8, width), f32),
-            pltpu.VMEM((2, n, 8, width), f32),
         ],
         compiler_params=params,
         name="substeps",
     )(code, tags, *mine, *theirs, across, across_sib, sweep)
-    arrived = [to_chip(x, path) for x, path in zip(out[4:], paths)]
-    vel = pl.pallas_call(
-        functools.partial(velocity_kernel, n),
+    arrived = [to_chip(x, path, CROSS2) for x, path in zip(out[5:], routes(chips, SWAP2)[1:])]
+    vel, home = pl.pallas_call(
+        functools.partial(side_kernel, n),
+        out_shape=[jax.ShapeDtypeStruct((2, rows, width), f32), jax.ShapeDtypeStruct(send_shape, f32)],
+        in_specs=[VMEM] * 7,
+        out_specs=[VMEM] * 2,
+        compiler_params=params,
+        name="velocities",
+    )(*out[:5], code, tags)
+    arrived = [home] + arrived
+    early = 2
+    sums = pl.pallas_call(
+        functools.partial(land_kernel, n, False),
         out_shape=jax.ShapeDtypeStruct((2, rows, width), f32),
-        in_specs=[VMEM] * 4,
+        in_specs=[VMEM] * early,
         out_specs=VMEM,
         compiler_params=params,
-        name="velocities",
-    )(*out[:4])
+        name="sums",
+    )(*arrived[:early])
     mass, energy = pl.pallas_call(
-        functools.partial(land_kernel, n),
+        functools.partial(land_kernel, n, True),
         out_shape=[jax.ShapeDtypeStruct((rows, width), f32)] * 2,
-        in_specs=[VMEM] * chips,
+        in_specs=[VMEM] * (1 + chips - early),
         out_specs=[pl.BlockSpec(memory_space=pl.ANY)] * 2,
-        scratch_shapes=[
-            pltpu.VMEM((rows, width), f32),
-            pltpu.VMEM((rows, width), f32),
-            pltpu.SemaphoreType.DMA((2, chips)),
-        ],
+        scratch_shapes=[pltpu.VMEM((2, rows, width), f32), pltpu.SemaphoreType.DMA((2, chips))],
         compiler_params=params,
         name="land",
-    )(*arrived)
+    )(sums, *arrived[early:])
     return mass, energy, vel
 
 

time: 21.6 us -> 21.2 us (0.981)
  starting transfers between devices: 9.31 us -> 8.79 us
  waiting for transfers between devices: 7.74 us -> 7.96 us
    ppermute x6, starting transfers between devices: 8.16 us -> 7.64 us  [to_chip(): return lax.ppermute(x, 'bis', links) if path[0] else x]
    ppermute x6, waiting for transfers between devices: 6.62 us -> 6.83 us  [to_chip(): return lax.ppermute(x, 'bis', links) if path[0] else x]
    pallas_call x2 -> x3, Pallas kernels: 1.64 us -> 1.62 us  [the longest x1 0.77 us: shards(): pl.pallas_call(functools.partial(land_kernel, n, True), out_shape=[jax.Sh...]
where the time goes in v7:
time: 21.2 us; the launch traced here: 21.1 us
  starting transfers between devices  8.79 us (41%)
  waiting for transfers between devices  7.96 us (38%)
  Pallas kernels  3.6 us (17%)
  between operations  0.7 us (3%)
    ppermute x6, starting transfers between devices, to_chip(): return lax.ppermute(x, 'bis', links) if path[0] else x  7.64 us
    ppermute x6, waiting for transfers between devices, to_chip(): return lax.ppermute(x, 'bis', links) if path[0] else x  6.83 us
    pallas_call x1, Pallas kernels, shards(): pl.pallas_call(functools.partial(pack_kernel, n), out_shape=[jax.ShapeDty...  1.28 us
    ppermute x5, starting transfers between devices, to_sibling(): return lax.ppermute(x, 'bis', [(i, i ^ 1) for i in range(n)])  1.15 us
    ppermute x5, waiting for transfers between devices, to_sibling(): return lax.ppermute(x, 'bis', [(i, i ^ 1) for i in range(n)])  1.12 us
    pallas_call x1, Pallas kernels, shards(): pl.pallas_call(functools.partial(land_kernel, n, True), out_shape=[jax.Sh...  0.77 us
    pallas_call x1, Pallas kernels, shards(): pl.pallas_call(functools.partial(side_kernel, n), out_shape=[jax.ShapeDty...  0.76 us
    pallas_call x1, Pallas kernels, shards(): pl.pallas_call(functools.partial(step_kernel, n), out_shape=[jax.ShapeDty...  0.64 us
  transfers between devices with their start and end apart: 12, of which 6 were waited for; matrix products, arithmetic and copies ran while one was open for 0% of the time, Pallas kernels for 4%

profile of v7, /device:TPU:0, one launch (start us, length us, event | category | flops | bytes accessed | tf_op | source)
XLA Modules:
  0.0 21.1 jit_solution(3887685478635983685)
XLA Ops:
  0.6 1.3 %pack.1 = (f32[88,512]{1,0:T(8,128)S(1)}, f32[48,512]{1,0:T(8,128)S(1)}, f32[48,512]{1,0:T(8,128)S(1)}, f32[48,512]{1,0:T(8,128)S(1)}, f32[8,512]{1,0:T(8,128)S(1)}) custom-call(s32[8]{0:T(128)} %bitcast.2, s32[8]{0:T(128)} %bitcast.3, s32[8]{0:T(128)} %refs_2_.1, f32[32,512]{1,0:T(8,128)} %refs_12_.1, f32[5,32,512]{2,1,0:T(8,128)} %refs_4_.1), custom_call_target="tpu_custom_call" | custom-call | tf_op jit(solution)/shard_map/pack/pallas_call | solution.py:382
  1.9 4.0 %collective-permute-start.1 = (f32[48,512]{1,0:T(8,128)S(1)}, f32[48,512]{1,0:T(8,128)S(1)}, u32[]{:S(2)}, u32[]{:S(2)}) collective-permute-start(f32[48,512]{1,0:T(8,128)S(1)} %get-tuple-element.25), channel_id=1, source_target_pairs={{0,6},{1,7},{2,4},{3,5},{4,2},{5,3},{6,0},{7,1},{8,14},{9,15},{10,... | collective-permute-start | bytes 294920 | tf_op jit(solution)/shard_map/ppermute | solution.py:376
  5.9 0.5 %collective-permute-start.2 = (f32[48,512]{1,0:T(8,128)S(1)}, f32[48,512]{1,0:T(8,128)S(1)}, u32[]{:S(2)}, u32[]{:S(2)}) collective-permute-start(f32[48,512]{1,0:T(8,128)S(1)} %get-tuple-element.26), channel_id=1, source_target_pairs={{0,2},{1,5},{2,0},{3,7},{4,6},{5,1},{6,4},{7,3},{8,10},{9,13},{10,... | collective-permute-start | bytes 294920 | tf_op jit(solution)/shard_map/ppermute | solution.py:376
  6.4 0.1 collective-permute-start.3
  6.5 0.0 collective-permute-start.7
  6.5 0.5 %collective-permute-start = (f32[88,512]{1,0:T(8,128)S(1)}, f32[88,512]{1,0:T(8,128)S(1)}, u32[]{:S(2)}, u32[]{:S(2)}) collective-permute-start(f32[88,512]{1,0:T(8,128)S(1)} %get-tuple-element.22.own_home.refs_2_), channel_id=1, source_target_pairs={{0,1},{1,0},{2,3},{3,2},{4,5},{5,4},{6,7},{7,6},{8,9},{9,8},{10,11... | collective-permute-start | bytes 540680 | tf_op jit(solution)/shard_map/ppermute | solution.py:372
  7.0 2.0 %collective-permute-done.1.refs_3_ = f32[48,512]{1,0:T(8,128)S(1)} collective-permute-done((f32[48,512]{1,0:T(8,128)S(1)}, f32[48,512]{1,0:T(8,128)S(1)}, u32[]{:S(2)}, u32[]{:S(2)}) %collective-permute-start.1) | collective-permute-done | bytes 98336 | tf_op jit(solution)/shard_map/ppermute | solution.py:376
  9.1 0.0 collective-permute-start.4
  9.1 2.0 %collective-permute-done.2.refs_4_ = f32[48,512]{1,0:T(8,128)S(1)} collective-permute-done((f32[48,512]{1,0:T(8,128)S(1)}, f32[48,512]{1,0:T(8,128)S(1)}, u32[]{:S(2)}, u32[]{:S(2)}) %collective-permute-start.2) | collective-permute-done | bytes 98336 | tf_op jit(solution)/shard_map/ppermute | solution.py:376
  11.1 0.0 collective-permute-start.5
  11.1 0.0 collective-permute-done.3.refs_5_
  11.1 0.5 %collective-permute-start.6 = (f32[48,512]{1,0:T(8,128)S(1)}, f32[48,512]{1,0:T(8,128)S(1)}, u32[]{:S(2)}, u32[]{:S(2)}) collective-permute-start(f32[48,512]{1,0:T(8,128)S(1)} %collective-permute-done.3.refs_5_), channel_id=1, source_target_pairs={{0,1},{1,0},{2,3},{3,2},{4,5},{5,4},{6,7},{7,6},{8,9},{9,8},{10,11... | collective-permute-start | bytes 294920 | tf_op jit(solution)/shard_map/ppermute | solution.py:372
  11.6 0.0 collective-permute-done.7.refs_10_
  11.6 0.0 copy-start
  11.7 0.1 collective-permute-start.8
  11.8 0.0 collective-permute-done.sib_home.refs_6_
  11.8 0.1 tags.1
  11.9 1.1 %collective-permute-done.8.refs_11_ = f32[32,512]{1,0:T(8,128)S(1)} collective-permute-done((f32[32,512]{1,0:T(8,128)S(1)}, f32[32,512]{1,0:T(8,128)S(1)}, u32[]{:S(2)}, u32[]{:S(2)}) %collective-permute-start.8) | collective-permute-done | bytes 65568 | tf_op jit(solution)/shard_map/ppermute | solution.py:372
  13.0 0.0 collective-permute-done.4.refs_7_
  13.0 0.0 collective-permute-done.5.refs_8_
  13.0 0.0 collective-permute-done.6.refs_9_
  13.0 0.0 copy-done
  13.0 0.6 %substeps.1 = (f32[80,512]{1,0:T(8,128)S(1)}, f32[80,512]{1,0:T(8,128)S(1)}, f32[80,512]{1,0:T(8,128)S(1)}, f32[80,512]{1,0:T(8,128)S(1)}, f32[2,8,8,512]{3,2,1,...) custom-call(s32[2,8,128]{2,1,0:T(8,128)S(1)} %get-tuple-element.23.refs_0_.code, ...), custom_call_target="tpu_custom_call" | custom-call | tf_op jit(solution)/shard_map/substeps/pallas_call | solution.py:419
  13.6 1.5 %collective-permute-start.9 = (f32[17,8,128]{2,1,0:T(8,128)S(1)}, f32[17,8,128]{2,1,0:T(8,128)S(1)}, u32[]{:S(2)}, u32[]{:S(2)}) collective-permute-start(f32[17,8,128]{2,1,0:T(8,128)S(1)} %get-tuple-element.35), channel_id=1, source_target_pairs={{0,7},{1,6},{2,5},{3,4},{4,3},{5,2},{6,1},{7,0},{8,15},{9,14},{10,... | collective-permute-start | bytes 208904 | tf_op jit(solution)/shard_map/ppermute | solution.py:376
  15.2 0.7 %collective-permute-start.10 = (f32[17,8,128]{2,1,0:T(8,128)S(1)}, f32[17,8,128]{2,1,0:T(8,128)S(1)}, u32[]{:S(2)}, u32[]{:S(2)}) collective-permute-start(f32[17,8,128]{2,1,0:T(8,128)S(1)} %get-tuple-element.36), channel_id=1, source_target_pairs={{0,3},{1,2},{2,1},{3,0},{4,7},{5,6},{6,5},{7,4},{8,11},{9,10},{10,... | collective-permute-start | bytes 208904 | tf_op jit(solution)/shard_map/ppermute | solution.py:376
  15.9 0.8 %collective-permute-start.11 = (f32[17,8,128]{2,1,0:T(8,128)S(1)}, f32[17,8,128]{2,1,0:T(8,128)S(1)}, u32[]{:S(2)}, u32[]{:S(2)}) collective-permute-start(f32[17,8,128]{2,1,0:T(8,128)S(1)} %get-tuple-element.37), channel_id=1, source_target_pairs={{0,5},{1,4},{2,7},{3,6},{4,1},{5,0},{6,3},{7,2},{8,13},{9,12},{10,... | collective-permute-start | bytes 208904 | tf_op jit(solution)/shard_map/ppermute | solution.py:376
  16.7 0.8 %velocities.1 = (f32[2,32,512]{2,1,0:T(8,128)}, f32[17,8,128]{2,1,0:T(8,128)S(1)}) custom-call(f32[80,512]{1,0:T(8,128)S(1)} %get-tuple-element.29.prs, f32[80,512]{1,0:T(8,128)S(1)} %get-tuple-element.30.velu, f32[80,512]{1,0:T(8,128)S(1)} %get-tuple-element.31.velv, f32[80,512]{1,0:T(8,128)S(1)} %get-tuple-element.32.coef, ...), custom_call_target="tpu_custom_call" | custom-call | tf_op jit(solution)/shard_map/velocities/pallas_call | solution.py:436
  17.4 1.3 %collective-permute-done.9.refs_1_ = f32[17,8,128]{2,1,0:T(8,128)S(1)} collective-permute-done((f32[17,8,128]{2,1,0:T(8,128)S(1)}, f32[17,8,128]{2,1,0:T(8,128)S(1)}, u32[]{:S(2)}, u32[]{:S(2)}) %collective-permute-start.9) | collective-permute-done | bytes 69664 | tf_op jit(solution)/shard_map/ppermute | solution.py:376
  18.8 0.1 sums.1.refs_0_
  18.8 0.8 %collective-permute-done.10.refs_1_ = f32[17,8,128]{2,1,0:T(8,128)S(1)} collective-permute-done((f32[17,8,128]{2,1,0:T(8,128)S(1)}, f32[17,8,128]{2,1,0:T(8,128)S(1)}, u32[]{:S(2)}, u32[]{:S(2)}) %collective-permute-start.10) | collective-permute-done | bytes 69664 | tf_op jit(solution)/shard_map/ppermute | solution.py:376
  19.7 0.6 %collective-permute-done.11.refs_2_ = f32[17,8,128]{2,1,0:T(8,128)S(1)} collective-permute-done((f32[17,8,128]{2,1,0:T(8,128)S(1)}, f32[17,8,128]{2,1,0:T(8,128)S(1)}, u32[]{:S(2)}, u32[]{:S(2)}) %collective-permute-start.11) | collective-permute-done | bytes 69664 | tf_op jit(solution)/shard_map/ppermute | solution.py:376
  20.3 0.8 %land.1 = (f32[32,512]{1,0:T(8,128)}, f32[32,512]{1,0:T(8,128)}) custom-call(f32[2,32,512]{2,1,0:T(8,128)S(1)} %sums.1.refs_0_, f32[17,8,128]{2,1,0:T(8,128)S(1)} %collective-permute-done.10.refs_1_, f32[17,8,128]{2,1,0:T(8,128)S(1)} %collective-permute-done.11.refs_2_), custom_call_target="tpu_custom_call" | custom-call | tf_op jit(solution)/shard_map/land/pallas_call | solution.py:454
  (4 shorter events, 0.0 us)
Async XLA Ops:
  1.9 7.1 %collective-permute-start.1 = (f32[48,512]{1,0:T(8,128)S(1)}, f32[48,512]{1,0:T(8,128)S(1)}, u32[]{:S(2)}, u32[]{:S(2)}) collective-permute-start(f32[48,512]{1,0:T(8,128)S(1)} %get-tuple-element.25), channel_id=1, source_target_pairs={{0,6},{1,7},{2,4},{3,5},{4,2},{5,3},{6,0},{7,1},{8,14},{9,15},{10,... | collective-permute-start | bytes 294920 | tf_op jit(solution)/shard_map/ppermute | solution.py:376
  5.9 5.2 %collective-permute-start.2 = (f32[48,512]{1,0:T(8,128)S(1)}, f32[48,512]{1,0:T(8,128)S(1)}, u32[]{:S(2)}, u32[]{:S(2)}) collective-permute-start(f32[48,512]{1,0:T(8,128)S(1)} %get-tuple-element.26), channel_id=1, source_target_pairs={{0,2},{1,5},{2,0},{3,7},{4,6},{5,1},{6,4},{7,3},{8,10},{9,13},{10,... | collective-permute-start | bytes 294920 | tf_op jit(solution)/shard_map/ppermute | solution.py:376
  6.4 4.7 %collective-permute-start.3 = (f32[48,512]{1,0:T(8,128)S(1)}, f32[48,512]{1,0:T(8,128)S(1)}, u32[]{:S(2)}, u32[]{:S(2)}) collective-permute-start(f32[48,512]{1,0:T(8,128)S(1)} %get-tuple-element.27), channel_id=1, source_target_pairs={{0,4},{1,3},{2,6},{3,1},{4,0},{5,7},{6,2},{7,5},{8,12},{9,11},{10,... | collective-permute-start | bytes 294920 | tf_op jit(solution)/shard_map/ppermute | solution.py:376
  6.5 5.1 %collective-permute-start.7 = (f32[8,512]{1,0:T(8,128)S(1)}, f32[8,512]{1,0:T(8,128)S(1)}, u32[]{:S(2)}, u32[]{:S(2)}) collective-permute-start(f32[8,512]{1,0:T(8,128)S(1)} %get-tuple-element.28), channel_id=1, source_target_pairs={{2,3},{3,2},{4,5},{5,4},{7,8},{8,7},{6,14},{14,6},{10,11},{11,10},... | collective-permute-start | bytes 49160 | tf_op jit(solution)/shard_map/ppermute | solution.py:400
  6.5 5.3 %collective-permute-start = (f32[88,512]{1,0:T(8,128)S(1)}, f32[88,512]{1,0:T(8,128)S(1)}, u32[]{:S(2)}, u32[]{:S(2)}) collective-permute-start(f32[88,512]{1,0:T(8,128)S(1)} %get-tuple-element.22.own_home.refs_2_), channel_id=1, source_target_pairs={{0,1},{1,0},{2,3},{3,2},{4,5},{5,4},{6,7},{7,6},{8,9},{9,8},{10,11... | collective-permute-start | bytes 540680 | tf_op jit(solution)/shard_map/ppermute | solution.py:372
  9.1 3.9 %collective-permute-start.4 = (f32[48,512]{1,0:T(8,128)S(1)}, f32[48,512]{1,0:T(8,128)S(1)}, u32[]{:S(2)}, u32[]{:S(2)}) collective-permute-start(f32[48,512]{1,0:T(8,128)S(1)} %collective-permute-done.1.refs_3_), channel_id=1, source_target_pairs={{0,1},{1,0},{2,3},{3,2},{4,5},{5,4},{6,7},{7,6},{8,9},{9,8},{10,11... | collective-permute-start | bytes 294920 | tf_op jit(solution)/shard_map/ppermute | solution.py:372
  11.1 1.9 %collective-permute-start.5 = (f32[48,512]{1,0:T(8,128)S(1)}, f32[48,512]{1,0:T(8,128)S(1)}, u32[]{:S(2)}, u32[]{:S(2)}) collective-permute-start(f32[48,512]{1,0:T(8,128)S(1)} %collective-permute-done.2.refs_4_), channel_id=1, source_target_pairs={{0,1},{1,0},{2,3},{3,2},{4,5},{5,4},{6,7},{7,6},{8,9},{9,8},{10,11... | collective-permute-start | bytes 294920 | tf_op jit(solution)/shard_map/ppermute | solution.py:372
  11.1 1.9 %collective-permute-start.6 = (f32[48,512]{1,0:T(8,128)S(1)}, f32[48,512]{1,0:T(8,128)S(1)}, u32[]{:S(2)}, u32[]{:S(2)}) collective-permute-start(f32[48,512]{1,0:T(8,128)S(1)} %collective-permute-done.3.refs_5_), channel_id=1, source_target_pairs={{0,1},{1,0},{2,3},{3,2},{4,5},{5,4},{6,7},{7,6},{8,9},{9,8},{10,11... | collective-permute-start | bytes 294920 | tf_op jit(solution)/shard_map/ppermute | solution.py:372
  11.6 1.3 %copy-start = (f32[32,512]{1,0:T(8,128)S(1)}, f32[32,512]{1,0:T(8,128)}, u32[]{:S(2)}) copy-start(f32[32,512]{1,0:T(8,128)} %refs_12_.1) | copy-start | bytes 196612
  11.7 1.3 %collective-permute-start.8 = (f32[32,512]{1,0:T(8,128)S(1)}, f32[32,512]{1,0:T(8,128)S(1)}, u32[]{:S(2)}, u32[]{:S(2)}) collective-permute-start(f32[32,512]{1,0:T(8,128)S(1)} %pad_maximum_fusion), channel_id=1, source_target_pairs={{0,1},{1,0},{2,3},{3,2},{4,5},{5,4},{6,7},{7,6},{8,9},{9,8},{10,11... | collective-permute-start | bytes 196616 | tf_op jit(solution)/shard_map/ppermute | solution.py:372
  13.6 5.1 %collective-permute-start.9 = (f32[17,8,128]{2,1,0:T(8,128)S(1)}, f32[17,8,128]{2,1,0:T(8,128)S(1)}, u32[]{:S(2)}, u32[]{:S(2)}) collective-permute-start(f32[17,8,128]{2,1,0:T(8,128)S(1)} %get-tuple-element.35), channel_id=1, source_target_pairs={{0,7},{1,6},{2,5},{3,4},{4,3},{5,2},{6,1},{7,0},{8,15},{9,14},{10,... | collective-permute-start | bytes 208904 | tf_op jit(solution)/shard_map/ppermute | solution.py:376
  15.2 4.5 %collective-permute-start.10 = (f32[17,8,128]{2,1,0:T(8,128)S(1)}, f32[17,8,128]{2,1,0:T(8,128)S(1)}, u32[]{:S(2)}, u32[]{:S(2)}) collective-permute-start(f32[17,8,128]{2,1,0:T(8,128)S(1)} %get-tuple-element.36), channel_id=1, source_target_pairs={{0,3},{1,2},{2,1},{3,0},{4,7},{5,6},{6,5},{7,4},{8,11},{9,10},{10,... | collective-permute-start | bytes 208904 | tf_op jit(solution)/shard_map/ppermute | solution.py:376
  15.9 4.4 %collective-permute-start.11 = (f32[17,8,128]{2,1,0:T(8,128)S(1)}, f32[17,8,128]{2,1,0:T(8,128)S(1)}, u32[]{:S(2)}, u32[]{:S(2)}) collective-permute-start(f32[17,8,128]{2,1,0:T(8,128)S(1)} %get-tuple-element.37), channel_id=1, source_target_pairs={{0,5},{1,4},{2,7},{3,6},{4,1},{5,0},{6,3},{7,2},{8,13},{9,12},{10,... | collective-permute-start | bytes 208904 | tf_op jit(solution)/shard_map/ppermute | solution.py:376

commit v8 on v7

--- a/solution.py
+++ b/solution.py
@@ -9,13 +9,11 @@
 
 BR = 4
 CAP = 2
-SWAP1, CROSS1 = 1, 0
-SWAP2, CROSS2 = 0, 1
 ZR = 8
 HALF_DT = 0.075
 NF = 5
 RHO, ENE, VELU, VELV, GAM = range(NF)
-FAR_P, FAR_U = 5, 6
+FAR_P, FAR_U, INFO = 5, 6, 7
 SMEM = pl.BlockSpec(memory_space=pltpu.SMEM)
 VMEM = pl.BlockSpec(memory_space=pltpu.VMEM)
 
@@ -48,7 +46,7 @@
 
 
 def target(path, core):
-    return 2 * reached(path, core) + (1 if CROSS2 and path[0] else 0)
+    return 2 * reached(path, core) + (1 if path[0] else 0)
 
 
 def where_am_i():
@@ -88,7 +86,7 @@
     chip, core = me // 2, me % 2
     sub = sublane(width)
     first = me == 0
-    goals = [chip ^ reached(route, core) for route in routes(chips, SWAP1)]
+    goals = [chip ^ reached(route, core) for route in routes(chips, True)]
     copies[0].wait()
 
     def tile_of(field, block):
@@ -119,41 +117,46 @@
     for copy in copies[1 + NF :]:
         copy.wait()
     lane = lax.broadcasted_iota(jnp.int32, (1, width), 1)
+    info = jnp.zeros((1, width), jnp.int32)
+    for index in range(2 * n):
+        value = owner[index] if index < n else slot[index - n]
+        info = jnp.where(lane // (width // (2 * n)) == index, value, info)
+    for buf in chip_bufs:
+        buf[8 * NF + INFO : 8 * NF + INFO + 1, :] = info.astype(jnp.float32)
     for block in range(n):
         line = jnp.where(lane < width // 2, owner[block], slot[block])
         chip_bufs[0][home + rows + block : home + rows + block + 1, :] = line.astype(jnp.float32)
 
 
-def tag_kernel(n, rows, own_home, sib_home, code, tags):
-    chips = n // 2
-    width = own_home.shape[1]
+def code_kernel(n, rows, own_home, sib_home, code):
     _, me = where_am_i()
-    chip, core = me // 2, me % 2
     span = pl.ds(8 * (NF + 1) + rows, n)
-    own, sib = own_home[span, :].astype(jnp.int32), sib_home[span, :].astype(jnp.int32)
-    both = (jnp.where(core == 0, own, sib), jnp.where(core == 0, sib, own))
+    own, sib = own_home[span, 0:128].astype(jnp.int32), sib_home[span, 0:128].astype(jnp.int32)
     line_id = lax.broadcasted_iota(jnp.int32, (n, 128), 0)
-    sub = sublane(128)
-    slots = []
-    for device, info in enumerate(both):
-        owner = info[:, 0:128]
+    for device in range(2):
+        owner = jnp.where(me % 2 == device, own, sib)
         rank = jnp.zeros((n, 128), jnp.int32)
         for block in range(n):
             same = jnp.logical_and(owner == owner[block : block + 1, :], line_id > block)
             rank = jnp.where(same, rank + 1, rank)
-        slots.append((owner ^ me) * (2 * CAP) + (device * CAP) + rank)
-        code[device] = slots[device]
-    for index, path in enumerate(routes(chips, SWAP2)):
-        want = sub + target(path, core) * (2 * CAP)
-        tile = jnp.full((8, 128), -1, jnp.int32)
-        for device, info in enumerate(both):
-            for block in range(n):
-                hit = jnp.logical_and(want == slots[device][block : block + 1, :], sub < 2 * CAP)
-                tile = jnp.where(hit, info[block : block + 1, width - 128 :], tile)
-        tags[index] = tile.astype(jnp.float32)
-
-
-def pack_partials(n, paths, core, code, tags, parts, sends):
+        code[device] = (owner ^ me) * (2 * CAP) + (device * CAP) + rank
+
+
+def labels_of(n, me, infos):
+    step = infos[0].shape[1] // (2 * n)
+    sub = sublane(128)
+    tile = jnp.full((8, 128), -1.0, jnp.float32)
+    for device, info in enumerate(infos):
+        value = lambda index: jnp.broadcast_to(info[:, index * step : index * step + 1], (8, 128))
+        place = jnp.full((8, 128), device * CAP, jnp.int32)
+        for block in range(n):
+            hit = value(block) == me.astype(jnp.float32)
+            tile = jnp.where(jnp.logical_and(hit, sub == place), value(n + block), tile)
+            place = jnp.where(hit, place + 1, place)
+    return tile
+
+
+def pack_partials(n, paths, core, code, parts, sends):
     width = parts.shape[3]
     pieces = width // 128
     lanes = [slice(piece * 128, piece * 128 + 128) for piece in range(pieces)]
@@ -170,15 +173,13 @@
             rank = device * CAP + index % CAP
             for piece in range(pieces):
                 sends[index // CAP][rank * pieces + piece] = found[index][piece]
-    for send, tag in zip(sends, tags):
-        send[2 * CAP * pieces] = tag[...]
 
 
 def step_kernel(n, *refs):
     chips = n // 2
     refs = list(refs)
     take = lambda count: [refs.pop(0) for _ in range(count)]
-    code, tags = take(2)
+    (code,) = take(1)
     mine, theirs = take(chips), take(chips)
     across, across_sib, sweep = take(3)
     nxt_prs, nxt_u, nxt_v, coef = take(4)
@@ -198,11 +199,9 @@
     def pair(own, sib):
         return jnp.where(is_low, own, sib), jnp.where(is_low, sib, own)
 
-    for index, path in enumerate(routes(chips, SWAP1)):
+    for index, path in enumerate(routes(chips, True)):
         source = chip ^ reached(path, core)
-        own, sib = mine[index], theirs[routes(chips, SWAP1).index((path[1], path[0]))]
-        if CROSS1 and path[0]:
-            own, sib = sib, own
+        own, sib = mine[index], theirs[routes(chips, True).index((path[1], path[0]))]
         for field in range(NF):
             span = pl.ds(8 * field, 8)
             even, odd = pair(own[span, :], sib[span, :])
@@ -279,16 +278,27 @@
     for device in range(2):
         lax.fori_loop(0, chips, lambda index, _, device=device: (second(device, index), 0)[1], 0, unroll=n <= 8)
 
-    pack_partials(n, routes(chips, SWAP2)[1:], core, code, [tags.at[1 + i] for i in range(chips - 1)], parts, sends)
-
-
-def side_kernel(n, prs, velu, velv, coef, parts, code, tags, vel, home):
+    pack_partials(n, routes(chips, False)[1:], core, code, parts, sends)
+
+
+def side_kernel(n, *refs):
     chips = n // 2
+    prs, velu, velv, coef, parts, code = refs[:6]
+    mine, theirs = refs[6 : 6 + chips], refs[6 + chips : 6 + 2 * chips]
+    vel, home, labels = refs[6 + 2 * chips :]
     _, me = where_am_i()
-    pack_partials(n, routes(chips, SWAP2)[:1], me % 2, code, [tags.at[0]], parts, [home])
+    core = me % 2
+    pack_partials(n, routes(chips, False)[:1], core, code, parts, [home])
+    paths = routes(chips, True)
+    line = slice(8 * NF + INFO, 8 * NF + INFO + 1)
+    for index, (mask, _) in enumerate(routes(chips, False)):
+        low, high = [path[0] for path in paths].index(mask), [path[1] for path in paths].index(mask)
+        even = jnp.where(core == 0, mine[low][line, :], theirs[low][line, :])
+        odd = jnp.where(core == 0, theirs[high][line, :], mine[high][line, :])
+        labels[index] = labels_of(n, me, (even, odd))
 
     def one(index, _):
-        tile = 1 + me % 2 * chips + index
+        tile = 1 + core * chips + index
         span, dest = at(tile), at(index)
         press, scale = prs[span, :], coef[span, :]
         vel[0, dest, :] = velu[span, :] - down_up(prs, tile, press) * scale
@@ -301,11 +311,13 @@
 def land_kernel(n, final, *refs):
     chips = n // 2
     refs = list(refs)
+    labels = refs.pop(0)
     if final:
         mass_out, energy_out, sums_out, sems = refs[-4:]
         sums_in, arrived = refs[0], refs[1:-4]
     else:
         sums_in, arrived, sums_out = None, refs[:-1], refs[-1]
+    skipped = chips - len(arrived) if final else 0
     parts = sums_out.shape[2] // 128
     sub = sublane(128)
 
@@ -317,10 +329,9 @@
     def tile_pair(index, _):
         span = pl.ds(pl.multiple_of(index * 8, 8), 8)
         sums = [[jnp.zeros((8, 128), jnp.float32) for _ in range(parts)] for _ in range(2)]
-        for buf in arrived:
-            tag_tile = buf[2 * CAP * parts]
+        for number, buf in enumerate(arrived):
             for rank in range(2 * CAP):
-                tag = jnp.broadcast_to(tag_tile[rank : rank + 1, :], (8, 128))
+                tag = jnp.broadcast_to(labels[skipped + number, rank : rank + 1, :], (8, 128))
                 for bit in range(2):
                     hit = tag == (2 * index + bit) * 1.0
                     for part in range(parts):
@@ -375,7 +386,7 @@
         links = [(i, i ^ 2 * path[i % 2] ^ cross) for i in range(n)]
         return lax.ppermute(x, "bis", links) if path[0] else x
 
-    paths = routes(chips, SWAP1)
+    paths = routes(chips, True)
 
     owner = owner.reshape(n)
     extra = -(-(rows + n) // 8) * 8
@@ -398,30 +409,27 @@
         name="pack",
     )(*[pltpu.with_memory_space_constraint(x, pltpu.HBM) for x in (order.reshape(n), owner, slot_target, sweep, state)])
     across = lax.ppermute(packed[chips], ("grp", "bis"), across_links(groups, n))
-    mine = [to_chip(x, path, CROSS1) for x, path in zip(packed, paths)]
+    mine = [to_chip(x, path, 0) for x, path in zip(packed, paths)]
     theirs = [to_sibling(x) for x in mine]
     across_sib = to_sibling(jnp.concatenate([across] + [x[0:8] for x in mine[1:]]))
 
-    code, tags = pl.pallas_call(
-        functools.partial(tag_kernel, n, rows),
-        out_shape=[
-            jax.ShapeDtypeStruct((2, n, 128), jnp.int32),
-            jax.ShapeDtypeStruct((chips, 8, 128), f32),
-        ],
+    code = pl.pallas_call(
+        functools.partial(code_kernel, n, rows),
+        out_shape=jax.ShapeDtypeStruct((2, n, 128), jnp.int32),
         in_specs=[VMEM] * 2,
-        out_specs=[VMEM] * 2,
-        compiler_params=params,
-        name="tags",
+        out_specs=VMEM,
+        compiler_params=params,
+        name="code",
     )(mine[0], theirs[0])
 
     stack = (2 * chips + 2) * 8
-    send_shape = (2 * CAP * parts + 1, 8, 128)
+    send_shape = (2 * CAP * parts, 8, 128)
     out = pl.pallas_call(
         functools.partial(step_kernel, n),
         out_shape=[jax.ShapeDtypeStruct((stack, width), f32)] * 4
         + [jax.ShapeDtypeStruct((2, n, 8, width), f32)]
         + [jax.ShapeDtypeStruct(send_shape, f32)] * (chips - 1),
-        in_specs=[VMEM] * (2 * chips + 5),
+        in_specs=[VMEM] * (2 * chips + 4),
         out_specs=[VMEM] * (chips + 4),
         scratch_shapes=[
             pltpu.VMEM((NF, stack, width), f32),
@@ -431,35 +439,39 @@
         ],
         compiler_params=params,
         name="substeps",
-    )(code, tags, *mine, *theirs, across, across_sib, sweep)
-    arrived = [to_chip(x, path, CROSS2) for x, path in zip(out[5:], routes(chips, SWAP2)[1:])]
-    vel, home = pl.pallas_call(
+    )(code, *mine, *theirs, across, across_sib, sweep)
+    arrived = [to_chip(x, path, 1) for x, path in zip(out[5:], routes(chips, False)[1:])]
+    vel, home, labels = pl.pallas_call(
         functools.partial(side_kernel, n),
-        out_shape=[jax.ShapeDtypeStruct((2, rows, width), f32), jax.ShapeDtypeStruct(send_shape, f32)],
-        in_specs=[VMEM] * 7,
-        out_specs=[VMEM] * 2,
+        out_shape=[
+            jax.ShapeDtypeStruct((2, rows, width), f32),
+            jax.ShapeDtypeStruct(send_shape, f32),
+            jax.ShapeDtypeStruct((chips, 8, 128), f32),
+        ],
+        in_specs=[VMEM] * (6 + 2 * chips),
+        out_specs=[VMEM] * 3,
         compiler_params=params,
         name="velocities",
-    )(*out[:5], code, tags)
+    )(*out[:5], code, *mine, *theirs)
     arrived = [home] + arrived
     early = 2
     sums = pl.pallas_call(
         functools.partial(land_kernel, n, False),
         out_shape=jax.ShapeDtypeStruct((2, rows, width), f32),
-        in_specs=[VMEM] * early,
+        in_specs=[VMEM] * (1 + early),
         out_specs=VMEM,
         compiler_params=params,
         name="sums",
-    )(*arrived[:early])
+    )(labels, *arrived[:early])
     mass, energy = pl.pallas_call(
         functools.partial(land_kernel, n, True),
         out_shape=[jax.ShapeDtypeStruct((rows, width), f32)] * 2,
-        in_specs=[VMEM] * (1 + chips - early),
+        in_specs=[VMEM] * (2 + chips - early),
         out_specs=[pl.BlockSpec(memory_space=pl.ANY)] * 2,
         scratch_shapes=[pltpu.VMEM((2, rows, width), f32), pltpu.SemaphoreType.DMA((2, chips))],
         compiler_params=params,
         name="land",
-    )(sums, *arrived[early:])
+    )(labels, sums, *arrived[early:])
     return mass, energy, vel
 
 

time: 21.2 us -> 21 us (level)
  waiting for transfers between devices: 7.96 us -> 7.52 us
    ppermute x6, waiting for transfers between devices: 6.83 us -> 6.36 us  [to_chip(): return lax.ppermute(x, 'bis', links) if path[0] else x]
    pallas_call x1, Pallas kernels: 0.76 us -> 0.97 us  [shards(): pl.pallas_call(functools.partial(side_kernel, n), out_shape=[jax.ShapeDty...]
  transfers between devices with their start and end apart: 12 -> 12, of which waited for: 6 -> 6; matrix products, arithmetic and copies ran while one was open for 0% -> 0% of each run, Pallas kernels for 4% -> 5%
where the time goes in v8:
time: 21 us; the launch traced here: 20.8 us
  starting transfers between devices  8.79 us (42%)
  waiting for transfers between devices  7.52 us (36%)
  Pallas kernels  3.8 us (18%)
  between operations  0.7 us (3%)
    ppermute x6, starting transfers between devices, to_chip(): return lax.ppermute(x, 'bis', links) if path[0] else x  7.64 us
    ppermute x6, waiting for transfers between devices, to_chip(): return lax.ppermute(x, 'bis', links) if path[0] else x  6.36 us
    pallas_call x1, Pallas kernels, shards(): pl.pallas_call(functools.partial(pack_kernel, n), out_shape=[jax.ShapeDty...  1.29 us
    ppermute x5, waiting for transfers between devices, to_sibling(): return lax.ppermute(x, 'bis', [(i, i ^ 1) for i in range(n)])  1.16 us
    ppermute x5, starting transfers between devices, to_sibling(): return lax.ppermute(x, 'bis', [(i, i ^ 1) for i in range(n)])  1.15 us
    pallas_call x1, Pallas kernels, shards(): pl.pallas_call(functools.partial(side_kernel, n), out_shape=[jax.ShapeDty...  0.97 us
    pallas_call x1, Pallas kernels, shards(): pl.pallas_call(functools.partial(land_kernel, n, True), out_shape=[jax.Sh...  0.78 us
    pallas_call x1, Pallas kernels, shards(): pl.pallas_call(functools.partial(step_kernel, n), out_shape=[jax.ShapeDty...  0.65 us
  transfers between devices with their start and end apart: 12, of which 6 were waited for; matrix products, arithmetic and copies ran while one was open for 0% of the time, Pallas kernels for 5%

profile of v8, /device:TPU:0, one launch (start us, length us, event | category | flops | bytes accessed | tf_op | source)
XLA Modules:
  0.0 20.8 jit_solution(12930835725201829089)
XLA Ops:
  0.6 1.3 %pack.1 = (f32[88,512]{1,0:T(8,128)S(1)}, f32[48,512]{1,0:T(8,128)S(1)}, f32[48,512]{1,0:T(8,128)S(1)}, f32[48,512]{1,0:T(8,128)S(1)}, f32[8,512]{1,0:T(8,128)S(1)}) custom-call(s32[8]{0:T(128)} %bitcast.2, s32[8]{0:T(128)} %bitcast.3, s32[8]{0:T(128)} %refs_2_.1, f32[32,512]{1,0:T(8,128)} %refs_11_.1, f32[5,32,512]{2,1,0:T(8,128)} %refs_4_.1), custom_call_target="tpu_custom_call" | custom-call | tf_op jit(solution)/shard_map/pack/pallas_call | solution.py:393
  1.9 4.0 %collective-permute-start.1 = (f32[48,512]{1,0:T(8,128)S(1)}, f32[48,512]{1,0:T(8,128)S(1)}, u32[]{:S(2)}, u32[]{:S(2)}) collective-permute-start(f32[48,512]{1,0:T(8,128)S(1)} %get-tuple-element.22), channel_id=1, source_target_pairs={{0,6},{1,7},{2,4},{3,5},{4,2},{5,3},{6,0},{7,1},{8,14},{9,15},{10,... | collective-permute-start | bytes 294920 | tf_op jit(solution)/shard_map/ppermute | solution.py:387
  5.9 0.5 %collective-permute-start.2 = (f32[48,512]{1,0:T(8,128)S(1)}, f32[48,512]{1,0:T(8,128)S(1)}, u32[]{:S(2)}, u32[]{:S(2)}) collective-permute-start(f32[48,512]{1,0:T(8,128)S(1)} %get-tuple-element.23), channel_id=1, source_target_pairs={{0,2},{1,5},{2,0},{3,7},{4,6},{5,1},{6,4},{7,3},{8,10},{9,13},{10,... | collective-permute-start | bytes 294920 | tf_op jit(solution)/shard_map/ppermute | solution.py:387
  6.4 0.1 collective-permute-start.3
  6.5 0.0 collective-permute-start.7
  6.5 0.5 %collective-permute-start = (f32[88,512]{1,0:T(8,128)S(1)}, f32[88,512]{1,0:T(8,128)S(1)}, u32[]{:S(2)}, u32[]{:S(2)}) collective-permute-start(f32[88,512]{1,0:T(8,128)S(1)} %get-tuple-element.21.own_home.refs_1_.refs_6_), channel_id=1, source_target_pairs={{0,1},{1,0},{2,3},{3,2},{4,5},{5,4},{6,7},{7,6},{8,9},{9,8},{10,11... | collective-permute-start | bytes 540680 | tf_op jit(solution)/shard_map/ppermute | solution.py:383
  7.0 2.0 %collective-permute-done.1.refs_2_.refs_7_ = f32[48,512]{1,0:T(8,128)S(1)} collective-permute-done((f32[48,512]{1,0:T(8,128)S(1)}, f32[48,512]{1,0:T(8,128)S(1)}, u32[]{:S(2)}, u32[]{:S(2)}) %collective-permute-start.1) | collective-permute-done | bytes 98336 | tf_op jit(solution)/shard_map/ppermute | solution.py:387
  9.1 0.0 collective-permute-start.4
  9.1 2.0 %collective-permute-done.2.refs_3_.refs_8_ = f32[48,512]{1,0:T(8,128)S(1)} collective-permute-done((f32[48,512]{1,0:T(8,128)S(1)}, f32[48,512]{1,0:T(8,128)S(1)}, u32[]{:S(2)}, u32[]{:S(2)}) %collective-permute-start.2) | collective-permute-done | bytes 98336 | tf_op jit(solution)/shard_map/ppermute | solution.py:387
  11.1 0.0 collective-permute-start.5
  11.1 0.0 collective-permute-done.3.refs_4_.refs_9_
  11.1 0.5 %collective-permute-start.6 = (f32[48,512]{1,0:T(8,128)S(1)}, f32[48,512]{1,0:T(8,128)S(1)}, u32[]{:S(2)}, u32[]{:S(2)}) collective-permute-start(f32[48,512]{1,0:T(8,128)S(1)} %collective-permute-done.3.refs_4_.refs_9_), channel_id=1, source_target_pairs={{0,1},{1,0},{2,3},{3,2},{4,5},{5,4},{6,7},{7,6},{8,9},{9,8},{10,11... | collective-permute-start | bytes 294920 | tf_op jit(solution)/shard_map/ppermute | solution.py:383
  11.6 0.0 collective-permute-done.7.refs_9_
  11.6 0.0 copy-start
  11.7 0.1 collective-permute-start.8
  11.8 0.0 collective-permute-done.sib_home.refs_5_.refs_10_
  11.8 1.1 %collective-permute-done.8.refs_10_ = f32[32,512]{1,0:T(8,128)S(1)} collective-permute-done((f32[32,512]{1,0:T(8,128)S(1)}, f32[32,512]{1,0:T(8,128)S(1)}, u32[]{:S(2)}, u32[]{:S(2)}) %collective-permute-start.8) | collective-permute-done | bytes 65568 | tf_op jit(solution)/shard_map/ppermute | solution.py:383
  13.0 0.0 collective-permute-done.4.refs_6_.refs_11_
  13.0 0.0 collective-permute-done.5.refs_7_.refs_12_
  13.0 0.0 collective-permute-done.6.refs_8_.refs_13_
  13.0 0.0 copy-done
  13.0 0.6 %substeps.1 = (f32[80,512]{1,0:T(8,128)S(1)}, f32[80,512]{1,0:T(8,128)S(1)}, f32[80,512]{1,0:T(8,128)S(1)}, f32[80,512]{1,0:T(8,128)S(1)}, f32[2,8,8,512]{3,2,1,...) custom-call(s32[2,8,128]{2,1,0:T(8,128)S(1)} %code.1.refs_0_.refs_5_, ...), custom_call_target="tpu_custom_call" | custom-call | tf_op jit(solution)/shard_map/substeps/pallas_call | solution.py:427
  13.7 1.5 %collective-permute-start.9 = (f32[16,8,128]{2,1,0:T(8,128)S(1)}, f32[16,8,128]{2,1,0:T(8,128)S(1)}, u32[]{:S(2)}, u32[]{:S(2)}) collective-permute-start(f32[16,8,128]{2,1,0:T(8,128)S(1)} %get-tuple-element.33), channel_id=1, source_target_pairs={{0,7},{1,6},{2,5},{3,4},{4,3},{5,2},{6,1},{7,0},{8,15},{9,14},{10,... | collective-permute-start | bytes 196616 | tf_op jit(solution)/shard_map/ppermute | solution.py:387
  15.2 0.7 %collective-permute-start.10 = (f32[16,8,128]{2,1,0:T(8,128)S(1)}, f32[16,8,128]{2,1,0:T(8,128)S(1)}, u32[]{:S(2)}, u32[]{:S(2)}) collective-permute-start(f32[16,8,128]{2,1,0:T(8,128)S(1)} %get-tuple-element.34), channel_id=1, source_target_pairs={{0,3},{1,2},{2,1},{3,0},{4,7},{5,6},{6,5},{7,4},{8,11},{9,10},{10,... | collective-permute-start | bytes 196616 | tf_op jit(solution)/shard_map/ppermute | solution.py:387
  15.9 0.8 %collective-permute-start.11 = (f32[16,8,128]{2,1,0:T(8,128)S(1)}, f32[16,8,128]{2,1,0:T(8,128)S(1)}, u32[]{:S(2)}, u32[]{:S(2)}) collective-permute-start(f32[16,8,128]{2,1,0:T(8,128)S(1)} %get-tuple-element.35), channel_id=1, source_target_pairs={{0,5},{1,4},{2,7},{3,6},{4,1},{5,0},{6,3},{7,2},{8,13},{9,12},{10,... | collective-permute-start | bytes 196616 | tf_op jit(solution)/shard_map/ppermute | solution.py:387
  16.7 1.0 %velocities.1 = (f32[2,32,512]{2,1,0:T(8,128)}, f32[16,8,128]{2,1,0:T(8,128)S(1)}, f32[4,8,128]{2,1,0:T(8,128)S(1)}) custom-call(f32[80,512]{1,0:T(8,128)S(1)} %get-tuple-element.26.refs_0_, f32[80,512]{1,0:T(8,128)S(1)} %get-tuple-element.27.refs_1_, f32[80,512]{1,0:T(8,128)S(1)} %get-tuple-element.28.refs_2_, f32[80,512]{1,0:T(8,128)S(1)} %get-tuple-element.29.refs_3_, ...), custom_call_target="tpu_custom_call" | custom-call | tf_op jit(solution)/shard_map/velocities/pallas_call | solution.py:444
  17.7 1.0 %collective-permute-done.9.refs_2_ = f32[16,8,128]{2,1,0:T(8,128)S(1)} collective-permute-done((f32[16,8,128]{2,1,0:T(8,128)S(1)}, f32[16,8,128]{2,1,0:T(8,128)S(1)}, u32[]{:S(2)}, u32[]{:S(2)}) %collective-permute-start.9) | collective-permute-done | bytes 65568 | tf_op jit(solution)/shard_map/ppermute | solution.py:387
  18.7 0.1 sums.1.refs_1_
  18.8 0.8 %collective-permute-done.10.refs_2_ = f32[16,8,128]{2,1,0:T(8,128)S(1)} collective-permute-done((f32[16,8,128]{2,1,0:T(8,128)S(1)}, f32[16,8,128]{2,1,0:T(8,128)S(1)}, u32[]{:S(2)}, u32[]{:S(2)}) %collective-permute-start.10) | collective-permute-done | bytes 65568 | tf_op jit(solution)/shard_map/ppermute | solution.py:387
  19.6 0.5 %collective-permute-done.11.refs_3_ = f32[16,8,128]{2,1,0:T(8,128)S(1)} collective-permute-done((f32[16,8,128]{2,1,0:T(8,128)S(1)}, f32[16,8,128]{2,1,0:T(8,128)S(1)}, u32[]{:S(2)}, u32[]{:S(2)}) %collective-permute-start.11) | collective-permute-done | bytes 65568 | tf_op jit(solution)/shard_map/ppermute | solution.py:387
  20.0 0.8 %land.1 = (f32[32,512]{1,0:T(8,128)}, f32[32,512]{1,0:T(8,128)}) custom-call(f32[4,8,128]{2,1,0:T(8,128)S(1)} %get-tuple-element.31.refs_0_, f32[2,32,512]{2,1,0:T(8,128)S(1)} %sums.1.refs_1_, f32[16,8,128]{2,1,0:T(8,128)S(1)} %collective-permute-done.10.refs_2_, f32[16,8,128]{2,1,0:T(8,128)S(1)} %collective-permute-done.11.refs_3_), custom_call_target="tpu_custom_call" | custom-call | tf_op jit(solution)/shard_map/land/pallas_call | solution.py:466
  (5 shorter events, 0.0 us)
Async XLA Ops:
  1.9 7.1 %collective-permute-start.1 = (f32[48,512]{1,0:T(8,128)S(1)}, f32[48,512]{1,0:T(8,128)S(1)}, u32[]{:S(2)}, u32[]{:S(2)}) collective-permute-start(f32[48,512]{1,0:T(8,128)S(1)} %get-tuple-element.22), channel_id=1, source_target_pairs={{0,6},{1,7},{2,4},{3,5},{4,2},{5,3},{6,0},{7,1},{8,14},{9,15},{10,... | collective-permute-start | bytes 294920 | tf_op jit(solution)/shard_map/ppermute | solution.py:387
  5.9 5.2 %collective-permute-start.2 = (f32[48,512]{1,0:T(8,128)S(1)}, f32[48,512]{1,0:T(8,128)S(1)}, u32[]{:S(2)}, u32[]{:S(2)}) collective-permute-start(f32[48,512]{1,0:T(8,128)S(1)} %get-tuple-element.23), channel_id=1, source_target_pairs={{0,2},{1,5},{2,0},{3,7},{4,6},{5,1},{6,4},{7,3},{8,10},{9,13},{10,... | collective-permute-start | bytes 294920 | tf_op jit(solution)/shard_map/ppermute | solution.py:387
  6.4 4.7 %collective-permute-start.3 = (f32[48,512]{1,0:T(8,128)S(1)}, f32[48,512]{1,0:T(8,128)S(1)}, u32[]{:S(2)}, u32[]{:S(2)}) collective-permute-start(f32[48,512]{1,0:T(8,128)S(1)} %get-tuple-element.24), channel_id=1, source_target_pairs={{0,4},{1,3},{2,6},{3,1},{4,0},{5,7},{6,2},{7,5},{8,12},{9,11},{10,... | collective-permute-start | bytes 294920 | tf_op jit(solution)/shard_map/ppermute | solution.py:387
  6.5 5.1 %collective-permute-start.7 = (f32[8,512]{1,0:T(8,128)S(1)}, f32[8,512]{1,0:T(8,128)S(1)}, u32[]{:S(2)}, u32[]{:S(2)}) collective-permute-start(f32[8,512]{1,0:T(8,128)S(1)} %get-tuple-element.25), channel_id=1, source_target_pairs={{2,3},{3,2},{4,5},{5,4},{7,8},{8,7},{6,14},{14,6},{10,11},{11,10},... | collective-permute-start | bytes 49160 | tf_op jit(solution)/shard_map/ppermute | solution.py:411
  6.5 5.3 %collective-permute-start = (f32[88,512]{1,0:T(8,128)S(1)}, f32[88,512]{1,0:T(8,128)S(1)}, u32[]{:S(2)}, u32[]{:S(2)}) collective-permute-start(f32[88,512]{1,0:T(8,128)S(1)} %get-tuple-element.21.own_home.refs_1_.refs_6_), channel_id=1, source_target_pairs={{0,1},{1,0},{2,3},{3,2},{4,5},{5,4},{6,7},{7,6},{8,9},{9,8},{10,11... | collective-permute-start | bytes 540680 | tf_op jit(solution)/shard_map/ppermute | solution.py:383
  9.1 3.9 %collective-permute-start.4 = (f32[48,512]{1,0:T(8,128)S(1)}, f32[48,512]{1,0:T(8,128)S(1)}, u32[]{:S(2)}, u32[]{:S(2)}) collective-permute-start(f32[48,512]{1,0:T(8,128)S(1)} %collective-permute-done.1.refs_2_.refs_7_), channel_id=1, source_target_pairs={{0,1},{1,0},{2,3},{3,2},{4,5},{5,4},{6,7},{7,6},{8,9},{9,8},{10,11... | collective-permute-start | bytes 294920 | tf_op jit(solution)/shard_map/ppermute | solution.py:383
  11.1 1.9 %collective-permute-start.5 = (f32[48,512]{1,0:T(8,128)S(1)}, f32[48,512]{1,0:T(8,128)S(1)}, u32[]{:S(2)}, u32[]{:S(2)}) collective-permute-start(f32[48,512]{1,0:T(8,128)S(1)} %collective-permute-done.2.refs_3_.refs_8_), channel_id=1, source_target_pairs={{0,1},{1,0},{2,3},{3,2},{4,5},{5,4},{6,7},{7,6},{8,9},{9,8},{10,11... | collective-permute-start | bytes 294920 | tf_op jit(solution)/shard_map/ppermute | solution.py:383
  11.1 1.9 %collective-permute-start.6 = (f32[48,512]{1,0:T(8,128)S(1)}, f32[48,512]{1,0:T(8,128)S(1)}, u32[]{:S(2)}, u32[]{:S(2)}) collective-permute-start(f32[48,512]{1,0:T(8,128)S(1)} %collective-permute-done.3.refs_4_.refs_9_), channel_id=1, source_target_pairs={{0,1},{1,0},{2,3},{3,2},{4,5},{5,4},{6,7},{7,6},{8,9},{9,8},{10,11... | collective-permute-start | bytes 294920 | tf_op jit(solution)/shard_map/ppermute | solution.py:383
  11.6 1.3 %copy-start = (f32[32,512]{1,0:T(8,128)S(1)}, f32[32,512]{1,0:T(8,128)}, u32[]{:S(2)}) copy-start(f32[32,512]{1,0:T(8,128)} %refs_11_.1) | copy-start | bytes 196612
  11.7 1.3 %collective-permute-start.8 = (f32[32,512]{1,0:T(8,128)S(1)}, f32[32,512]{1,0:T(8,128)S(1)}, u32[]{:S(2)}, u32[]{:S(2)}) collective-permute-start(f32[32,512]{1,0:T(8,128)S(1)} %pad_maximum_fusion), channel_id=1, source_target_pairs={{0,1},{1,0},{2,3},{3,2},{4,5},{5,4},{6,7},{7,6},{8,9},{9,8},{10,11... | collective-permute-start | bytes 196616 | tf_op jit(solution)/shard_map/ppermute | solution.py:383
  13.7 5.0 %collective-permute-start.9 = (f32[16,8,128]{2,1,0:T(8,128)S(1)}, f32[16,8,128]{2,1,0:T(8,128)S(1)}, u32[]{:S(2)}, u32[]{:S(2)}) collective-permute-start(f32[16,8,128]{2,1,0:T(8,128)S(1)} %get-tuple-element.33), channel_id=1, source_target_pairs={{0,7},{1,6},{2,5},{3,4},{4,3},{5,2},{6,1},{7,0},{8,15},{9,14},{10,... | collective-permute-start | bytes 196616 | tf_op jit(solution)/shard_map/ppermute | solution.py:387
  15.2 4.4 %collective-permute-start.10 = (f32[16,8,128]{2,1,0:T(8,128)S(1)}, f32[16,8,128]{2,1,0:T(8,128)S(1)}, u32[]{:S(2)}, u32[]{:S(2)}) collective-permute-start(f32[16,8,128]{2,1,0:T(8,128)S(1)} %get-tuple-element.34), channel_id=1, source_target_pairs={{0,3},{1,2},{2,1},{3,0},{4,7},{5,6},{6,5},{7,4},{8,11},{9,10},{10,... | collective-permute-start | bytes 196616 | tf_op jit(solution)/shard_map/ppermute | solution.py:387
  15.9 4.1 %collective-permute-start.11 = (f32[16,8,128]{2,1,0:T(8,128)S(1)}, f32[16,8,128]{2,1,0:T(8,128)S(1)}, u32[]{:S(2)}, u32[]{:S(2)}) collective-permute-start(f32[16,8,128]{2,1,0:T(8,128)S(1)} %get-tuple-element.35), channel_id=1, source_target_pairs={{0,5},{1,4},{2,7},{3,6},{4,1},{5,0},{6,3},{7,2},{8,13},{9,12},{10,... | collective-permute-start | bytes 196616 | tf_op jit(solution)/shard_map/ppermute | solution.py:387

commit v9 on v8

--- a/solution.py
+++ b/solution.py
@@ -75,12 +75,17 @@
     home = 8 * (NF + 1)
     copies = [pltpu.make_async_copy(order_in, order, sems.at[0])]
     copies += [pltpu.make_async_copy(state_in.at[field], state.at[field], sems.at[1 + field]) for field in range(NF)]
+    halves = [slice(0, rows // 2), slice(rows // 2, rows)]
     copies += [
         pltpu.make_async_copy(owner_in, owner, sems.at[1 + NF]),
         pltpu.make_async_copy(slot_in, slot, sems.at[2 + NF]),
         pltpu.make_async_copy(sweep_in, chip_bufs[0].at[home : home + rows, :], sems.at[3 + NF]),
     ]
-    for copy in copies:
+    copies[0].start()
+    for field in range(NF):
+        for half in halves:
+            pltpu.make_async_copy(state_in.at[field, half, :], state.at[field, half, :], sems.at[1 + field]).start()
+    for copy in copies[1 + NF :]:
         copy.start()
     _, me = where_am_i()
     chip, core = me // 2, me % 2
@@ -89,31 +94,31 @@
     goals = [chip ^ reached(route, core) for route in routes(chips, True)]
     copies[0].wait()
 
-    def tile_of(field, block):
-        return state[field, pl.ds(pl.multiple_of(block // 2 * 8, 8), 8), :]
-
-    def halo(buf, base, index):
-        block = order[index]
-        near = block * 4 + jnp.where(first, 0, BR - 1)
-        far = block * 4 + jnp.where(first, 1, BR - 2)
+    def rim_rows(index):
+        start = order[index] * BR
+        return start + jnp.where(first, 0, BR - 1), start + jnp.where(first, 1, BR - 2)
+
+    def halo(buf, base, near, far):
         for field in range(NF):
             buf[base + field : base + field + 1, :] = state[field, pl.ds(near, 1), :]
         line = lambda field: state[field, pl.ds(far, 1), :]
         buf[base + FAR_P : base + FAR_P + 1, :] = (line(GAM) - 1.0) * line(RHO) * line(ENE)
         buf[base + FAR_U : base + FAR_U + 1, :] = line(VELU)
 
+    picks = [(order[2 * goal], order[2 * goal + 1]) for goal in goals]
+    beyond = [jnp.where(first, jnp.minimum(2 * goal + 2, n - 1), jnp.maximum(2 * goal - 1, 0)) for goal in goals]
+    rims = [rim_rows(index) for index in beyond + [jnp.where(first, 0, n - 1)]]
     for field in range(NF):
         copies[1 + field].wait()
-        for buf, goal in zip(chip_bufs, goals):
-            low = order[2 * goal]
-            high = order[2 * goal + 1]
-            for line in range(BR):
-                buf[8 * field + line : 8 * field + line + 1, :] = state[field, pl.ds(low * BR + line, 1), :]
-                buf[8 * field + BR + line : 8 * field + BR + line + 1, :] = state[field, pl.ds(high * BR + line, 1), :]
-    for buf, goal in zip(chip_bufs, goals):
-        beyond = jnp.where(first, jnp.minimum(2 * goal + 2, n - 1), jnp.maximum(2 * goal - 1, 0))
-        halo(buf, 8 * NF, beyond)
-    halo(across, 0, jnp.where(first, 0, n - 1))
+        for buf, (low, high) in zip(chip_bufs, picks):
+            ta = state[field, pl.ds(pl.multiple_of(low // 2 * 8, 8), 8), :]
+            tb = state[field, pl.ds(pl.multiple_of(high // 2 * 8, 8), 8), :]
+            even = jnp.where(low % 2 == 0, ta, turn(ta, 4))
+            odd = jnp.where(high % 2 == 1, tb, turn(tb, 4))
+            buf[8 * field : 8 * field + 8, :] = jnp.where(sub < 4, even, odd)
+    for buf, rim in zip(chip_bufs, rims):
+        halo(buf, 8 * NF, *rim)
+    halo(across, 0, *rims[-1])
     for copy in copies[1 + NF :]:
         copy.wait()
     lane = lax.broadcasted_iota(jnp.int32, (1, width), 1)

time: 21 us -> 20.8 us (level)
  no operation moved by 1% of the time
where the time goes in v9:
time: 20.8 us; the launch traced here: 20.7 us
  starting transfers between devices  8.79 us (42%)
  waiting for transfers between devices  7.52 us (36%)
  Pallas kernels  3.64 us (18%)
  between operations  0.7 us (3%)
    ppermute x6, starting transfers between devices, to_chip(): return lax.ppermute(x, 'bis', links) if path[0] else x  7.64 us
    ppermute x6, waiting for transfers between devices, to_chip(): return lax.ppermute(x, 'bis', links) if path[0] else x  6.36 us
    ppermute x5, waiting for transfers between devices, to_sibling(): return lax.ppermute(x, 'bis', [(i, i ^ 1) for i in range(n)])  1.16 us
    ppermute x5, starting transfers between devices, to_sibling(): return lax.ppermute(x, 'bis', [(i, i ^ 1) for i in range(n)])  1.15 us
    pallas_call x1, Pallas kernels, shards(): pl.pallas_call(functools.partial(pack_kernel, n), out_shape=[jax.ShapeDty...  1.12 us
    pallas_call x1, Pallas kernels, shards(): pl.pallas_call(functools.partial(side_kernel, n), out_shape=[jax.ShapeDty...  0.97 us
    pallas_call x1, Pallas kernels, shards(): pl.pallas_call(functools.partial(land_kernel, n, True), out_shape=[jax.Sh...  0.78 us
    pallas_call x1, Pallas kernels, shards(): pl.pallas_call(functools.partial(step_kernel, n), out_shape=[jax.ShapeDty...  0.65 us
  transfers between devices with their start and end apart: 12, of which 6 were waited for; matrix products, arithmetic and copies ran while one was open for 0% of the time, Pallas kernels for 5%

profile of v9, /device:TPU:0, one launch (start us, length us, event | category | flops | bytes accessed | tf_op | source)
XLA Modules:
  0.0 20.7 jit_solution(5238565665011467387)
XLA Ops:
  0.6 1.1 %pack.1 = (f32[88,512]{1,0:T(8,128)S(1)}, f32[48,512]{1,0:T(8,128)S(1)}, f32[48,512]{1,0:T(8,128)S(1)}, f32[48,512]{1,0:T(8,128)S(1)}, f32[8,512]{1,0:T(8,128)S(1)}) custom-call(s32[8]{0:T(128)} %bitcast.2, s32[8]{0:T(128)} %bitcast.3, s32[8]{0:T(128)} %refs_2_.1, f32[32,512]{1,0:T(8,128)} %refs_11_.1, f32[5,32,512]{2,1,0:T(8,128)} %refs_4_.1), custom_call_target="tpu_custom_call" | custom-call | tf_op jit(solution)/shard_map/pack/pallas_call | solution.py:398
  1.8 4.0 %collective-permute-start.1 = (f32[48,512]{1,0:T(8,128)S(1)}, f32[48,512]{1,0:T(8,128)S(1)}, u32[]{:S(2)}, u32[]{:S(2)}) collective-permute-start(f32[48,512]{1,0:T(8,128)S(1)} %get-tuple-element.22), channel_id=1, source_target_pairs={{0,6},{1,7},{2,4},{3,5},{4,2},{5,3},{6,0},{7,1},{8,14},{9,15},{10,... | collective-permute-start | bytes 294920 | tf_op jit(solution)/shard_map/ppermute | solution.py:392
  5.7 0.5 %collective-permute-start.2 = (f32[48,512]{1,0:T(8,128)S(1)}, f32[48,512]{1,0:T(8,128)S(1)}, u32[]{:S(2)}, u32[]{:S(2)}) collective-permute-start(f32[48,512]{1,0:T(8,128)S(1)} %get-tuple-element.23), channel_id=1, source_target_pairs={{0,2},{1,5},{2,0},{3,7},{4,6},{5,1},{6,4},{7,3},{8,10},{9,13},{10,... | collective-permute-start | bytes 294920 | tf_op jit(solution)/shard_map/ppermute | solution.py:392
  6.3 0.1 collective-permute-start.3
  6.4 0.0 collective-permute-start.7
  6.4 0.5 %collective-permute-start = (f32[88,512]{1,0:T(8,128)S(1)}, f32[88,512]{1,0:T(8,128)S(1)}, u32[]{:S(2)}, u32[]{:S(2)}) collective-permute-start(f32[88,512]{1,0:T(8,128)S(1)} %get-tuple-element.21.own_home.refs_1_.refs_6_), channel_id=1, source_target_pairs={{0,1},{1,0},{2,3},{3,2},{4,5},{5,4},{6,7},{7,6},{8,9},{9,8},{10,11... | collective-permute-start | bytes 540680 | tf_op jit(solution)/shard_map/ppermute | solution.py:388
  6.9 2.0 %collective-permute-done.1.refs_2_.refs_7_ = f32[48,512]{1,0:T(8,128)S(1)} collective-permute-done((f32[48,512]{1,0:T(8,128)S(1)}, f32[48,512]{1,0:T(8,128)S(1)}, u32[]{:S(2)}, u32[]{:S(2)}) %collective-permute-start.1) | collective-permute-done | bytes 98336 | tf_op jit(solution)/shard_map/ppermute | solution.py:392
  8.9 0.0 collective-permute-start.4
  8.9 2.0 %collective-permute-done.2.refs_3_.refs_8_ = f32[48,512]{1,0:T(8,128)S(1)} collective-permute-done((f32[48,512]{1,0:T(8,128)S(1)}, f32[48,512]{1,0:T(8,128)S(1)}, u32[]{:S(2)}, u32[]{:S(2)}) %collective-permute-start.2) | collective-permute-done | bytes 98336 | tf_op jit(solution)/shard_map/ppermute | solution.py:392
  11.0 0.0 collective-permute-start.5
  11.0 0.0 collective-permute-done.3.refs_4_.refs_9_
  11.0 0.5 %collective-permute-start.6 = (f32[48,512]{1,0:T(8,128)S(1)}, f32[48,512]{1,0:T(8,128)S(1)}, u32[]{:S(2)}, u32[]{:S(2)}) collective-permute-start(f32[48,512]{1,0:T(8,128)S(1)} %collective-permute-done.3.refs_4_.refs_9_), channel_id=1, source_target_pairs={{0,1},{1,0},{2,3},{3,2},{4,5},{5,4},{6,7},{7,6},{8,9},{9,8},{10,11... | collective-permute-start | bytes 294920 | tf_op jit(solution)/shard_map/ppermute | solution.py:388
  11.5 0.0 collective-permute-done.7.refs_9_
  11.5 0.0 copy-start
  11.5 0.1 collective-permute-start.8
  11.6 0.0 collective-permute-done.sib_home.refs_5_.refs_10_
  11.7 1.1 %collective-permute-done.8.refs_10_ = f32[32,512]{1,0:T(8,128)S(1)} collective-permute-done((f32[32,512]{1,0:T(8,128)S(1)}, f32[32,512]{1,0:T(8,128)S(1)}, u32[]{:S(2)}, u32[]{:S(2)}) %collective-permute-start.8) | collective-permute-done | bytes 65568 | tf_op jit(solution)/shard_map/ppermute | solution.py:388
  12.8 0.0 collective-permute-done.4.refs_6_.refs_11_
  12.8 0.0 collective-permute-done.5.refs_7_.refs_12_
  12.8 0.0 collective-permute-done.6.refs_8_.refs_13_
  12.8 0.0 copy-done
  12.8 0.6 %substeps.1 = (f32[80,512]{1,0:T(8,128)S(1)}, f32[80,512]{1,0:T(8,128)S(1)}, f32[80,512]{1,0:T(8,128)S(1)}, f32[80,512]{1,0:T(8,128)S(1)}, f32[2,8,8,512]{3,2,1,...) custom-call(s32[2,8,128]{2,1,0:T(8,128)S(1)} %code.1.refs_0_.refs_5_, ...), custom_call_target="tpu_custom_call" | custom-call | tf_op jit(solution)/shard_map/substeps/pallas_call | solution.py:432
  13.5 1.5 %collective-permute-start.9 = (f32[16,8,128]{2,1,0:T(8,128)S(1)}, f32[16,8,128]{2,1,0:T(8,128)S(1)}, u32[]{:S(2)}, u32[]{:S(2)}) collective-permute-start(f32[16,8,128]{2,1,0:T(8,128)S(1)} %get-tuple-element.33), channel_id=1, source_target_pairs={{0,7},{1,6},{2,5},{3,4},{4,3},{5,2},{6,1},{7,0},{8,15},{9,14},{10,... | collective-permute-start | bytes 196616 | tf_op jit(solution)/shard_map/ppermute | solution.py:392
  15.0 0.7 %collective-permute-start.10 = (f32[16,8,128]{2,1,0:T(8,128)S(1)}, f32[16,8,128]{2,1,0:T(8,128)S(1)}, u32[]{:S(2)}, u32[]{:S(2)}) collective-permute-start(f32[16,8,128]{2,1,0:T(8,128)S(1)} %get-tuple-element.34), channel_id=1, source_target_pairs={{0,3},{1,2},{2,1},{3,0},{4,7},{5,6},{6,5},{7,4},{8,11},{9,10},{10,... | collective-permute-start | bytes 196616 | tf_op jit(solution)/shard_map/ppermute | solution.py:392
  15.8 0.8 %collective-permute-start.11 = (f32[16,8,128]{2,1,0:T(8,128)S(1)}, f32[16,8,128]{2,1,0:T(8,128)S(1)}, u32[]{:S(2)}, u32[]{:S(2)}) collective-permute-start(f32[16,8,128]{2,1,0:T(8,128)S(1)} %get-tuple-element.35), channel_id=1, source_target_pairs={{0,5},{1,4},{2,7},{3,6},{4,1},{5,0},{6,3},{7,2},{8,13},{9,12},{10,... | collective-permute-start | bytes 196616 | tf_op jit(solution)/shard_map/ppermute | solution.py:392
  16.5 1.0 %velocities.1 = (f32[2,32,512]{2,1,0:T(8,128)}, f32[16,8,128]{2,1,0:T(8,128)S(1)}, f32[4,8,128]{2,1,0:T(8,128)S(1)}) custom-call(f32[80,512]{1,0:T(8,128)S(1)} %get-tuple-element.26.refs_0_, f32[80,512]{1,0:T(8,128)S(1)} %get-tuple-element.27.refs_1_, f32[80,512]{1,0:T(8,128)S(1)} %get-tuple-element.28.refs_2_, f32[80,512]{1,0:T(8,128)S(1)} %get-tuple-element.29.refs_3_, ...), custom_call_target="tpu_custom_call" | custom-call | tf_op jit(solution)/shard_map/velocities/pallas_call | solution.py:449
  17.5 1.0 %collective-permute-done.9.refs_2_ = f32[16,8,128]{2,1,0:T(8,128)S(1)} collective-permute-done((f32[16,8,128]{2,1,0:T(8,128)S(1)}, f32[16,8,128]{2,1,0:T(8,128)S(1)}, u32[]{:S(2)}, u32[]{:S(2)}) %collective-permute-start.9) | collective-permute-done | bytes 65568 | tf_op jit(solution)/shard_map/ppermute | solution.py:392
  18.5 0.1 sums.1.refs_1_
  18.6 0.8 %collective-permute-done.10.refs_2_ = f32[16,8,128]{2,1,0:T(8,128)S(1)} collective-permute-done((f32[16,8,128]{2,1,0:T(8,128)S(1)}, f32[16,8,128]{2,1,0:T(8,128)S(1)}, u32[]{:S(2)}, u32[]{:S(2)}) %collective-permute-start.10) | collective-permute-done | bytes 65568 | tf_op jit(solution)/shard_map/ppermute | solution.py:392
  19.4 0.5 %collective-permute-done.11.refs_3_ = f32[16,8,128]{2,1,0:T(8,128)S(1)} collective-permute-done((f32[16,8,128]{2,1,0:T(8,128)S(1)}, f32[16,8,128]{2,1,0:T(8,128)S(1)}, u32[]{:S(2)}, u32[]{:S(2)}) %collective-permute-start.11) | collective-permute-done | bytes 65568 | tf_op jit(solution)/shard_map/ppermute | solution.py:392
  19.9 0.8 %land.1 = (f32[32,512]{1,0:T(8,128)}, f32[32,512]{1,0:T(8,128)}) custom-call(f32[4,8,128]{2,1,0:T(8,128)S(1)} %get-tuple-element.31.refs_0_, f32[2,32,512]{2,1,0:T(8,128)S(1)} %sums.1.refs_1_, f32[16,8,128]{2,1,0:T(8,128)S(1)} %collective-permute-done.10.refs_2_, f32[16,8,128]{2,1,0:T(8,128)S(1)} %collective-permute-done.11.refs_3_), custom_call_target="tpu_custom_call" | custom-call | tf_op jit(solution)/shard_map/land/pallas_call | solution.py:471
  (5 shorter events, 0.0 us)
Async XLA Ops:
  1.8 7.1 %collective-permute-start.1 = (f32[48,512]{1,0:T(8,128)S(1)}, f32[48,512]{1,0:T(8,128)S(1)}, u32[]{:S(2)}, u32[]{:S(2)}) collective-permute-start(f32[48,512]{1,0:T(8,128)S(1)} %get-tuple-element.22), channel_id=1, source_target_pairs={{0,6},{1,7},{2,4},{3,5},{4,2},{5,3},{6,0},{7,1},{8,14},{9,15},{10,... | collective-permute-start | bytes 294920 | tf_op jit(solution)/shard_map/ppermute | solution.py:392
  5.7 5.2 %collective-permute-start.2 = (f32[48,512]{1,0:T(8,128)S(1)}, f32[48,512]{1,0:T(8,128)S(1)}, u32[]{:S(2)}, u32[]{:S(2)}) collective-permute-start(f32[48,512]{1,0:T(8,128)S(1)} %get-tuple-element.23), channel_id=1, source_target_pairs={{0,2},{1,5},{2,0},{3,7},{4,6},{5,1},{6,4},{7,3},{8,10},{9,13},{10,... | collective-permute-start | bytes 294920 | tf_op jit(solution)/shard_map/ppermute | solution.py:392
  6.3 4.7 %collective-permute-start.3 = (f32[48,512]{1,0:T(8,128)S(1)}, f32[48,512]{1,0:T(8,128)S(1)}, u32[]{:S(2)}, u32[]{:S(2)}) collective-permute-start(f32[48,512]{1,0:T(8,128)S(1)} %get-tuple-element.24), channel_id=1, source_target_pairs={{0,4},{1,3},{2,6},{3,1},{4,0},{5,7},{6,2},{7,5},{8,12},{9,11},{10,... | collective-permute-start | bytes 294920 | tf_op jit(solution)/shard_map/ppermute | solution.py:392
  6.4 5.1 %collective-permute-start.7 = (f32[8,512]{1,0:T(8,128)S(1)}, f32[8,512]{1,0:T(8,128)S(1)}, u32[]{:S(2)}, u32[]{:S(2)}) collective-permute-start(f32[8,512]{1,0:T(8,128)S(1)} %get-tuple-element.25), channel_id=1, source_target_pairs={{2,3},{3,2},{4,5},{5,4},{7,8},{8,7},{6,14},{14,6},{10,11},{11,10},... | collective-permute-start | bytes 49160 | tf_op jit(solution)/shard_map/ppermute | solution.py:416
  6.4 5.3 %collective-permute-start = (f32[88,512]{1,0:T(8,128)S(1)}, f32[88,512]{1,0:T(8,128)S(1)}, u32[]{:S(2)}, u32[]{:S(2)}) collective-permute-start(f32[88,512]{1,0:T(8,128)S(1)} %get-tuple-element.21.own_home.refs_1_.refs_6_), channel_id=1, source_target_pairs={{0,1},{1,0},{2,3},{3,2},{4,5},{5,4},{6,7},{7,6},{8,9},{9,8},{10,11... | collective-permute-start | bytes 540680 | tf_op jit(solution)/shard_map/ppermute | solution.py:388
  8.9 3.9 %collective-permute-start.4 = (f32[48,512]{1,0:T(8,128)S(1)}, f32[48,512]{1,0:T(8,128)S(1)}, u32[]{:S(2)}, u32[]{:S(2)}) collective-permute-start(f32[48,512]{1,0:T(8,128)S(1)} %collective-permute-done.1.refs_2_.refs_7_), channel_id=1, source_target_pairs={{0,1},{1,0},{2,3},{3,2},{4,5},{5,4},{6,7},{7,6},{8,9},{9,8},{10,11... | collective-permute-start | bytes 294920 | tf_op jit(solution)/shard_map/ppermute | solution.py:388
  11.0 1.9 %collective-permute-start.5 = (f32[48,512]{1,0:T(8,128)S(1)}, f32[48,512]{1,0:T(8,128)S(1)}, u32[]{:S(2)}, u32[]{:S(2)}) collective-permute-start(f32[48,512]{1,0:T(8,128)S(1)} %collective-permute-done.2.refs_3_.refs_8_), channel_id=1, source_target_pairs={{0,1},{1,0},{2,3},{3,2},{4,5},{5,4},{6,7},{7,6},{8,9},{9,8},{10,11... | collective-permute-start | bytes 294920 | tf_op jit(solution)/shard_map/ppermute | solution.py:388
  11.0 1.9 %collective-permute-start.6 = (f32[48,512]{1,0:T(8,128)S(1)}, f32[48,512]{1,0:T(8,128)S(1)}, u32[]{:S(2)}, u32[]{:S(2)}) collective-permute-start(f32[48,512]{1,0:T(8,128)S(1)} %collective-permute-done.3.refs_4_.refs_9_), channel_id=1, source_target_pairs={{0,1},{1,0},{2,3},{3,2},{4,5},{5,4},{6,7},{7,6},{8,9},{9,8},{10,11... | collective-permute-start | bytes 294920 | tf_op jit(solution)/shard_map/ppermute | solution.py:388
  11.5 1.3 %copy-start = (f32[32,512]{1,0:T(8,128)S(1)}, f32[32,512]{1,0:T(8,128)}, u32[]{:S(2)}) copy-start(f32[32,512]{1,0:T(8,128)} %refs_11_.1) | copy-start | bytes 196612
  11.5 1.3 %collective-permute-start.8 = (f32[32,512]{1,0:T(8,128)S(1)}, f32[32,512]{1,0:T(8,128)S(1)}, u32[]{:S(2)}, u32[]{:S(2)}) collective-permute-start(f32[32,512]{1,0:T(8,128)S(1)} %pad_maximum_fusion), channel_id=1, source_target_pairs={{0,1},{1,0},{2,3},{3,2},{4,5},{5,4},{6,7},{7,6},{8,9},{9,8},{10,11... | collective-permute-start | bytes 196616 | tf_op jit(solution)/shard_map/ppermute | solution.py:388
  13.5 5.0 %collective-permute-start.9 = (f32[16,8,128]{2,1,0:T(8,128)S(1)}, f32[16,8,128]{2,1,0:T(8,128)S(1)}, u32[]{:S(2)}, u32[]{:S(2)}) collective-permute-start(f32[16,8,128]{2,1,0:T(8,128)S(1)} %get-tuple-element.33), channel_id=1, source_target_pairs={{0,7},{1,6},{2,5},{3,4},{4,3},{5,2},{6,1},{7,0},{8,15},{9,14},{10,... | collective-permute-start | bytes 196616 | tf_op jit(solution)/shard_map/ppermute | solution.py:392
  15.0 4.4 %collective-permute-start.10 = (f32[16,8,128]{2,1,0:T(8,128)S(1)}, f32[16,8,128]{2,1,0:T(8,128)S(1)}, u32[]{:S(2)}, u32[]{:S(2)}) collective-permute-start(f32[16,8,128]{2,1,0:T(8,128)S(1)} %get-tuple-element.34), channel_id=1, source_target_pairs={{0,3},{1,2},{2,1},{3,0},{4,7},{5,6},{6,5},{7,4},{8,11},{9,10},{10,... | collective-permute-start | bytes 196616 | tf_op jit(solution)/shard_map/ppermute | solution.py:392
  15.8 4.1 %collective-permute-start.11 = (f32[16,8,128]{2,1,0:T(8,128)S(1)}, f32[16,8,128]{2,1,0:T(8,128)S(1)}, u32[]{:S(2)}, u32[]{:S(2)}) collective-permute-start(f32[16,8,128]{2,1,0:T(8,128)S(1)} %get-tuple-element.35), channel_id=1, source_target_pairs={{0,5},{1,4},{2,7},{3,6},{4,1},{5,0},{6,3},{7,2},{8,13},{9,12},{10,... | collective-permute-start | bytes 196616 | tf_op jit(solution)/shard_map/ppermute | solution.py:392

commit v10 on v9

--- a/solution.py
+++ b/solution.py
@@ -45,24 +45,20 @@
     return turn(jnp.where(sub == 0, after, x), 7) - turn(jnp.where(sub == 7, before, x), 1)
 
 
-def target(path, core):
-    return 2 * reached(path, core) + (1 if path[0] else 0)
-
-
 def where_am_i():
     return lax.axis_index("grp"), lax.axis_index("bis")
 
 
-def routes(chips, swapped):
-    bits = chips.bit_length() - 1
-    half = bits // 2 if swapped and bits % 2 == 0 else 0
-    swap = lambda mask: (mask << half | mask >> bits - half) & chips - 1
-    masks = sorted(range(1, chips), key=lambda mask: (-mask.bit_count(), mask))
-    return [(0, 0)] + [(mask, swap(mask)) for mask in masks]
-
-
-def reached(route, core):
-    return route[0] if route[0] == route[1] else jnp.where(core == 0, route[0], route[1])
+def routes(chips):
+    return [0] + sorted(range(1, chips), key=lambda mask: (-mask.bit_count(), mask))
+
+
+def crossed(mask):
+    return 1 if mask.bit_count() == 1 else 0
+
+
+def target(mask):
+    return 2 * mask + crossed(mask)
 
 
 def pack_kernel(n, *refs):
@@ -91,7 +87,7 @@
     chip, core = me // 2, me % 2
     sub = sublane(width)
     first = me == 0
-    goals = [chip ^ reached(route, core) for route in routes(chips, True)]
+    goals = [chip ^ mask for mask in routes(chips)]
     copies[0].wait()
 
     def rim_rows(index):
@@ -161,12 +157,12 @@
     return tile
 
 
-def pack_partials(n, paths, core, code, parts, sends):
+def pack_partials(n, masks, code, parts, sends):
     width = parts.shape[3]
     pieces = width // 128
     lanes = [slice(piece * 128, piece * 128 + 128) for piece in range(pieces)]
     for device in range(2):
-        wants = [target(path, core) * (2 * CAP) + device * CAP + again for path in paths for again in range(CAP)]
+        wants = [target(mask) * (2 * CAP) + device * CAP + again for mask in masks for again in range(CAP)]
         found = [[jnp.zeros((8, 128), jnp.float32)] * pieces for _ in wants]
         for block in range(n):
             taken = jnp.broadcast_to(code[device, block : block + 1, :], (8, 128))
@@ -204,9 +200,11 @@
     def pair(own, sib):
         return jnp.where(is_low, own, sib), jnp.where(is_low, sib, own)
 
-    for index, path in enumerate(routes(chips, True)):
-        source = chip ^ reached(path, core)
-        own, sib = mine[index], theirs[routes(chips, True).index((path[1], path[0]))]
+    for index, mask in enumerate(routes(chips)):
+        source = chip ^ mask
+        own, sib = mine[index], theirs[index]
+        if crossed(mask):
+            own, sib = sib, own
         for field in range(NF):
             span = pl.ds(8 * field, 8)
             even, odd = pair(own[span, :], sib[span, :])
@@ -283,7 +281,7 @@
     for device in range(2):
         lax.fori_loop(0, chips, lambda index, _, device=device: (second(device, index), 0)[1], 0, unroll=n <= 8)
 
-    pack_partials(n, routes(chips, False)[1:], core, code, parts, sends)
+    pack_partials(n, routes(chips)[1:], code, parts, sends)
 
 
 def side_kernel(n, *refs):
@@ -293,14 +291,13 @@
     vel, home, labels = refs[6 + 2 * chips :]
     _, me = where_am_i()
     core = me % 2
-    pack_partials(n, routes(chips, False)[:1], core, code, parts, [home])
-    paths = routes(chips, True)
+    pack_partials(n, routes(chips)[:1], code, parts, [home])
     line = slice(8 * NF + INFO, 8 * NF + INFO + 1)
-    for index, (mask, _) in enumerate(routes(chips, False)):
-        low, high = [path[0] for path in paths].index(mask), [path[1] for path in paths].index(mask)
-        even = jnp.where(core == 0, mine[low][line, :], theirs[low][line, :])
-        odd = jnp.where(core == 0, theirs[high][line, :], mine[high][line, :])
-        labels[index] = labels_of(n, me, (even, odd))
+    for index, mask in enumerate(routes(chips)):
+        own, sib = mine[index][line, :], theirs[index][line, :]
+        if crossed(mask):
+            own, sib = sib, own
+        labels[index] = labels_of(n, me, (jnp.where(core == 0, own, sib), jnp.where(core == 0, sib, own)))
 
     def one(index, _):
         tile = 1 + core * chips + index
@@ -387,12 +384,10 @@
     def to_sibling(x):
         return lax.ppermute(x, "bis", [(i, i ^ 1) for i in range(n)])
 
-    def to_chip(x, path, cross):
-        links = [(i, i ^ 2 * path[i % 2] ^ cross) for i in range(n)]
-        return lax.ppermute(x, "bis", links) if path[0] else x
-
-    paths = routes(chips, True)
-
+    def to_chip(x, mask):
+        return lax.ppermute(x, "bis", [(i, i ^ target(mask)) for i in range(n)]) if mask else x
+
+    masks = routes(chips)
     owner = owner.reshape(n)
     extra = -(-(rows + n) // 8) * 8
     packed = pl.pallas_call(
@@ -414,7 +409,7 @@
         name="pack",
     )(*[pltpu.with_memory_space_constraint(x, pltpu.HBM) for x in (order.reshape(n), owner, slot_target, sweep, state)])
     across = lax.ppermute(packed[chips], ("grp", "bis"), across_links(groups, n))
-    mine = [to_chip(x, path, 0) for x, path in zip(packed, paths)]
+    mine = [to_chip(x, mask) for x, mask in zip(packed, masks)]
     theirs = [to_sibling(x) for x in mine]
     across_sib = to_sibling(jnp.concatenate([across] + [x[0:8] for x in mine[1:]]))
 
@@ -445,7 +440,7 @@
         compiler_params=params,
         name="substeps",
     )(code, *mine, *theirs, across, across_sib, sweep)
-    arrived = [to_chip(x, path, 1) for x, path in zip(out[5:], routes(chips, False)[1:])]
+    arrived = [to_chip(x, mask) for x, mask in zip(out[5:], masks[1:])]
     vel, home, labels = pl.pallas_call(
         functools.partial(side_kernel, n),
         out_shape=[

time: 20.8 us -> 20.6 us (level)
  waiting for transfers between devices: 7.52 us -> 7.24 us
    ppermute x1, starting transfers between devices: 0.01 us -> 0.29 us  [shards(): lax.ppermute(packed[chips], ('grp', 'bis'), across_links(groups, n))]
    ppermute x6, waiting for transfers between devices: 6.36 us -> 6.11 us  [to_chip(): lax.ppermute(x, 'bis', [(i, i ^ target(mask)) for i in range(n)])]
    ppermute x5, starting transfers between devices: 1.15 us -> 0.91 us  [to_sibling(): return lax.ppermute(x, 'bis', [(i, i ^ 1) for i in range(n)])]
  transfers between devices with their start and end apart: 12 -> 12, of which waited for: 6 -> 5; matrix products, arithmetic and copies ran while one was open for 0% -> 0% of each run, Pallas kernels for 5% -> 5%
where the time goes in v10:
time: 20.6 us; the launch traced here: 20.4 us
  starting transfers between devices  8.8 us (43%)
  waiting for transfers between devices  7.24 us (35%)
  Pallas kernels  3.63 us (18%)
  between operations  0.69 us (3%)
    ppermute x6, starting transfers between devices, to_chip(): lax.ppermute(x, 'bis', [(i, i ^ target(mask)) for i in range(n)])  7.6 us
    ppermute x6, waiting for transfers between devices, to_chip(): lax.ppermute(x, 'bis', [(i, i ^ target(mask)) for i in range(n)])  6.11 us
    pallas_call x1, Pallas kernels, shards(): pl.pallas_call(functools.partial(pack_kernel, n), out_shape=[jax.ShapeDty...  1.12 us
    ppermute x5, waiting for transfers between devices, to_sibling(): return lax.ppermute(x, 'bis', [(i, i ^ 1) for i in range(n)])  1.12 us
    pallas_call x1, Pallas kernels, shards(): pl.pallas_call(functools.partial(side_kernel, n), out_shape=[jax.ShapeDty...  0.97 us
    ppermute x5, starting transfers between devices, to_sibling(): return lax.ppermute(x, 'bis', [(i, i ^ 1) for i in range(n)])  0.91 us
    pallas_call x1, Pallas kernels, shards(): pl.pallas_call(functools.partial(land_kernel, n, True), out_shape=[jax.Sh...  0.78 us
    pallas_call x1, Pallas kernels, shards(): pl.pallas_call(functools.partial(step_kernel, n), out_shape=[jax.ShapeDty...  0.65 us
  transfers between devices with their start and end apart: 12, of which 5 were waited for; matrix products, arithmetic and copies ran while one was open for 0% of the time, Pallas kernels for 5%

profile of v10, /device:TPU:0, one launch (start us, length us, event | category | flops | bytes accessed | tf_op | source)
XLA Modules:
  0.0 20.4 jit_solution(820306478934192088)
XLA Ops:
  0.6 1.1 %pack.1 = (f32[88,512]{1,0:T(8,128)S(1)}, f32[48,512]{1,0:T(8,128)S(1)}, f32[48,512]{1,0:T(8,128)S(1)}, f32[48,512]{1,0:T(8,128)S(1)}, f32[8,512]{1,0:T(8,128)S(1)}) custom-call(s32[8]{0:T(128)} %bitcast.2, s32[8]{0:T(128)} %bitcast.3, s32[8]{0:T(128)} %refs_2_.1, f32[32,512]{1,0:T(8,128)} %refs_11_.1, f32[5,32,512]{2,1,0:T(8,128)} %refs_4_.1), custom_call_target="tpu_custom_call" | custom-call | tf_op jit(solution)/shard_map/pack/pallas_call | solution.py:393
  1.8 4.0 %collective-permute-start.1 = (f32[48,512]{1,0:T(8,128)S(1)}, f32[48,512]{1,0:T(8,128)S(1)}, u32[]{:S(2)}, u32[]{:S(2)}) collective-permute-start(f32[48,512]{1,0:T(8,128)S(1)} %get-tuple-element.22), channel_id=1, source_target_pairs={{0,6},{1,7},{2,4},{3,5},{4,2},{5,3},{6,0},{7,1},{8,14},{9,15},{10,... | collective-permute-start | bytes 294920 | tf_op jit(solution)/shard_map/ppermute | solution.py:388
  5.7 0.0 collective-permute-start.2
  5.7 0.4 %collective-permute-start.3 = (f32[48,512]{1,0:T(8,128)S(1)}, f32[48,512]{1,0:T(8,128)S(1)}, u32[]{:S(2)}, u32[]{:S(2)}) collective-permute-start(f32[48,512]{1,0:T(8,128)S(1)} %get-tuple-element.24), channel_id=1, source_target_pairs={{0,5},{1,4},{2,7},{3,6},{4,1},{5,0},{6,3},{7,2},{8,13},{9,12},{10,... | collective-permute-start | bytes 294920 | tf_op jit(solution)/shard_map/ppermute | solution.py:388
  6.1 0.3 %collective-permute-start.7 = (f32[8,512]{1,0:T(8,128)S(1)}, f32[8,512]{1,0:T(8,128)S(1)}, u32[]{:S(2)}, u32[]{:S(2)}) collective-permute-start(f32[8,512]{1,0:T(8,128)S(1)} %get-tuple-element.25), channel_id=1, source_target_pairs={{2,3},{3,2},{4,5},{5,4},{7,8},{8,7},{6,14},{14,6},{10,11},{11,10},... | collective-permute-start | bytes 49160 | tf_op jit(solution)/shard_map/ppermute | solution.py:411
  6.4 0.2 %collective-permute-start = (f32[88,512]{1,0:T(8,128)S(1)}, f32[88,512]{1,0:T(8,128)S(1)}, u32[]{:S(2)}, u32[]{:S(2)}) collective-permute-start(f32[88,512]{1,0:T(8,128)S(1)} %get-tuple-element.21.own_home.refs_1_.refs_6_), channel_id=1, source_target_pairs={{0,1},{1,0},{2,3},{3,2},{4,5},{5,4},{6,7},{7,6},{8,9},{9,8},{10,11... | collective-permute-start | bytes 540680 | tf_op jit(solution)/shard_map/ppermute | solution.py:385
  6.6 2.3 %collective-permute-done.1.refs_2_.refs_7_ = f32[48,512]{1,0:T(8,128)S(1)} collective-permute-done((f32[48,512]{1,0:T(8,128)S(1)}, f32[48,512]{1,0:T(8,128)S(1)}, u32[]{:S(2)}, u32[]{:S(2)}) %collective-permute-start.1) | collective-permute-done | bytes 98336 | tf_op jit(solution)/shard_map/ppermute | solution.py:388
  8.9 0.0 collective-permute-start.4
  8.9 1.9 %collective-permute-done.2.refs_3_.refs_8_ = f32[48,512]{1,0:T(8,128)S(1)} collective-permute-done((f32[48,512]{1,0:T(8,128)S(1)}, f32[48,512]{1,0:T(8,128)S(1)}, u32[]{:S(2)}, u32[]{:S(2)}) %collective-permute-start.2) | collective-permute-done | bytes 98336 | tf_op jit(solution)/shard_map/ppermute | solution.py:388
  10.8 0.1 collective-permute-start.5
  10.9 0.0 collective-permute-done.3.refs_4_.refs_9_
  10.9 0.4 %collective-permute-start.6 = (f32[48,512]{1,0:T(8,128)S(1)}, f32[48,512]{1,0:T(8,128)S(1)}, u32[]{:S(2)}, u32[]{:S(2)}) collective-permute-start(f32[48,512]{1,0:T(8,128)S(1)} %collective-permute-done.3.refs_4_.refs_9_), channel_id=1, source_target_pairs={{0,1},{1,0},{2,3},{3,2},{4,5},{5,4},{6,7},{7,6},{8,9},{9,8},{10,11... | collective-permute-start | bytes 294920 | tf_op jit(solution)/shard_map/ppermute | solution.py:385
  11.3 0.0 collective-permute-done.7.refs_9_
  11.3 0.0 copy-start
  11.3 0.2 collective-permute-start.8
  11.5 0.0 collective-permute-done.sib_home.refs_5_.refs_10_
  11.6 1.1 %collective-permute-done.8.refs_10_ = f32[32,512]{1,0:T(8,128)S(1)} collective-permute-done((f32[32,512]{1,0:T(8,128)S(1)}, f32[32,512]{1,0:T(8,128)S(1)}, u32[]{:S(2)}, u32[]{:S(2)}) %collective-permute-start.8) | collective-permute-done | bytes 65568 | tf_op jit(solution)/shard_map/ppermute | solution.py:385
  12.7 0.0 collective-permute-done.4.refs_6_.refs_11_
  12.7 0.0 collective-permute-done.5.refs_7_.refs_12_
  12.7 0.0 collective-permute-done.6.refs_8_.refs_13_
  12.7 0.0 copy-done
  12.7 0.6 %substeps.1 = (f32[80,512]{1,0:T(8,128)S(1)}, f32[80,512]{1,0:T(8,128)S(1)}, f32[80,512]{1,0:T(8,128)S(1)}, f32[80,512]{1,0:T(8,128)S(1)}, f32[2,8,8,512]{3,2,1,...) custom-call(s32[2,8,128]{2,1,0:T(8,128)S(1)} %code.1.refs_0_.refs_5_, ...), custom_call_target="tpu_custom_call" | custom-call | tf_op jit(solution)/shard_map/substeps/pallas_call | solution.py:427
  13.3 1.9 %collective-permute-start.9 = (f32[16,8,128]{2,1,0:T(8,128)S(1)}, f32[16,8,128]{2,1,0:T(8,128)S(1)}, u32[]{:S(2)}, u32[]{:S(2)}) collective-permute-start(f32[16,8,128]{2,1,0:T(8,128)S(1)} %get-tuple-element.33), channel_id=1, source_target_pairs={{0,6},{1,7},{2,4},{3,5},{4,2},{5,3},{6,0},{7,1},{8,14},{9,15},{10,... | collective-permute-start | bytes 196616 | tf_op jit(solution)/shard_map/ppermute | solution.py:388
  15.2 0.4 %collective-permute-start.10 = (f32[16,8,128]{2,1,0:T(8,128)S(1)}, f32[16,8,128]{2,1,0:T(8,128)S(1)}, u32[]{:S(2)}, u32[]{:S(2)}) collective-permute-start(f32[16,8,128]{2,1,0:T(8,128)S(1)} %get-tuple-element.34), channel_id=1, source_target_pairs={{0,3},{1,2},{2,1},{3,0},{4,7},{5,6},{6,5},{7,4},{8,11},{9,10},{10,... | collective-permute-start | bytes 196616 | tf_op jit(solution)/shard_map/ppermute | solution.py:388
  15.7 0.9 %collective-permute-start.11 = (f32[16,8,128]{2,1,0:T(8,128)S(1)}, f32[16,8,128]{2,1,0:T(8,128)S(1)}, u32[]{:S(2)}, u32[]{:S(2)}) collective-permute-start(f32[16,8,128]{2,1,0:T(8,128)S(1)} %get-tuple-element.35), channel_id=1, source_target_pairs={{0,5},{1,4},{2,7},{3,6},{4,1},{5,0},{6,3},{7,2},{8,13},{9,12},{10,... | collective-permute-start | bytes 196616 | tf_op jit(solution)/shard_map/ppermute | solution.py:388
  16.6 1.0 %velocities.1 = (f32[2,32,512]{2,1,0:T(8,128)}, f32[16,8,128]{2,1,0:T(8,128)S(1)}, f32[4,8,128]{2,1,0:T(8,128)S(1)}) custom-call(f32[80,512]{1,0:T(8,128)S(1)} %get-tuple-element.26.refs_0_, f32[80,512]{1,0:T(8,128)S(1)} %get-tuple-element.27.refs_1_, f32[80,512]{1,0:T(8,128)S(1)} %get-tuple-element.28.refs_2_, f32[80,512]{1,0:T(8,128)S(1)} %get-tuple-element.29.refs_3_, ...), custom_call_target="tpu_custom_call" | custom-call | tf_op jit(solution)/shard_map/velocities/pallas_call | solution.py:444
  17.6 1.1 %collective-permute-done.9.refs_2_ = f32[16,8,128]{2,1,0:T(8,128)S(1)} collective-permute-done((f32[16,8,128]{2,1,0:T(8,128)S(1)}, f32[16,8,128]{2,1,0:T(8,128)S(1)}, u32[]{:S(2)}, u32[]{:S(2)}) %collective-permute-start.9) | collective-permute-done | bytes 65568 | tf_op jit(solution)/shard_map/ppermute | solution.py:388
  18.7 0.1 sums.1.refs_1_
  18.8 0.8 %collective-permute-done.10.refs_2_ = f32[16,8,128]{2,1,0:T(8,128)S(1)} collective-permute-done((f32[16,8,128]{2,1,0:T(8,128)S(1)}, f32[16,8,128]{2,1,0:T(8,128)S(1)}, u32[]{:S(2)}, u32[]{:S(2)}) %collective-permute-start.10) | collective-permute-done | bytes 65568 | tf_op jit(solution)/shard_map/ppermute | solution.py:388
  19.6 0.0 collective-permute-done.11.refs_3_
  19.6 0.8 %land.1 = (f32[32,512]{1,0:T(8,128)}, f32[32,512]{1,0:T(8,128)}) custom-call(f32[4,8,128]{2,1,0:T(8,128)S(1)} %get-tuple-element.31.refs_0_, f32[2,32,512]{2,1,0:T(8,128)S(1)} %sums.1.refs_1_, f32[16,8,128]{2,1,0:T(8,128)S(1)} %collective-permute-done.10.refs_2_, f32[16,8,128]{2,1,0:T(8,128)S(1)} %collective-permute-done.11.refs_3_), custom_call_target="tpu_custom_call" | custom-call | tf_op jit(solution)/shard_map/land/pallas_call | solution.py:466
  (5 shorter events, 0.0 us)
Async XLA Ops:
  1.8 7.1 %collective-permute-start.1 = (f32[48,512]{1,0:T(8,128)S(1)}, f32[48,512]{1,0:T(8,128)S(1)}, u32[]{:S(2)}, u32[]{:S(2)}) collective-permute-start(f32[48,512]{1,0:T(8,128)S(1)} %get-tuple-element.22), channel_id=1, source_target_pairs={{0,6},{1,7},{2,4},{3,5},{4,2},{5,3},{6,0},{7,1},{8,14},{9,15},{10,... | collective-permute-start | bytes 294920 | tf_op jit(solution)/shard_map/ppermute | solution.py:388
  5.7 5.1 %collective-permute-start.2 = (f32[48,512]{1,0:T(8,128)S(1)}, f32[48,512]{1,0:T(8,128)S(1)}, u32[]{:S(2)}, u32[]{:S(2)}) collective-permute-start(f32[48,512]{1,0:T(8,128)S(1)} %get-tuple-element.23), channel_id=1, source_target_pairs={{0,3},{1,2},{2,1},{3,0},{4,7},{5,6},{6,5},{7,4},{8,11},{9,10},{10,... | collective-permute-start | bytes 294920 | tf_op jit(solution)/shard_map/ppermute | solution.py:388
  5.7 5.2 %collective-permute-start.3 = (f32[48,512]{1,0:T(8,128)S(1)}, f32[48,512]{1,0:T(8,128)S(1)}, u32[]{:S(2)}, u32[]{:S(2)}) collective-permute-start(f32[48,512]{1,0:T(8,128)S(1)} %get-tuple-element.24), channel_id=1, source_target_pairs={{0,5},{1,4},{2,7},{3,6},{4,1},{5,0},{6,3},{7,2},{8,13},{9,12},{10,... | collective-permute-start | bytes 294920 | tf_op jit(solution)/shard_map/ppermute | solution.py:388
  6.1 5.2 %collective-permute-start.7 = (f32[8,512]{1,0:T(8,128)S(1)}, f32[8,512]{1,0:T(8,128)S(1)}, u32[]{:S(2)}, u32[]{:S(2)}) collective-permute-start(f32[8,512]{1,0:T(8,128)S(1)} %get-tuple-element.25), channel_id=1, source_target_pairs={{2,3},{3,2},{4,5},{5,4},{7,8},{8,7},{6,14},{14,6},{10,11},{11,10},... | collective-permute-start | bytes 49160 | tf_op jit(solution)/shard_map/ppermute | solution.py:411
  6.4 5.2 %collective-permute-start = (f32[88,512]{1,0:T(8,128)S(1)}, f32[88,512]{1,0:T(8,128)S(1)}, u32[]{:S(2)}, u32[]{:S(2)}) collective-permute-start(f32[88,512]{1,0:T(8,128)S(1)} %get-tuple-element.21.own_home.refs_1_.refs_6_), channel_id=1, source_target_pairs={{0,1},{1,0},{2,3},{3,2},{4,5},{5,4},{6,7},{7,6},{8,9},{9,8},{10,11... | collective-permute-start | bytes 540680 | tf_op jit(solution)/shard_map/ppermute | solution.py:385
  8.9 3.8 %collective-permute-start.4 = (f32[48,512]{1,0:T(8,128)S(1)}, f32[48,512]{1,0:T(8,128)S(1)}, u32[]{:S(2)}, u32[]{:S(2)}) collective-permute-start(f32[48,512]{1,0:T(8,128)S(1)} %collective-permute-done.1.refs_2_.refs_7_), channel_id=1, source_target_pairs={{0,1},{1,0},{2,3},{3,2},{4,5},{5,4},{6,7},{7,6},{8,9},{9,8},{10,11... | collective-permute-start | bytes 294920 | tf_op jit(solution)/shard_map/ppermute | solution.py:385
  10.8 1.9 %collective-permute-start.5 = (f32[48,512]{1,0:T(8,128)S(1)}, f32[48,512]{1,0:T(8,128)S(1)}, u32[]{:S(2)}, u32[]{:S(2)}) collective-permute-start(f32[48,512]{1,0:T(8,128)S(1)} %collective-permute-done.2.refs_3_.refs_8_), channel_id=1, source_target_pairs={{0,1},{1,0},{2,3},{3,2},{4,5},{5,4},{6,7},{7,6},{8,9},{9,8},{10,11... | collective-permute-start | bytes 294920 | tf_op jit(solution)/shard_map/ppermute | solution.py:385
  10.9 1.7 %collective-permute-start.6 = (f32[48,512]{1,0:T(8,128)S(1)}, f32[48,512]{1,0:T(8,128)S(1)}, u32[]{:S(2)}, u32[]{:S(2)}) collective-permute-start(f32[48,512]{1,0:T(8,128)S(1)} %collective-permute-done.3.refs_4_.refs_9_), channel_id=1, source_target_pairs={{0,1},{1,0},{2,3},{3,2},{4,5},{5,4},{6,7},{7,6},{8,9},{9,8},{10,11... | collective-permute-start | bytes 294920 | tf_op jit(solution)/shard_map/ppermute | solution.py:385
  11.3 1.3 %copy-start = (f32[32,512]{1,0:T(8,128)S(1)}, f32[32,512]{1,0:T(8,128)}, u32[]{:S(2)}) copy-start(f32[32,512]{1,0:T(8,128)} %refs_11_.1) | copy-start | bytes 196612
  11.3 1.3 %collective-permute-start.8 = (f32[32,512]{1,0:T(8,128)S(1)}, f32[32,512]{1,0:T(8,128)S(1)}, u32[]{:S(2)}, u32[]{:S(2)}) collective-permute-start(f32[32,512]{1,0:T(8,128)S(1)} %pad_maximum_fusion), channel_id=1, source_target_pairs={{0,1},{1,0},{2,3},{3,2},{4,5},{5,4},{6,7},{7,6},{8,9},{9,8},{10,11... | collective-permute-start | bytes 196616 | tf_op jit(solution)/shard_map/ppermute | solution.py:385
  13.3 5.3 %collective-permute-start.9 = (f32[16,8,128]{2,1,0:T(8,128)S(1)}, f32[16,8,128]{2,1,0:T(8,128)S(1)}, u32[]{:S(2)}, u32[]{:S(2)}) collective-permute-start(f32[16,8,128]{2,1,0:T(8,128)S(1)} %get-tuple-element.33), channel_id=1, source_target_pairs={{0,6},{1,7},{2,4},{3,5},{4,2},{5,3},{6,0},{7,1},{8,14},{9,15},{10,... | collective-permute-start | bytes 196616 | tf_op jit(solution)/shard_map/ppermute | solution.py:388
  15.2 4.3 %collective-permute-start.10 = (f32[16,8,128]{2,1,0:T(8,128)S(1)}, f32[16,8,128]{2,1,0:T(8,128)S(1)}, u32[]{:S(2)}, u32[]{:S(2)}) collective-permute-start(f32[16,8,128]{2,1,0:T(8,128)S(1)} %get-tuple-element.34), channel_id=1, source_target_pairs={{0,3},{1,2},{2,1},{3,0},{4,7},{5,6},{6,5},{7,4},{8,11},{9,10},{10,... | collective-permute-start | bytes 196616 | tf_op jit(solution)/shard_map/ppermute | solution.py:388
  15.7 3.9 %collective-permute-start.11 = (f32[16,8,128]{2,1,0:T(8,128)S(1)}, f32[16,8,128]{2,1,0:T(8,128)S(1)}, u32[]{:S(2)}, u32[]{:S(2)}) collective-permute-start(f32[16,8,128]{2,1,0:T(8,128)S(1)} %get-tuple-element.35), channel_id=1, source_target_pairs={{0,5},{1,4},{2,7},{3,6},{4,1},{5,0},{6,3},{7,2},{8,13},{9,12},{10,... | collective-permute-start | bytes 196616 | tf_op jit(solution)/shard_map/ppermute | solution.py:388

commit v11 on v10

--- a/solution.py
+++ b/solution.py
@@ -205,11 +205,16 @@
         own, sib = mine[index], theirs[index]
         if crossed(mask):
             own, sib = sib, own
+        placed = (at(1 + source), at(1 + chips + source))
+        blocks = []
         for field in range(NF):
             span = pl.ds(8 * field, 8)
             even, odd = pair(own[span, :], sib[span, :])
-            fld[field, at(1 + source), :] = jnp.where(sub < 4, even, turn(odd, 4))
-            fld[field, at(1 + chips + source), :] = jnp.where(sub < 4, turn(even, 4), odd)
+            blocks.append((jnp.where(sub < 4, even, turn(odd, 4)), jnp.where(sub < 4, turn(even, 4), odd)))
+            for where_to, block in zip(placed, blocks[field]):
+                fld[field, where_to, :] = block
+        for device, where_to in enumerate(placed):
+            prs[where_to, :] = (blocks[GAM][device] - 1.0) * blocks[RHO][device] * blocks[ENE][device]
         even, odd = pair(own[8 * NF : home, :], sib[8 * NF : home, :])
         halo[0, source] = even
         halo[1, source] = odd
@@ -229,13 +234,6 @@
         fld[VELU, span, :] = jnp.where(sub == near, line(tile, VELU), line(tile, FAR_U))
         press = (line(tile, GAM) - 1.0) * line(tile, RHO) * line(tile, ENE)
         prs[span, :] = jnp.where(sub == near, press, line(tile, FAR_P))
-
-    def pressure(tile, _):
-        span = at(tile)
-        prs[span, :] = (fld[GAM, span, :] - 1.0) * fld[RHO, span, :] * fld[ENE, span, :]
-        return 0
-
-    lax.fori_loop(1, tiles + 1, pressure, 0, unroll=n <= 8)
 
     def first(tile, _):
         span = at(tile)

time: 20.6 us -> 20.5 us (level)
  no operation moved by 1% of the time
where the time goes in v11:
time: 20.5 us; the launch traced here: 20.4 us
  starting transfers between devices  8.8 us (43%)
  waiting for transfers between devices  7.23 us (35%)
  Pallas kernels  3.62 us (18%)
  between operations  0.69 us (3%)
    ppermute x6, starting transfers between devices, to_chip(): lax.ppermute(x, 'bis', [(i, i ^ target(mask)) for i in range(n)])  7.6 us
    ppermute x6, waiting for transfers between devices, to_chip(): lax.ppermute(x, 'bis', [(i, i ^ target(mask)) for i in range(n)])  6.11 us
    pallas_call x1, Pallas kernels, shards(): pl.pallas_call(functools.partial(pack_kernel, n), out_shape=[jax.ShapeDty...  1.12 us
    ppermute x5, waiting for transfers between devices, to_sibling(): return lax.ppermute(x, 'bis', [(i, i ^ 1) for i in range(n)])  1.12 us
    pallas_call x1, Pallas kernels, shards(): pl.pallas_call(functools.partial(side_kernel, n), out_shape=[jax.ShapeDty...  0.97 us
    ppermute x5, starting transfers between devices, to_sibling(): return lax.ppermute(x, 'bis', [(i, i ^ 1) for i in range(n)])  0.91 us
    pallas_call x1, Pallas kernels, shards(): pl.pallas_call(functools.partial(land_kernel, n, True), out_shape=[jax.Sh...  0.78 us
    pallas_call x1, Pallas kernels, shards(): pl.pallas_call(functools.partial(step_kernel, n), out_shape=[jax.ShapeDty...  0.63 us
  transfers between devices with their start and end apart: 12, of which 5 were waited for; matrix products, arithmetic and copies ran while one was open for 0% of the time, Pallas kernels for 5%

profile of v11, /device:TPU:0, one launch (start us, length us, event | category | flops | bytes accessed | tf_op | source)
XLA Modules:
  0.0 20.4 jit_solution(287609884647600897)
XLA Ops:
  0.6 1.1 %pack.1 = (f32[88,512]{1,0:T(8,128)S(1)}, f32[48,512]{1,0:T(8,128)S(1)}, f32[48,512]{1,0:T(8,128)S(1)}, f32[48,512]{1,0:T(8,128)S(1)}, f32[8,512]{1,0:T(8,128)S(1)}) custom-call(s32[8]{0:T(128)} %bitcast.2, s32[8]{0:T(128)} %bitcast.3, s32[8]{0:T(128)} %refs_2_.1, f32[32,512]{1,0:T(8,128)} %refs_11_.1, f32[5,32,512]{2,1,0:T(8,128)} %refs_4_.1), custom_call_target="tpu_custom_call" | custom-call | tf_op jit(solution)/shard_map/pack/pallas_call | solution.py:391
  1.8 4.0 %collective-permute-start.1 = (f32[48,512]{1,0:T(8,128)S(1)}, f32[48,512]{1,0:T(8,128)S(1)}, u32[]{:S(2)}, u32[]{:S(2)}) collective-permute-start(f32[48,512]{1,0:T(8,128)S(1)} %get-tuple-element.22), channel_id=1, source_target_pairs={{0,6},{1,7},{2,4},{3,5},{4,2},{5,3},{6,0},{7,1},{8,14},{9,15},{10,... | collective-permute-start | bytes 294920 | tf_op jit(solution)/shard_map/ppermute | solution.py:386
  5.7 0.0 collective-permute-start.2
  5.7 0.4 %collective-permute-start.3 = (f32[48,512]{1,0:T(8,128)S(1)}, f32[48,512]{1,0:T(8,128)S(1)}, u32[]{:S(2)}, u32[]{:S(2)}) collective-permute-start(f32[48,512]{1,0:T(8,128)S(1)} %get-tuple-element.24), channel_id=1, source_target_pairs={{0,5},{1,4},{2,7},{3,6},{4,1},{5,0},{6,3},{7,2},{8,13},{9,12},{10,... | collective-permute-start | bytes 294920 | tf_op jit(solution)/shard_map/ppermute | solution.py:386
  6.1 0.3 %collective-permute-start.7 = (f32[8,512]{1,0:T(8,128)S(1)}, f32[8,512]{1,0:T(8,128)S(1)}, u32[]{:S(2)}, u32[]{:S(2)}) collective-permute-start(f32[8,512]{1,0:T(8,128)S(1)} %get-tuple-element.25), channel_id=1, source_target_pairs={{2,3},{3,2},{4,5},{5,4},{7,8},{8,7},{6,14},{14,6},{10,11},{11,10},... | collective-permute-start | bytes 49160 | tf_op jit(solution)/shard_map/ppermute | solution.py:409
  6.4 0.2 %collective-permute-start = (f32[88,512]{1,0:T(8,128)S(1)}, f32[88,512]{1,0:T(8,128)S(1)}, u32[]{:S(2)}, u32[]{:S(2)}) collective-permute-start(f32[88,512]{1,0:T(8,128)S(1)} %get-tuple-element.21.own_home.refs_1_.refs_6_), channel_id=1, source_target_pairs={{0,1},{1,0},{2,3},{3,2},{4,5},{5,4},{6,7},{7,6},{8,9},{9,8},{10,11... | collective-permute-start | bytes 540680 | tf_op jit(solution)/shard_map/ppermute | solution.py:383
  6.6 2.3 %collective-permute-done.1.refs_2_.refs_7_ = f32[48,512]{1,0:T(8,128)S(1)} collective-permute-done((f32[48,512]{1,0:T(8,128)S(1)}, f32[48,512]{1,0:T(8,128)S(1)}, u32[]{:S(2)}, u32[]{:S(2)}) %collective-permute-start.1) | collective-permute-done | bytes 98336 | tf_op jit(solution)/shard_map/ppermute | solution.py:386
  8.9 0.0 collective-permute-start.4
  8.9 1.9 %collective-permute-done.2.refs_3_.refs_8_ = f32[48,512]{1,0:T(8,128)S(1)} collective-permute-done((f32[48,512]{1,0:T(8,128)S(1)}, f32[48,512]{1,0:T(8,128)S(1)}, u32[]{:S(2)}, u32[]{:S(2)}) %collective-permute-start.2) | collective-permute-done | bytes 98336 | tf_op jit(solution)/shard_map/ppermute | solution.py:386
  10.8 0.1 collective-permute-start.5
  10.9 0.0 collective-permute-done.3.refs_4_.refs_9_
  10.9 0.4 %collective-permute-start.6 = (f32[48,512]{1,0:T(8,128)S(1)}, f32[48,512]{1,0:T(8,128)S(1)}, u32[]{:S(2)}, u32[]{:S(2)}) collective-permute-start(f32[48,512]{1,0:T(8,128)S(1)} %collective-permute-done.3.refs_4_.refs_9_), channel_id=1, source_target_pairs={{0,1},{1,0},{2,3},{3,2},{4,5},{5,4},{6,7},{7,6},{8,9},{9,8},{10,11... | collective-permute-start | bytes 294920 | tf_op jit(solution)/shard_map/ppermute | solution.py:383
  11.3 0.0 collective-permute-done.7.refs_9_
  11.3 0.0 copy-start
  11.3 0.2 collective-permute-start.8
  11.5 0.0 collective-permute-done.sib_home.refs_5_.refs_10_
  11.6 1.1 %collective-permute-done.8.refs_10_ = f32[32,512]{1,0:T(8,128)S(1)} collective-permute-done((f32[32,512]{1,0:T(8,128)S(1)}, f32[32,512]{1,0:T(8,128)S(1)}, u32[]{:S(2)}, u32[]{:S(2)}) %collective-permute-start.8) | collective-permute-done | bytes 65568 | tf_op jit(solution)/shard_map/ppermute | solution.py:383
  12.7 0.0 collective-permute-done.4.refs_6_.refs_11_
  12.7 0.0 collective-permute-done.5.refs_7_.refs_12_
  12.7 0.0 collective-permute-done.6.refs_8_.refs_13_
  12.7 0.0 copy-done
  12.7 0.6 %substeps.1 = (f32[80,512]{1,0:T(8,128)S(1)}, f32[80,512]{1,0:T(8,128)S(1)}, f32[80,512]{1,0:T(8,128)S(1)}, f32[80,512]{1,0:T(8,128)S(1)}, f32[2,8,8,512]{3,2,1,...) custom-call(s32[2,8,128]{2,1,0:T(8,128)S(1)} %code.1.refs_0_.refs_5_, ...), custom_call_target="tpu_custom_call" | custom-call | tf_op jit(solution)/shard_map/substeps/pallas_call | solution.py:425
  13.3 1.9 %collective-permute-start.9 = (f32[16,8,128]{2,1,0:T(8,128)S(1)}, f32[16,8,128]{2,1,0:T(8,128)S(1)}, u32[]{:S(2)}, u32[]{:S(2)}) collective-permute-start(f32[16,8,128]{2,1,0:T(8,128)S(1)} %get-tuple-element.33), channel_id=1, source_target_pairs={{0,6},{1,7},{2,4},{3,5},{4,2},{5,3},{6,0},{7,1},{8,14},{9,15},{10,... | collective-permute-start | bytes 196616 | tf_op jit(solution)/shard_map/ppermute | solution.py:386
  15.2 0.4 %collective-permute-start.10 = (f32[16,8,128]{2,1,0:T(8,128)S(1)}, f32[16,8,128]{2,1,0:T(8,128)S(1)}, u32[]{:S(2)}, u32[]{:S(2)}) collective-permute-start(f32[16,8,128]{2,1,0:T(8,128)S(1)} %get-tuple-element.34), channel_id=1, source_target_pairs={{0,3},{1,2},{2,1},{3,0},{4,7},{5,6},{6,5},{7,4},{8,11},{9,10},{10,... | collective-permute-start | bytes 196616 | tf_op jit(solution)/shard_map/ppermute | solution.py:386
  15.7 0.9 %collective-permute-start.11 = (f32[16,8,128]{2,1,0:T(8,128)S(1)}, f32[16,8,128]{2,1,0:T(8,128)S(1)}, u32[]{:S(2)}, u32[]{:S(2)}) collective-permute-start(f32[16,8,128]{2,1,0:T(8,128)S(1)} %get-tuple-element.35), channel_id=1, source_target_pairs={{0,5},{1,4},{2,7},{3,6},{4,1},{5,0},{6,3},{7,2},{8,13},{9,12},{10,... | collective-permute-start | bytes 196616 | tf_op jit(solution)/shard_map/ppermute | solution.py:386
  16.6 1.0 %velocities.1 = (f32[2,32,512]{2,1,0:T(8,128)}, f32[16,8,128]{2,1,0:T(8,128)S(1)}, f32[4,8,128]{2,1,0:T(8,128)S(1)}) custom-call(f32[80,512]{1,0:T(8,128)S(1)} %get-tuple-element.26.refs_0_, f32[80,512]{1,0:T(8,128)S(1)} %get-tuple-element.27.refs_1_, f32[80,512]{1,0:T(8,128)S(1)} %get-tuple-element.28.refs_2_, f32[80,512]{1,0:T(8,128)S(1)} %get-tuple-element.29.refs_3_, ...), custom_call_target="tpu_custom_call" | custom-call | tf_op jit(solution)/shard_map/velocities/pallas_call | solution.py:442
  17.6 1.1 %collective-permute-done.9.refs_2_ = f32[16,8,128]{2,1,0:T(8,128)S(1)} collective-permute-done((f32[16,8,128]{2,1,0:T(8,128)S(1)}, f32[16,8,128]{2,1,0:T(8,128)S(1)}, u32[]{:S(2)}, u32[]{:S(2)}) %collective-permute-start.9) | collective-permute-done | bytes 65568 | tf_op jit(solution)/shard_map/ppermute | solution.py:386
  18.6 0.1 sums.1.refs_1_
  18.7 0.8 %collective-permute-done.10.refs_2_ = f32[16,8,128]{2,1,0:T(8,128)S(1)} collective-permute-done((f32[16,8,128]{2,1,0:T(8,128)S(1)}, f32[16,8,128]{2,1,0:T(8,128)S(1)}, u32[]{:S(2)}, u32[]{:S(2)}) %collective-permute-start.10) | collective-permute-done | bytes 65568 | tf_op jit(solution)/shard_map/ppermute | solution.py:386
  19.6 0.0 collective-permute-done.11.refs_3_
  19.6 0.8 %land.1 = (f32[32,512]{1,0:T(8,128)}, f32[32,512]{1,0:T(8,128)}) custom-call(f32[4,8,128]{2,1,0:T(8,128)S(1)} %get-tuple-element.31.refs_0_, f32[2,32,512]{2,1,0:T(8,128)S(1)} %sums.1.refs_1_, f32[16,8,128]{2,1,0:T(8,128)S(1)} %collective-permute-done.10.refs_2_, f32[16,8,128]{2,1,0:T(8,128)S(1)} %collective-permute-done.11.refs_3_), custom_call_target="tpu_custom_call" | custom-call | tf_op jit(solution)/shard_map/land/pallas_call | solution.py:464
  (5 shorter events, 0.0 us)
Async XLA Ops:
  1.8 7.1 %collective-permute-start.1 = (f32[48,512]{1,0:T(8,128)S(1)}, f32[48,512]{1,0:T(8,128)S(1)}, u32[]{:S(2)}, u32[]{:S(2)}) collective-permute-start(f32[48,512]{1,0:T(8,128)S(1)} %get-tuple-element.22), channel_id=1, source_target_pairs={{0,6},{1,7},{2,4},{3,5},{4,2},{5,3},{6,0},{7,1},{8,14},{9,15},{10,... | collective-permute-start | bytes 294920 | tf_op jit(solution)/shard_map/ppermute | solution.py:386
  5.7 5.1 %collective-permute-start.2 = (f32[48,512]{1,0:T(8,128)S(1)}, f32[48,512]{1,0:T(8,128)S(1)}, u32[]{:S(2)}, u32[]{:S(2)}) collective-permute-start(f32[48,512]{1,0:T(8,128)S(1)} %get-tuple-element.23), channel_id=1, source_target_pairs={{0,3},{1,2},{2,1},{3,0},{4,7},{5,6},{6,5},{7,4},{8,11},{9,10},{10,... | collective-permute-start | bytes 294920 | tf_op jit(solution)/shard_map/ppermute | solution.py:386
  5.7 5.2 %collective-permute-start.3 = (f32[48,512]{1,0:T(8,128)S(1)}, f32[48,512]{1,0:T(8,128)S(1)}, u32[]{:S(2)}, u32[]{:S(2)}) collective-permute-start(f32[48,512]{1,0:T(8,128)S(1)} %get-tuple-element.24), channel_id=1, source_target_pairs={{0,5},{1,4},{2,7},{3,6},{4,1},{5,0},{6,3},{7,2},{8,13},{9,12},{10,... | collective-permute-start | bytes 294920 | tf_op jit(solution)/shard_map/ppermute | solution.py:386
  6.1 5.2 %collective-permute-start.7 = (f32[8,512]{1,0:T(8,128)S(1)}, f32[8,512]{1,0:T(8,128)S(1)}, u32[]{:S(2)}, u32[]{:S(2)}) collective-permute-start(f32[8,512]{1,0:T(8,128)S(1)} %get-tuple-element.25), channel_id=1, source_target_pairs={{2,3},{3,2},{4,5},{5,4},{7,8},{8,7},{6,14},{14,6},{10,11},{11,10},... | collective-permute-start | bytes 49160 | tf_op jit(solution)/shard_map/ppermute | solution.py:409
  6.4 5.2 %collective-permute-start = (f32[88,512]{1,0:T(8,128)S(1)}, f32[88,512]{1,0:T(8,128)S(1)}, u32[]{:S(2)}, u32[]{:S(2)}) collective-permute-start(f32[88,512]{1,0:T(8,128)S(1)} %get-tuple-element.21.own_home.refs_1_.refs_6_), channel_id=1, source_target_pairs={{0,1},{1,0},{2,3},{3,2},{4,5},{5,4},{6,7},{7,6},{8,9},{9,8},{10,11... | collective-permute-start | bytes 540680 | tf_op jit(solution)/shard_map/ppermute | solution.py:383
  8.9 3.8 %collective-permute-start.4 = (f32[48,512]{1,0:T(8,128)S(1)}, f32[48,512]{1,0:T(8,128)S(1)}, u32[]{:S(2)}, u32[]{:S(2)}) collective-permute-start(f32[48,512]{1,0:T(8,128)S(1)} %collective-permute-done.1.refs_2_.refs_7_), channel_id=1, source_target_pairs={{0,1},{1,0},{2,3},{3,2},{4,5},{5,4},{6,7},{7,6},{8,9},{9,8},{10,11... | collective-permute-start | bytes 294920 | tf_op jit(solution)/shard_map/ppermute | solution.py:383
  10.8 1.9 %collective-permute-start.5 = (f32[48,512]{1,0:T(8,128)S(1)}, f32[48,512]{1,0:T(8,128)S(1)}, u32[]{:S(2)}, u32[]{:S(2)}) collective-permute-start(f32[48,512]{1,0:T(8,128)S(1)} %collective-permute-done.2.refs_3_.refs_8_), channel_id=1, source_target_pairs={{0,1},{1,0},{2,3},{3,2},{4,5},{5,4},{6,7},{7,6},{8,9},{9,8},{10,11... | collective-permute-start | bytes 294920 | tf_op jit(solution)/shard_map/ppermute | solution.py:383
  10.9 1.7 %collective-permute-start.6 = (f32[48,512]{1,0:T(8,128)S(1)}, f32[48,512]{1,0:T(8,128)S(1)}, u32[]{:S(2)}, u32[]{:S(2)}) collective-permute-start(f32[48,512]{1,0:T(8,128)S(1)} %collective-permute-done.3.refs_4_.refs_9_), channel_id=1, source_target_pairs={{0,1},{1,0},{2,3},{3,2},{4,5},{5,4},{6,7},{7,6},{8,9},{9,8},{10,11... | collective-permute-start | bytes 294920 | tf_op jit(solution)/shard_map/ppermute | solution.py:383
  11.3 1.3 %copy-start = (f32[32,512]{1,0:T(8,128)S(1)}, f32[32,512]{1,0:T(8,128)}, u32[]{:S(2)}) copy-start(f32[32,512]{1,0:T(8,128)} %refs_11_.1) | copy-start | bytes 196612
  11.3 1.3 %collective-permute-start.8 = (f32[32,512]{1,0:T(8,128)S(1)}, f32[32,512]{1,0:T(8,128)S(1)}, u32[]{:S(2)}, u32[]{:S(2)}) collective-permute-start(f32[32,512]{1,0:T(8,128)S(1)} %pad_maximum_fusion), channel_id=1, source_target_pairs={{0,1},{1,0},{2,3},{3,2},{4,5},{5,4},{6,7},{7,6},{8,9},{9,8},{10,11... | collective-permute-start | bytes 196616 | tf_op jit(solution)/shard_map/ppermute | solution.py:383
  13.3 5.3 %collective-permute-start.9 = (f32[16,8,128]{2,1,0:T(8,128)S(1)}, f32[16,8,128]{2,1,0:T(8,128)S(1)}, u32[]{:S(2)}, u32[]{:S(2)}) collective-permute-start(f32[16,8,128]{2,1,0:T(8,128)S(1)} %get-tuple-element.33), channel_id=1, source_target_pairs={{0,6},{1,7},{2,4},{3,5},{4,2},{5,3},{6,0},{7,1},{8,14},{9,15},{10,... | collective-permute-start | bytes 196616 | tf_op jit(solution)/shard_map/ppermute | solution.py:386
  15.2 4.3 %collective-permute-start.10 = (f32[16,8,128]{2,1,0:T(8,128)S(1)}, f32[16,8,128]{2,1,0:T(8,128)S(1)}, u32[]{:S(2)}, u32[]{:S(2)}) collective-permute-start(f32[16,8,128]{2,1,0:T(8,128)S(1)} %get-tuple-element.34), channel_id=1, source_target_pairs={{0,3},{1,2},{2,1},{3,0},{4,7},{5,6},{6,5},{7,4},{8,11},{9,10},{10,... | collective-permute-start | bytes 196616 | tf_op jit(solution)/shard_map/ppermute | solution.py:386
  15.7 3.9 %collective-permute-start.11 = (f32[16,8,128]{2,1,0:T(8,128)S(1)}, f32[16,8,128]{2,1,0:T(8,128)S(1)}, u32[]{:S(2)}, u32[]{:S(2)}) collective-permute-start(f32[16,8,128]{2,1,0:T(8,128)S(1)} %get-tuple-element.35), channel_id=1, source_target_pairs={{0,5},{1,4},{2,7},{3,6},{4,1},{5,0},{6,3},{7,2},{8,13},{9,12},{10,... | collective-permute-start | bytes 196616 | tf_op jit(solution)/shard_map/ppermute | solution.py:386

commit v12 on v11

--- a/solution.py
+++ b/solution.py
@@ -438,7 +438,10 @@
         compiler_params=params,
         name="substeps",
     )(code, *mine, *theirs, across, across_sib, sweep)
-    arrived = [to_chip(x, mask) for x, mask in zip(out[5:], masks[1:])]
+    sends = dict(zip(masks[1:], out[5:]))
+    onward = sorted(sends, key=lambda mask: (-mask.bit_count(), -mask))
+    got = {mask: to_chip(sends[mask], mask) for mask in onward}
+    arrived = [got[mask] for mask in masks[1:]]
     vel, home, labels = pl.pallas_call(
         functools.partial(side_kernel, n),
         out_shape=[

time: 20.5 us -> 20.5 us (level)
  no operation moved by 1% of the time
where the time goes in v12:
time: 20.5 us; the launch traced here: 20.4 us
  starting transfers between devices  8.8 us (43%)
  waiting for transfers between devices  7.23 us (35%)
  Pallas kernels  3.62 us (18%)
  between operations  0.69 us (3%)
    ppermute x6, starting transfers between devices, to_chip(): lax.ppermute(x, 'bis', [(i, i ^ target(mask)) for i in range(n)])  7.6 us
    ppermute x6, waiting for transfers between devices, to_chip(): lax.ppermute(x, 'bis', [(i, i ^ target(mask)) for i in range(n)])  6.11 us
    pallas_call x1, Pallas kernels, shards(): pl.pallas_call(functools.partial(pack_kernel, n), out_shape=[jax.ShapeDty...  1.12 us
    ppermute x5, waiting for transfers between devices, to_sibling(): return lax.ppermute(x, 'bis', [(i, i ^ 1) for i in range(n)])  1.12 us
    pallas_call x1, Pallas kernels, shards(): pl.pallas_call(functools.partial(side_kernel, n), out_shape=[jax.ShapeDty...  0.97 us
    ppermute x5, starting transfers between devices, to_sibling(): return lax.ppermute(x, 'bis', [(i, i ^ 1) for i in range(n)])  0.91 us
    pallas_call x1, Pallas kernels, shards(): pl.pallas_call(functools.partial(land_kernel, n, True), out_shape=[jax.Sh...  0.78 us
    pallas_call x1, Pallas kernels, shards(): pl.pallas_call(functools.partial(step_kernel, n), out_shape=[jax.ShapeDty...  0.63 us
  transfers between devices with their start and end apart: 12, of which 5 were waited for; matrix products, arithmetic and copies ran while one was open for 0% of the time, Pallas kernels for 5%

profile of v12, /device:TPU:0, one launch (start us, length us, event | category | flops | bytes accessed | tf_op | source)
XLA Modules:
  0.0 20.4 jit_solution(287609884647600897)
XLA Ops:
  0.6 1.1 %pack.1 = (f32[88,512]{1,0:T(8,128)S(1)}, f32[48,512]{1,0:T(8,128)S(1)}, f32[48,512]{1,0:T(8,128)S(1)}, f32[48,512]{1,0:T(8,128)S(1)}, f32[8,512]{1,0:T(8,128)S(1)}) custom-call(s32[8]{0:T(128)} %bitcast.2, s32[8]{0:T(128)} %bitcast.3, s32[8]{0:T(128)} %refs_2_.1, f32[32,512]{1,0:T(8,128)} %refs_11_.1, f32[5,32,512]{2,1,0:T(8,128)} %refs_4_.1), custom_call_target="tpu_custom_call" | custom-call | tf_op jit(solution)/shard_map/pack/pallas_call | solution.py:391
  1.8 4.0 %collective-permute-start.1 = (f32[48,512]{1,0:T(8,128)S(1)}, f32[48,512]{1,0:T(8,128)S(1)}, u32[]{:S(2)}, u32[]{:S(2)}) collective-permute-start(f32[48,512]{1,0:T(8,128)S(1)} %get-tuple-element.22), channel_id=1, source_target_pairs={{0,6},{1,7},{2,4},{3,5},{4,2},{5,3},{6,0},{7,1},{8,14},{9,15},{10,... | collective-permute-start | bytes 294920 | tf_op jit(solution)/shard_map/ppermute | solution.py:386
  5.7 0.0 collective-permute-start.2
  5.7 0.4 %collective-permute-start.3 = (f32[48,512]{1,0:T(8,128)S(1)}, f32[48,512]{1,0:T(8,128)S(1)}, u32[]{:S(2)}, u32[]{:S(2)}) collective-permute-start(f32[48,512]{1,0:T(8,128)S(1)} %get-tuple-element.24), channel_id=1, source_target_pairs={{0,5},{1,4},{2,7},{3,6},{4,1},{5,0},{6,3},{7,2},{8,13},{9,12},{10,... | collective-permute-start | bytes 294920 | tf_op jit(solution)/shard_map/ppermute | solution.py:386
  6.1 0.3 %collective-permute-start.7 = (f32[8,512]{1,0:T(8,128)S(1)}, f32[8,512]{1,0:T(8,128)S(1)}, u32[]{:S(2)}, u32[]{:S(2)}) collective-permute-start(f32[8,512]{1,0:T(8,128)S(1)} %get-tuple-element.25), channel_id=1, source_target_pairs={{2,3},{3,2},{4,5},{5,4},{7,8},{8,7},{6,14},{14,6},{10,11},{11,10},... | collective-permute-start | bytes 49160 | tf_op jit(solution)/shard_map/ppermute | solution.py:409
  6.4 0.2 %collective-permute-start = (f32[88,512]{1,0:T(8,128)S(1)}, f32[88,512]{1,0:T(8,128)S(1)}, u32[]{:S(2)}, u32[]{:S(2)}) collective-permute-start(f32[88,512]{1,0:T(8,128)S(1)} %get-tuple-element.21.own_home.refs_1_.refs_6_), channel_id=1, source_target_pairs={{0,1},{1,0},{2,3},{3,2},{4,5},{5,4},{6,7},{7,6},{8,9},{9,8},{10,11... | collective-permute-start | bytes 540680 | tf_op jit(solution)/shard_map/ppermute | solution.py:383
  6.6 2.3 %collective-permute-done.1.refs_2_.refs_7_ = f32[48,512]{1,0:T(8,128)S(1)} collective-permute-done((f32[48,512]{1,0:T(8,128)S(1)}, f32[48,512]{1,0:T(8,128)S(1)}, u32[]{:S(2)}, u32[]{:S(2)}) %collective-permute-start.1) | collective-permute-done | bytes 98336 | tf_op jit(solution)/shard_map/ppermute | solution.py:386
  8.9 0.0 collective-permute-start.4
  8.9 1.9 %collective-permute-done.2.refs_3_.refs_8_ = f32[48,512]{1,0:T(8,128)S(1)} collective-permute-done((f32[48,512]{1,0:T(8,128)S(1)}, f32[48,512]{1,0:T(8,128)S(1)}, u32[]{:S(2)}, u32[]{:S(2)}) %collective-permute-start.2) | collective-permute-done | bytes 98336 | tf_op jit(solution)/shard_map/ppermute | solution.py:386
  10.8 0.1 collective-permute-start.5
  10.9 0.0 collective-permute-done.3.refs_4_.refs_9_
  10.9 0.4 %collective-permute-start.6 = (f32[48,512]{1,0:T(8,128)S(1)}, f32[48,512]{1,0:T(8,128)S(1)}, u32[]{:S(2)}, u32[]{:S(2)}) collective-permute-start(f32[48,512]{1,0:T(8,128)S(1)} %collective-permute-done.3.refs_4_.refs_9_), channel_id=1, source_target_pairs={{0,1},{1,0},{2,3},{3,2},{4,5},{5,4},{6,7},{7,6},{8,9},{9,8},{10,11... | collective-permute-start | bytes 294920 | tf_op jit(solution)/shard_map/ppermute | solution.py:383
  11.3 0.0 collective-permute-done.7.refs_9_
  11.3 0.0 copy-start
  11.3 0.2 collective-permute-start.8
  11.5 0.0 collective-permute-done.sib_home.refs_5_.refs_10_
  11.6 1.1 %collective-permute-done.8.refs_10_ = f32[32,512]{1,0:T(8,128)S(1)} collective-permute-done((f32[32,512]{1,0:T(8,128)S(1)}, f32[32,512]{1,0:T(8,128)S(1)}, u32[]{:S(2)}, u32[]{:S(2)}) %collective-permute-start.8) | collective-permute-done | bytes 65568 | tf_op jit(solution)/shard_map/ppermute | solution.py:383
  12.7 0.0 collective-permute-done.4.refs_6_.refs_11_
  12.7 0.0 collective-permute-done.5.refs_7_.refs_12_
  12.7 0.0 collective-permute-done.6.refs_8_.refs_13_
  12.7 0.0 copy-done
  12.7 0.6 %substeps.1 = (f32[80,512]{1,0:T(8,128)S(1)}, f32[80,512]{1,0:T(8,128)S(1)}, f32[80,512]{1,0:T(8,128)S(1)}, f32[80,512]{1,0:T(8,128)S(1)}, f32[2,8,8,512]{3,2,1,...) custom-call(s32[2,8,128]{2,1,0:T(8,128)S(1)} %code.1.refs_0_.refs_5_, ...), custom_call_target="tpu_custom_call" | custom-call | tf_op jit(solution)/shard_map/substeps/pallas_call | solution.py:425
  13.3 1.9 %collective-permute-start.9 = (f32[16,8,128]{2,1,0:T(8,128)S(1)}, f32[16,8,128]{2,1,0:T(8,128)S(1)}, u32[]{:S(2)}, u32[]{:S(2)}) collective-permute-start(f32[16,8,128]{2,1,0:T(8,128)S(1)} %get-tuple-element.33), channel_id=1, source_target_pairs={{0,6},{1,7},{2,4},{3,5},{4,2},{5,3},{6,0},{7,1},{8,14},{9,15},{10,... | collective-permute-start | bytes 196616 | tf_op jit(solution)/shard_map/ppermute | solution.py:386
  15.2 0.4 %collective-permute-start.10 = (f32[16,8,128]{2,1,0:T(8,128)S(1)}, f32[16,8,128]{2,1,0:T(8,128)S(1)}, u32[]{:S(2)}, u32[]{:S(2)}) collective-permute-start(f32[16,8,128]{2,1,0:T(8,128)S(1)} %get-tuple-element.34), channel_id=1, source_target_pairs={{0,3},{1,2},{2,1},{3,0},{4,7},{5,6},{6,5},{7,4},{8,11},{9,10},{10,... | collective-permute-start | bytes 196616 | tf_op jit(solution)/shard_map/ppermute | solution.py:386
  15.7 0.9 %collective-permute-start.11 = (f32[16,8,128]{2,1,0:T(8,128)S(1)}, f32[16,8,128]{2,1,0:T(8,128)S(1)}, u32[]{:S(2)}, u32[]{:S(2)}) collective-permute-start(f32[16,8,128]{2,1,0:T(8,128)S(1)} %get-tuple-element.35), channel_id=1, source_target_pairs={{0,5},{1,4},{2,7},{3,6},{4,1},{5,0},{6,3},{7,2},{8,13},{9,12},{10,... | collective-permute-start | bytes 196616 | tf_op jit(solution)/shard_map/ppermute | solution.py:386
  16.6 1.0 %velocities.1 = (f32[2,32,512]{2,1,0:T(8,128)}, f32[16,8,128]{2,1,0:T(8,128)S(1)}, f32[4,8,128]{2,1,0:T(8,128)S(1)}) custom-call(f32[80,512]{1,0:T(8,128)S(1)} %get-tuple-element.26.refs_0_, f32[80,512]{1,0:T(8,128)S(1)} %get-tuple-element.27.refs_1_, f32[80,512]{1,0:T(8,128)S(1)} %get-tuple-element.28.refs_2_, f32[80,512]{1,0:T(8,128)S(1)} %get-tuple-element.29.refs_3_, ...), custom_call_target="tpu_custom_call" | custom-call | tf_op jit(solution)/shard_map/velocities/pallas_call | solution.py:445
  17.6 1.1 %collective-permute-done.9.refs_2_ = f32[16,8,128]{2,1,0:T(8,128)S(1)} collective-permute-done((f32[16,8,128]{2,1,0:T(8,128)S(1)}, f32[16,8,128]{2,1,0:T(8,128)S(1)}, u32[]{:S(2)}, u32[]{:S(2)}) %collective-permute-start.9) | collective-permute-done | bytes 65568 | tf_op jit(solution)/shard_map/ppermute | solution.py:386
  18.6 0.1 sums.1.refs_1_
  18.7 0.8 %collective-permute-done.10.refs_2_ = f32[16,8,128]{2,1,0:T(8,128)S(1)} collective-permute-done((f32[16,8,128]{2,1,0:T(8,128)S(1)}, f32[16,8,128]{2,1,0:T(8,128)S(1)}, u32[]{:S(2)}, u32[]{:S(2)}) %collective-permute-start.10) | collective-permute-done | bytes 65568 | tf_op jit(solution)/shard_map/ppermute | solution.py:386
  19.6 0.0 collective-permute-done.11.refs_3_
  19.6 0.8 %land.1 = (f32[32,512]{1,0:T(8,128)}, f32[32,512]{1,0:T(8,128)}) custom-call(f32[4,8,128]{2,1,0:T(8,128)S(1)} %get-tuple-element.31.refs_0_, f32[2,32,512]{2,1,0:T(8,128)S(1)} %sums.1.refs_1_, f32[16,8,128]{2,1,0:T(8,128)S(1)} %collective-permute-done.10.refs_2_, f32[16,8,128]{2,1,0:T(8,128)S(1)} %collective-permute-done.11.refs_3_), custom_call_target="tpu_custom_call" | custom-call | tf_op jit(solution)/shard_map/land/pallas_call | solution.py:467
  (5 shorter events, 0.0 us)
Async XLA Ops:
  1.8 7.1 %collective-permute-start.1 = (f32[48,512]{1,0:T(8,128)S(1)}, f32[48,512]{1,0:T(8,128)S(1)}, u32[]{:S(2)}, u32[]{:S(2)}) collective-permute-start(f32[48,512]{1,0:T(8,128)S(1)} %get-tuple-element.22), channel_id=1, source_target_pairs={{0,6},{1,7},{2,4},{3,5},{4,2},{5,3},{6,0},{7,1},{8,14},{9,15},{10,... | collective-permute-start | bytes 294920 | tf_op jit(solution)/shard_map/ppermute | solution.py:386
  5.7 5.1 %collective-permute-start.2 = (f32[48,512]{1,0:T(8,128)S(1)}, f32[48,512]{1,0:T(8,128)S(1)}, u32[]{:S(2)}, u32[]{:S(2)}) collective-permute-start(f32[48,512]{1,0:T(8,128)S(1)} %get-tuple-element.23), channel_id=1, source_target_pairs={{0,3},{1,2},{2,1},{3,0},{4,7},{5,6},{6,5},{7,4},{8,11},{9,10},{10,... | collective-permute-start | bytes 294920 | tf_op jit(solution)/shard_map/ppermute | solution.py:386
  5.7 5.2 %collective-permute-start.3 = (f32[48,512]{1,0:T(8,128)S(1)}, f32[48,512]{1,0:T(8,128)S(1)}, u32[]{:S(2)}, u32[]{:S(2)}) collective-permute-start(f32[48,512]{1,0:T(8,128)S(1)} %get-tuple-element.24), channel_id=1, source_target_pairs={{0,5},{1,4},{2,7},{3,6},{4,1},{5,0},{6,3},{7,2},{8,13},{9,12},{10,... | collective-permute-start | bytes 294920 | tf_op jit(solution)/shard_map/ppermute | solution.py:386
  6.1 5.2 %collective-permute-start.7 = (f32[8,512]{1,0:T(8,128)S(1)}, f32[8,512]{1,0:T(8,128)S(1)}, u32[]{:S(2)}, u32[]{:S(2)}) collective-permute-start(f32[8,512]{1,0:T(8,128)S(1)} %get-tuple-element.25), channel_id=1, source_target_pairs={{2,3},{3,2},{4,5},{5,4},{7,8},{8,7},{6,14},{14,6},{10,11},{11,10},... | collective-permute-start | bytes 49160 | tf_op jit(solution)/shard_map/ppermute | solution.py:409
  6.4 5.2 %collective-permute-start = (f32[88,512]{1,0:T(8,128)S(1)}, f32[88,512]{1,0:T(8,128)S(1)}, u32[]{:S(2)}, u32[]{:S(2)}) collective-permute-start(f32[88,512]{1,0:T(8,128)S(1)} %get-tuple-element.21.own_home.refs_1_.refs_6_), channel_id=1, source_target_pairs={{0,1},{1,0},{2,3},{3,2},{4,5},{5,4},{6,7},{7,6},{8,9},{9,8},{10,11... | collective-permute-start | bytes 540680 | tf_op jit(solution)/shard_map/ppermute | solution.py:383
  8.9 3.8 %collective-permute-start.4 = (f32[48,512]{1,0:T(8,128)S(1)}, f32[48,512]{1,0:T(8,128)S(1)}, u32[]{:S(2)}, u32[]{:S(2)}) collective-permute-start(f32[48,512]{1,0:T(8,128)S(1)} %collective-permute-done.1.refs_2_.refs_7_), channel_id=1, source_target_pairs={{0,1},{1,0},{2,3},{3,2},{4,5},{5,4},{6,7},{7,6},{8,9},{9,8},{10,11... | collective-permute-start | bytes 294920 | tf_op jit(solution)/shard_map/ppermute | solution.py:383
  10.8 1.9 %collective-permute-start.5 = (f32[48,512]{1,0:T(8,128)S(1)}, f32[48,512]{1,0:T(8,128)S(1)}, u32[]{:S(2)}, u32[]{:S(2)}) collective-permute-start(f32[48,512]{1,0:T(8,128)S(1)} %collective-permute-done.2.refs_3_.refs_8_), channel_id=1, source_target_pairs={{0,1},{1,0},{2,3},{3,2},{4,5},{5,4},{6,7},{7,6},{8,9},{9,8},{10,11... | collective-permute-start | bytes 294920 | tf_op jit(solution)/shard_map/ppermute | solution.py:383
  10.9 1.7 %collective-permute-start.6 = (f32[48,512]{1,0:T(8,128)S(1)}, f32[48,512]{1,0:T(8,128)S(1)}, u32[]{:S(2)}, u32[]{:S(2)}) collective-permute-start(f32[48,512]{1,0:T(8,128)S(1)} %collective-permute-done.3.refs_4_.refs_9_), channel_id=1, source_target_pairs={{0,1},{1,0},{2,3},{3,2},{4,5},{5,4},{6,7},{7,6},{8,9},{9,8},{10,11... | collective-permute-start | bytes 294920 | tf_op jit(solution)/shard_map/ppermute | solution.py:383
  11.3 1.3 %copy-start = (f32[32,512]{1,0:T(8,128)S(1)}, f32[32,512]{1,0:T(8,128)}, u32[]{:S(2)}) copy-start(f32[32,512]{1,0:T(8,128)} %refs_11_.1) | copy-start | bytes 196612
  11.3 1.3 %collective-permute-start.8 = (f32[32,512]{1,0:T(8,128)S(1)}, f32[32,512]{1,0:T(8,128)S(1)}, u32[]{:S(2)}, u32[]{:S(2)}) collective-permute-start(f32[32,512]{1,0:T(8,128)S(1)} %pad_maximum_fusion), channel_id=1, source_target_pairs={{0,1},{1,0},{2,3},{3,2},{4,5},{5,4},{6,7},{7,6},{8,9},{9,8},{10,11... | collective-permute-start | bytes 196616 | tf_op jit(solution)/shard_map/ppermute | solution.py:383
  13.3 5.3 %collective-permute-start.9 = (f32[16,8,128]{2,1,0:T(8,128)S(1)}, f32[16,8,128]{2,1,0:T(8,128)S(1)}, u32[]{:S(2)}, u32[]{:S(2)}) collective-permute-start(f32[16,8,128]{2,1,0:T(8,128)S(1)} %get-tuple-element.33), channel_id=1, source_target_pairs={{0,6},{1,7},{2,4},{3,5},{4,2},{5,3},{6,0},{7,1},{8,14},{9,15},{10,... | collective-permute-start | bytes 196616 | tf_op jit(solution)/shard_map/ppermute | solution.py:386
  15.2 4.3 %collective-permute-start.10 = (f32[16,8,128]{2,1,0:T(8,128)S(1)}, f32[16,8,128]{2,1,0:T(8,128)S(1)}, u32[]{:S(2)}, u32[]{:S(2)}) collective-permute-start(f32[16,8,128]{2,1,0:T(8,128)S(1)} %get-tuple-element.34), channel_id=1, source_target_pairs={{0,3},{1,2},{2,1},{3,0},{4,7},{5,6},{6,5},{7,4},{8,11},{9,10},{10,... | collective-permute-start | bytes 196616 | tf_op jit(solution)/shard_map/ppermute | solution.py:386
  15.7 3.9 %collective-permute-start.11 = (f32[16,8,128]{2,1,0:T(8,128)S(1)}, f32[16,8,128]{2,1,0:T(8,128)S(1)}, u32[]{:S(2)}, u32[]{:S(2)}) collective-permute-start(f32[16,8,128]{2,1,0:T(8,128)S(1)} %get-tuple-element.35), channel_id=1, source_target_pairs={{0,5},{1,4},{2,7},{3,6},{4,1},{5,0},{6,3},{7,2},{8,13},{9,12},{10,... | collective-permute-start | bytes 196616 | tf_op jit(solution)/shard_map/ppermute | solution.py:386

commit v13 on v11

--- a/solution.py
+++ b/solution.py
@@ -285,18 +285,10 @@
 def side_kernel(n, *refs):
     chips = n // 2
     prs, velu, velv, coef, parts, code = refs[:6]
-    mine, theirs = refs[6 : 6 + chips], refs[6 + chips : 6 + 2 * chips]
-    vel, home, labels = refs[6 + 2 * chips :]
+    vel, home = refs[6:]
     _, me = where_am_i()
     core = me % 2
     pack_partials(n, routes(chips)[:1], code, parts, [home])
-    line = slice(8 * NF + INFO, 8 * NF + INFO + 1)
-    for index, mask in enumerate(routes(chips)):
-        own, sib = mine[index][line, :], theirs[index][line, :]
-        if crossed(mask):
-            own, sib = sib, own
-        labels[index] = labels_of(n, me, (jnp.where(core == 0, own, sib), jnp.where(core == 0, sib, own)))
-
     def one(index, _):
         tile = 1 + core * chips + index
         span, dest = at(tile), at(index)
@@ -306,6 +298,19 @@
         return 0
 
     lax.fori_loop(0, chips, one, 0, unroll=n <= 8)
+
+
+def label_kernel(n, *refs):
+    chips = n // 2
+    mine, theirs, labels = refs[:chips], refs[chips : 2 * chips], refs[2 * chips]
+    _, me = where_am_i()
+    core = me % 2
+    line = slice(8 * NF + INFO, 8 * NF + INFO + 1)
+    for index, mask in enumerate(routes(chips)):
+        own, sib = mine[index][line, :], theirs[index][line, :]
+        if crossed(mask):
+            own, sib = sib, own
+        labels[index] = labels_of(n, me, (jnp.where(core == 0, own, sib), jnp.where(core == 0, sib, own)))
 
 
 def land_kernel(n, final, *refs):
@@ -439,18 +444,25 @@
         name="substeps",
     )(code, *mine, *theirs, across, across_sib, sweep)
     arrived = [to_chip(x, mask) for x, mask in zip(out[5:], masks[1:])]
-    vel, home, labels = pl.pallas_call(
+    labels = pl.pallas_call(
+        functools.partial(label_kernel, n),
+        out_shape=jax.ShapeDtypeStruct((chips, 8, 128), f32),
+        in_specs=[VMEM] * (2 * chips),
+        out_specs=VMEM,
+        compiler_params=params,
+        name="labels",
+    )(*mine, *theirs)
+    vel, home = pl.pallas_call(
         functools.partial(side_kernel, n),
         out_shape=[
             jax.ShapeDtypeStruct((2, rows, width), f32),
             jax.ShapeDtypeStruct(send_shape, f32),
-            jax.ShapeDtypeStruct((chips, 8, 128), f32),
         ],
-        in_specs=[VMEM] * (6 + 2 * chips),
-        out_specs=[VMEM] * 3,
+        in_specs=[VMEM] * 6,
+        out_specs=[VMEM] * 2,
         compiler_params=params,
         name="velocities",
-    )(*out[:5], code, *mine, *theirs)
+    )(*out[:5], code)
     arrived = [home] + arrived
     early = 2
     sums = pl.pallas_call(

time: 20.5 us -> 20.5 us (level)
    pallas_call x0 -> x1, Pallas kernels: none -> 0.28 us  [shards(): pl.pallas_call(functools.partial(label_kernel, n), out_shape=jax.ShapeDty...]
    pallas_call x1, Pallas kernels: 0.97 us -> 0.76 us  [shards(): pl.pallas_call(functools.partial(side_kernel, n), out_shape=[jax.ShapeDty...]
  transfers between devices with their start and end apart: 12 -> 12, of which waited for: 5 -> 5; matrix products, arithmetic and copies ran while one was open for 0% -> 0% of each run, Pallas kernels for 5% -> 6%
where the time goes in v13:
time: 20.5 us; the launch traced here: 20.4 us
  starting transfers between devices  8.8 us (43%)
  waiting for transfers between devices  7.16 us (35%)
  Pallas kernels  3.68 us (18%)
  between operations  0.7 us (3%)
    ppermute x6, starting transfers between devices, to_chip(): lax.ppermute(x, 'bis', [(i, i ^ target(mask)) for i in range(n)])  7.6 us
    ppermute x6, waiting for transfers between devices, to_chip(): lax.ppermute(x, 'bis', [(i, i ^ target(mask)) for i in range(n)])  6.04 us
    pallas_call x1, Pallas kernels, shards(): pl.pallas_call(functools.partial(pack_kernel, n), out_shape=[jax.ShapeDty...  1.12 us
    ppermute x5, waiting for transfers between devices, to_sibling(): return lax.ppermute(x, 'bis', [(i, i ^ 1) for i in range(n)])  1.12 us
    ppermute x5, starting transfers between devices, to_sibling(): return lax.ppermute(x, 'bis', [(i, i ^ 1) for i in range(n)])  0.91 us
    pallas_call x1, Pallas kernels, shards(): pl.pallas_call(functools.partial(land_kernel, n, True), out_shape=[jax.Sh...  0.77 us
    pallas_call x1, Pallas kernels, shards(): pl.pallas_call(functools.partial(side_kernel, n), out_shape=[jax.ShapeDty...  0.76 us
    pallas_call x1, Pallas kernels, shards(): pl.pallas_call(functools.partial(step_kernel, n), out_shape=[jax.ShapeDty...  0.63 us
  transfers between devices with their start and end apart: 12, of which 5 were waited for; matrix products, arithmetic and copies ran while one was open for 0% of the time, Pallas kernels for 6%

profile of v13, /device:TPU:0, one launch (start us, length us, event | category | flops | bytes accessed | tf_op | source)
XLA Modules:
  0.0 20.4 jit_solution(13573913677737909408)
XLA Ops:
  0.6 1.1 %pack.1 = (f32[88,512]{1,0:T(8,128)S(1)}, f32[48,512]{1,0:T(8,128)S(1)}, f32[48,512]{1,0:T(8,128)S(1)}, f32[48,512]{1,0:T(8,128)S(1)}, f32[8,512]{1,0:T(8,128)S(1)}) custom-call(s32[8]{0:T(128)} %bitcast.2, s32[8]{0:T(128)} %bitcast.3, s32[8]{0:T(128)} %refs_2_.1, f32[32,512]{1,0:T(8,128)} %refs_11_.1, f32[5,32,512]{2,1,0:T(8,128)} %refs_4_.1), custom_call_target="tpu_custom_call" | custom-call | tf_op jit(solution)/shard_map/pack/pallas_call | solution.py:396
  1.8 4.0 %collective-permute-start = (f32[48,512]{1,0:T(8,128)S(1)}, f32[48,512]{1,0:T(8,128)S(1)}, u32[]{:S(2)}, u32[]{:S(2)}) collective-permute-start(f32[48,512]{1,0:T(8,128)S(1)} %get-tuple-element.21), channel_id=1, source_target_pairs={{0,6},{1,7},{2,4},{3,5},{4,2},{5,3},{6,0},{7,1},{8,14},{9,15},{10,... | collective-permute-start | bytes 294920 | tf_op jit(solution)/shard_map/ppermute | solution.py:391
  5.7 0.0 collective-permute-start.1
  5.7 0.4 %collective-permute-start.2 = (f32[48,512]{1,0:T(8,128)S(1)}, f32[48,512]{1,0:T(8,128)S(1)}, u32[]{:S(2)}, u32[]{:S(2)}) collective-permute-start(f32[48,512]{1,0:T(8,128)S(1)} %get-tuple-element.23), channel_id=1, source_target_pairs={{0,5},{1,4},{2,7},{3,6},{4,1},{5,0},{6,3},{7,2},{8,13},{9,12},{10,... | collective-permute-start | bytes 294920 | tf_op jit(solution)/shard_map/ppermute | solution.py:391
  6.1 0.3 %collective-permute-start.7 = (f32[8,512]{1,0:T(8,128)S(1)}, f32[8,512]{1,0:T(8,128)S(1)}, u32[]{:S(2)}, u32[]{:S(2)}) collective-permute-start(f32[8,512]{1,0:T(8,128)S(1)} %get-tuple-element.24), channel_id=1, source_target_pairs={{2,3},{3,2},{4,5},{5,4},{7,8},{8,7},{6,14},{14,6},{10,11},{11,10},... | collective-permute-start | bytes 49160 | tf_op jit(solution)/shard_map/ppermute | solution.py:414
  6.4 0.2 %collective-permute-start.3 = (f32[88,512]{1,0:T(8,128)S(1)}, f32[88,512]{1,0:T(8,128)S(1)}, u32[]{:S(2)}, u32[]{:S(2)}) collective-permute-start(f32[88,512]{1,0:T(8,128)S(1)} %get-tuple-element.20.refs_0_.own_home.refs_1_), channel_id=1, source_target_pairs={{0,1},{1,0},{2,3},{3,2},{4,5},{5,4},{6,7},{7,6},{8,9},{9,8},{10,11... | collective-permute-start | bytes 540680 | tf_op jit(solution)/shard_map/ppermute | solution.py:388
  6.6 2.3 %collective-permute-done.refs_1_.refs_2_ = f32[48,512]{1,0:T(8,128)S(1)} collective-permute-done((f32[48,512]{1,0:T(8,128)S(1)}, f32[48,512]{1,0:T(8,128)S(1)}, u32[]{:S(2)}, u32[]{:S(2)}) %collective-permute-start) | collective-permute-done | bytes 98336 | tf_op jit(solution)/shard_map/ppermute | solution.py:391
  8.9 0.0 collective-permute-start.4
  8.9 1.9 %collective-permute-done.1.refs_2_.refs_3_ = f32[48,512]{1,0:T(8,128)S(1)} collective-permute-done((f32[48,512]{1,0:T(8,128)S(1)}, f32[48,512]{1,0:T(8,128)S(1)}, u32[]{:S(2)}, u32[]{:S(2)}) %collective-permute-start.1) | collective-permute-done | bytes 98336 | tf_op jit(solution)/shard_map/ppermute | solution.py:391
  10.8 0.1 collective-permute-start.5
  10.9 0.0 collective-permute-done.2.refs_3_.refs_4_
  10.9 0.4 %collective-permute-start.6 = (f32[48,512]{1,0:T(8,128)S(1)}, f32[48,512]{1,0:T(8,128)S(1)}, u32[]{:S(2)}, u32[]{:S(2)}) collective-permute-start(f32[48,512]{1,0:T(8,128)S(1)} %collective-permute-done.2.refs_3_.refs_4_), channel_id=1, source_target_pairs={{0,1},{1,0},{2,3},{3,2},{4,5},{5,4},{6,7},{7,6},{8,9},{9,8},{10,11... | collective-permute-start | bytes 294920 | tf_op jit(solution)/shard_map/ppermute | solution.py:388
  11.3 0.0 collective-permute-done.7.refs_9_
  11.3 0.0 copy-start
  11.3 0.2 collective-permute-start.8
  11.5 0.0 collective-permute-done.3.refs_4_.sib_home.refs_5_
  11.6 1.1 %collective-permute-done.8.refs_10_ = f32[32,512]{1,0:T(8,128)S(1)} collective-permute-done((f32[32,512]{1,0:T(8,128)S(1)}, f32[32,512]{1,0:T(8,128)S(1)}, u32[]{:S(2)}, u32[]{:S(2)}) %collective-permute-start.8) | collective-permute-done | bytes 65568 | tf_op jit(solution)/shard_map/ppermute | solution.py:388
  12.7 0.0 collective-permute-done.4.refs_5_.refs_6_
  12.7 0.0 collective-permute-done.5.refs_6_.refs_7_
  12.7 0.0 collective-permute-done.6.refs_7_.refs_8_
  12.7 0.0 copy-done
  12.7 0.6 %substeps.1 = (f32[80,512]{1,0:T(8,128)S(1)}, f32[80,512]{1,0:T(8,128)S(1)}, f32[80,512]{1,0:T(8,128)S(1)}, f32[80,512]{1,0:T(8,128)S(1)}, f32[2,8,8,512]{3,2,1,...) custom-call(s32[2,8,128]{2,1,0:T(8,128)S(1)} %code.1.refs_0_.refs_5_, ...), custom_call_target="tpu_custom_call" | custom-call | tf_op jit(solution)/shard_map/substeps/pallas_call | solution.py:430
  13.3 1.9 %collective-permute-start.9 = (f32[16,8,128]{2,1,0:T(8,128)S(1)}, f32[16,8,128]{2,1,0:T(8,128)S(1)}, u32[]{:S(2)}, u32[]{:S(2)}) collective-permute-start(f32[16,8,128]{2,1,0:T(8,128)S(1)} %get-tuple-element.31), channel_id=1, source_target_pairs={{0,6},{1,7},{2,4},{3,5},{4,2},{5,3},{6,0},{7,1},{8,14},{9,15},{10,... | collective-permute-start | bytes 196616 | tf_op jit(solution)/shard_map/ppermute | solution.py:391
  15.2 0.4 %collective-permute-start.10 = (f32[16,8,128]{2,1,0:T(8,128)S(1)}, f32[16,8,128]{2,1,0:T(8,128)S(1)}, u32[]{:S(2)}, u32[]{:S(2)}) collective-permute-start(f32[16,8,128]{2,1,0:T(8,128)S(1)} %get-tuple-element.32), channel_id=1, source_target_pairs={{0,3},{1,2},{2,1},{3,0},{4,7},{5,6},{6,5},{7,4},{8,11},{9,10},{10,... | collective-permute-start | bytes 196616 | tf_op jit(solution)/shard_map/ppermute | solution.py:391
  15.7 0.9 %collective-permute-start.11 = (f32[16,8,128]{2,1,0:T(8,128)S(1)}, f32[16,8,128]{2,1,0:T(8,128)S(1)}, u32[]{:S(2)}, u32[]{:S(2)}) collective-permute-start(f32[16,8,128]{2,1,0:T(8,128)S(1)} %get-tuple-element.33), channel_id=1, source_target_pairs={{0,5},{1,4},{2,7},{3,6},{4,1},{5,0},{6,3},{7,2},{8,13},{9,12},{10,... | collective-permute-start | bytes 196616 | tf_op jit(solution)/shard_map/ppermute | solution.py:391
  16.6 0.8 %velocities.1 = (f32[2,32,512]{2,1,0:T(8,128)}, f32[16,8,128]{2,1,0:T(8,128)S(1)}) custom-call(f32[80,512]{1,0:T(8,128)S(1)} %get-tuple-element.25.refs_0_, f32[80,512]{1,0:T(8,128)S(1)} %get-tuple-element.26.refs_1_, f32[80,512]{1,0:T(8,128)S(1)} %get-tuple-element.27.refs_2_, f32[80,512]{1,0:T(8,128)S(1)} %get-tuple-element.28.refs_3_, ...), custom_call_target="tpu_custom_call" | custom-call | tf_op jit(solution)/shard_map/velocities/pallas_call | solution.py:455
  17.4 0.3 %labels.1.refs_0_ = f32[4,8,128]{2,1,0:T(8,128)S(1)} custom-call(f32[88,512]{1,0:T(8,128)S(1)} %get-tuple-element.20.refs_0_.own_home.refs_1_, f32[48,512]{1,0:T(8,128)S(1)} %collective-permute-done.refs_1_.refs_2_, f32[48,512]{1,0:T(8,128)S(1)} %collective-permute-done.1.refs_2_.refs_3_, f32[48,512]{1,0:T(8,128)S(1)} %collective-permute-done.2.refs_3_.refs_4_, ...), custom_call_target="tpu_custom_call" | custom-call | tf_op jit(solution)/shard_map/labels/pallas_call | solution.py:447
  17.6 1.0 %collective-permute-done.9.refs_2_ = f32[16,8,128]{2,1,0:T(8,128)S(1)} collective-permute-done((f32[16,8,128]{2,1,0:T(8,128)S(1)}, f32[16,8,128]{2,1,0:T(8,128)S(1)}, u32[]{:S(2)}, u32[]{:S(2)}) %collective-permute-start.9) | collective-permute-done | bytes 65568 | tf_op jit(solution)/shard_map/ppermute | solution.py:391
  18.6 0.1 sums.1.refs_1_
  18.7 0.8 %collective-permute-done.10.refs_2_ = f32[16,8,128]{2,1,0:T(8,128)S(1)} collective-permute-done((f32[16,8,128]{2,1,0:T(8,128)S(1)}, f32[16,8,128]{2,1,0:T(8,128)S(1)}, u32[]{:S(2)}, u32[]{:S(2)}) %collective-permute-start.10) | collective-permute-done | bytes 65568 | tf_op jit(solution)/shard_map/ppermute | solution.py:391
  19.6 0.0 collective-permute-done.11.refs_3_
  19.6 0.8 %land.1 = (f32[32,512]{1,0:T(8,128)}, f32[32,512]{1,0:T(8,128)}) custom-call(f32[4,8,128]{2,1,0:T(8,128)S(1)} %labels.1.refs_0_, f32[2,32,512]{2,1,0:T(8,128)S(1)} %sums.1.refs_1_, f32[16,8,128]{2,1,0:T(8,128)S(1)} %collective-permute-done.10.refs_2_, f32[16,8,128]{2,1,0:T(8,128)S(1)} %collective-permute-done.11.refs_3_), custom_call_target="tpu_custom_call" | custom-call | tf_op jit(solution)/shard_map/land/pallas_call | solution.py:476
  (5 shorter events, 0.0 us)
Async XLA Ops:
  1.8 7.1 %collective-permute-start = (f32[48,512]{1,0:T(8,128)S(1)}, f32[48,512]{1,0:T(8,128)S(1)}, u32[]{:S(2)}, u32[]{:S(2)}) collective-permute-start(f32[48,512]{1,0:T(8,128)S(1)} %get-tuple-element.21), channel_id=1, source_target_pairs={{0,6},{1,7},{2,4},{3,5},{4,2},{5,3},{6,0},{7,1},{8,14},{9,15},{10,... | collective-permute-start | bytes 294920 | tf_op jit(solution)/shard_map/ppermute | solution.py:391
  5.7 5.1 %collective-permute-start.1 = (f32[48,512]{1,0:T(8,128)S(1)}, f32[48,512]{1,0:T(8,128)S(1)}, u32[]{:S(2)}, u32[]{:S(2)}) collective-permute-start(f32[48,512]{1,0:T(8,128)S(1)} %get-tuple-element.22), channel_id=1, source_target_pairs={{0,3},{1,2},{2,1},{3,0},{4,7},{5,6},{6,5},{7,4},{8,11},{9,10},{10,... | collective-permute-start | bytes 294920 | tf_op jit(solution)/shard_map/ppermute | solution.py:391
  5.7 5.2 %collective-permute-start.2 = (f32[48,512]{1,0:T(8,128)S(1)}, f32[48,512]{1,0:T(8,128)S(1)}, u32[]{:S(2)}, u32[]{:S(2)}) collective-permute-start(f32[48,512]{1,0:T(8,128)S(1)} %get-tuple-element.23), channel_id=1, source_target_pairs={{0,5},{1,4},{2,7},{3,6},{4,1},{5,0},{6,3},{7,2},{8,13},{9,12},{10,... | collective-permute-start | bytes 294920 | tf_op jit(solution)/shard_map/ppermute | solution.py:391
  6.1 5.2 %collective-permute-start.7 = (f32[8,512]{1,0:T(8,128)S(1)}, f32[8,512]{1,0:T(8,128)S(1)}, u32[]{:S(2)}, u32[]{:S(2)}) collective-permute-start(f32[8,512]{1,0:T(8,128)S(1)} %get-tuple-element.24), channel_id=1, source_target_pairs={{2,3},{3,2},{4,5},{5,4},{7,8},{8,7},{6,14},{14,6},{10,11},{11,10},... | collective-permute-start | bytes 49160 | tf_op jit(solution)/shard_map/ppermute | solution.py:414
  6.4 5.2 %collective-permute-start.3 = (f32[88,512]{1,0:T(8,128)S(1)}, f32[88,512]{1,0:T(8,128)S(1)}, u32[]{:S(2)}, u32[]{:S(2)}) collective-permute-start(f32[88,512]{1,0:T(8,128)S(1)} %get-tuple-element.20.refs_0_.own_home.refs_1_), channel_id=1, source_target_pairs={{0,1},{1,0},{2,3},{3,2},{4,5},{5,4},{6,7},{7,6},{8,9},{9,8},{10,11... | collective-permute-start | bytes 540680 | tf_op jit(solution)/shard_map/ppermute | solution.py:388
  8.9 3.8 %collective-permute-start.4 = (f32[48,512]{1,0:T(8,128)S(1)}, f32[48,512]{1,0:T(8,128)S(1)}, u32[]{:S(2)}, u32[]{:S(2)}) collective-permute-start(f32[48,512]{1,0:T(8,128)S(1)} %collective-permute-done.refs_1_.refs_2_), channel_id=1, source_target_pairs={{0,1},{1,0},{2,3},{3,2},{4,5},{5,4},{6,7},{7,6},{8,9},{9,8},{10,11... | collective-permute-start | bytes 294920 | tf_op jit(solution)/shard_map/ppermute | solution.py:388
  10.8 1.9 %collective-permute-start.5 = (f32[48,512]{1,0:T(8,128)S(1)}, f32[48,512]{1,0:T(8,128)S(1)}, u32[]{:S(2)}, u32[]{:S(2)}) collective-permute-start(f32[48,512]{1,0:T(8,128)S(1)} %collective-permute-done.1.refs_2_.refs_3_), channel_id=1, source_target_pairs={{0,1},{1,0},{2,3},{3,2},{4,5},{5,4},{6,7},{7,6},{8,9},{9,8},{10,11... | collective-permute-start | bytes 294920 | tf_op jit(solution)/shard_map/ppermute | solution.py:388
  10.9 1.7 %collective-permute-start.6 = (f32[48,512]{1,0:T(8,128)S(1)}, f32[48,512]{1,0:T(8,128)S(1)}, u32[]{:S(2)}, u32[]{:S(2)}) collective-permute-start(f32[48,512]{1,0:T(8,128)S(1)} %collective-permute-done.2.refs_3_.refs_4_), channel_id=1, source_target_pairs={{0,1},{1,0},{2,3},{3,2},{4,5},{5,4},{6,7},{7,6},{8,9},{9,8},{10,11... | collective-permute-start | bytes 294920 | tf_op jit(solution)/shard_map/ppermute | solution.py:388
  11.3 1.3 %copy-start = (f32[32,512]{1,0:T(8,128)S(1)}, f32[32,512]{1,0:T(8,128)}, u32[]{:S(2)}) copy-start(f32[32,512]{1,0:T(8,128)} %refs_11_.1) | copy-start | bytes 196612
  11.3 1.3 %collective-permute-start.8 = (f32[32,512]{1,0:T(8,128)S(1)}, f32[32,512]{1,0:T(8,128)S(1)}, u32[]{:S(2)}, u32[]{:S(2)}) collective-permute-start(f32[32,512]{1,0:T(8,128)S(1)} %pad_maximum_fusion), channel_id=1, source_target_pairs={{0,1},{1,0},{2,3},{3,2},{4,5},{5,4},{6,7},{7,6},{8,9},{9,8},{10,11... | collective-permute-start | bytes 196616 | tf_op jit(solution)/shard_map/ppermute | solution.py:388
  13.3 5.3 %collective-permute-start.9 = (f32[16,8,128]{2,1,0:T(8,128)S(1)}, f32[16,8,128]{2,1,0:T(8,128)S(1)}, u32[]{:S(2)}, u32[]{:S(2)}) collective-permute-start(f32[16,8,128]{2,1,0:T(8,128)S(1)} %get-tuple-element.31), channel_id=1, source_target_pairs={{0,6},{1,7},{2,4},{3,5},{4,2},{5,3},{6,0},{7,1},{8,14},{9,15},{10,... | collective-permute-start | bytes 196616 | tf_op jit(solution)/shard_map/ppermute | solution.py:391
  15.2 4.3 %collective-permute-start.10 = (f32[16,8,128]{2,1,0:T(8,128)S(1)}, f32[16,8,128]{2,1,0:T(8,128)S(1)}, u32[]{:S(2)}, u32[]{:S(2)}) collective-permute-start(f32[16,8,128]{2,1,0:T(8,128)S(1)} %get-tuple-element.32), channel_id=1, source_target_pairs={{0,3},{1,2},{2,1},{3,0},{4,7},{5,6},{6,5},{7,4},{8,11},{9,10},{10,... | collective-permute-start | bytes 196616 | tf_op jit(solution)/shard_map/ppermute | solution.py:391
  15.7 3.9 %collective-permute-start.11 = (f32[16,8,128]{2,1,0:T(8,128)S(1)}, f32[16,8,128]{2,1,0:T(8,128)S(1)}, u32[]{:S(2)}, u32[]{:S(2)}) collective-permute-start(f32[16,8,128]{2,1,0:T(8,128)S(1)} %get-tuple-element.33), channel_id=1, source_target_pairs={{0,5},{1,4},{2,7},{3,6},{4,1},{5,0},{6,3},{7,2},{8,13},{9,12},{10,... | collective-permute-start | bytes 196616 | tf_op jit(solution)/shard_map/ppermute | solution.py:391
